TPU v7x, 512 devices: a whole 4x4x16 slice. The times are simulated.
512 devices in a mesh: herd: 128 (over y, z, core), snp: 4 (over x).
Axes of the slice: x: 4, y: 4, z: 16, core: 2. Of those that a mesh axis runs over, the one named last changes fastest.
Arguments:
- sol_u: float32 [16, 524288], P('snp', 'herd'), may hold values from -6 to 6
- res_u: float32 [16, 524288], P('snp', 'herd'), may hold values from -50 to 50
- dir_u: float32 [16, 524288], P('snp', 'herd'), may hold values from -50 to 50
- rec_weight: float32 [16, 524288], P('snp', 'herd'), may hold values from 0.1 to 2
- inv_diag_u: float32 [16, 524288], P('snp', 'herd'), may hold values from 0.15 to 0.5
- sol_a: float32 [16, 4, 10240], P(None, 'snp', 'herd'), may hold values from -6 to 6
- res_a: float32 [16, 4, 10240], P(None, 'snp', 'herd'), may hold values from -50 to 50
- dir_a: float32 [16, 4, 10240], P(None, 'snp', 'herd'), may hold values from -50 to 50
- inv_diag_a: float32 [16, 4, 10240], P(None, 'snp', 'herd'), may hold values from 0.3 to 1
- genotypes: bfloat16 [4096, 40960], P('herd', 'snp'), may hold values from 0 to 2, as said below
- allele_freq: float32 [40960], P('snp'), may hold values from 0.05 to 0.5
- geno_weight: float32 [16], P('snp'), may hold values from 0.5 to 2
- snp_ridge: float32 [16], replicated, may hold values from 0.5 to 2
- genetic_inv: float32 [16, 16], P('snp'), may hold values from -0.1 to 2, as said below
- sire: int32 [524288], P('herd'), may hold values from -1 to 524287, as said below
- dam: int32 [524288], P('herd'), may hold values from -1 to 524286, as said below
Outputs:
- next_sol_u: float32 [16, 524288], P('snp', 'herd')
- next_res_u: float32 [16, 524288], P('snp', 'herd')
- next_dir_u: float32 [16, 524288], P('snp', 'herd')
- next_sol_a: float32 [16, 4, 10240], P(None, 'snp', 'herd')
- next_res_a: float32 [16, 4, 10240], P(None, 'snp', 'herd')
- next_dir_a: float32 [16, 4, 10240], P(None, 'snp', 'herd')
Inputs may be any that keep to these rules, and one draw needn't show every extreme that they name: A sire is -1 or an animal of another herd group (herd group of animal i: i // 4096); the sires of one herd group's animals lie in at most 2 distinct parent blocks (animals 128 b to 128 b + 127 within one group) of any one other group, and some group has exactly 2 such blocks taken by every other group. A dam is -1 or an earlier animal of the same herd group. `genotypes`: every entry is 0, 1 or 2. `genetic_inv`: symmetric positive definite.
All inputs are finite; a program needn't handle non-finite values.
Results may differ from a plain program's by a relative error of at most 0.0003.
Values sent between devices are 32-bit elements; how exact they have to be, the bound alone decides.
No kernel may reach another device: no remote copies, remote signals or barrier semaphores. Data moves between devices by JAX's collectives and lax.ppermute only.
A program may use at most 128 MiB of HBM per device.

v0:
```python
import math

import jax
import jax.numpy as jnp
from jax import lax
from jax.sharding import PartitionSpec as P

SLOTS = 2


def pedigree(field, sire, dam):
    traits_here, animals = field.shape
    herd_count = lax.axis_size("herd")
    herd_index = lax.axis_index("herd")
    block_count = animals // 128
    span = SLOTS * 128
    has_sire = sire >= 0
    has_dam = dam >= 0
    sire_known = has_sire.astype(jnp.float32)
    dam_known = has_dam.astype(jnp.float32)
    owner_herd = jnp.where(has_sire, sire // animals, 0)
    block_index = jnp.where(has_sire, sire % animals // 128, 0)
    offset = jnp.where(has_sire, sire % 128, 0)
    flat_block = jnp.where(
        has_sire, owner_herd * block_count + block_index, herd_count * block_count
    )
    present = jnp.zeros((herd_count * block_count + 1,), jnp.int32).at[flat_block].max(1)
    present = present[:-1].reshape(herd_count, block_count)
    slot_order = jnp.cumsum(present, axis=1) - 1
    slot_range = jnp.arange(SLOTS, dtype=jnp.int32)
    slot_match = (present[:, :, None] == 1) & (slot_order[:, :, None] == slot_range[None, None, :])
    block_ids = jnp.arange(block_count, dtype=jnp.int32)[None, :, None] + 1
    wanted = jnp.sum(jnp.where(slot_match, block_ids, 0), axis=1) - 1
    requests = lax.all_to_all(wanted, "herd", split_axis=0, concat_axis=0, tiled=True)
    live_slot = requests >= 0
    field_tiles = field.reshape(traits_here, block_count, 128)
    outgoing = field_tiles[:, jnp.where(live_slot, requests, 0), :]
    outgoing = jnp.where(live_slot[None, :, :, None], outgoing, 0.0).reshape(
        traits_here, herd_count, span
    )
    fetched = lax.all_to_all(outgoing, "herd", split_axis=1, concat_axis=1, tiled=True).reshape(
        traits_here, herd_count * span
    )
    slot_index = slot_order[owner_herd, block_index]
    buffer_place = owner_herd * span + slot_index * 128 + offset
    sire_values = fetched[:, jnp.where(has_sire, buffer_place, 0)]
    local_dam = jnp.where(has_dam, dam - herd_index * animals, 0)
    dam_values = field[:, local_dam]
    weight = 4.0 / (4.0 - sire_known - dam_known)
    scaled = weight * (field - 0.5 * sire_known * sire_values - 0.5 * dam_known * dam_values)
    dam_target = jnp.where(has_dam, local_dam, animals)
    dam_terms = (
        jnp.zeros((traits_here, animals + 1), jnp.float32)
        .at[:, dam_target]
        .add(-0.5 * dam_known * scaled)
    )
    result = scaled + dam_terms[:, :animals]
    sire_target = jnp.where(has_sire, buffer_place, herd_count * span)
    outbound = (
        jnp.zeros((traits_here, herd_count * span + 1), jnp.float32)
        .at[:, sire_target]
        .add(-0.5 * sire_known * scaled)
    )
    outbound = outbound[:, :-1].reshape(traits_here, herd_count, span)
    returned = lax.all_to_all(outbound, "herd", split_axis=1, concat_axis=1, tiled=True).reshape(
        traits_here, herd_count * SLOTS, 128
    )
    block_target = jnp.where(live_slot, requests, block_count).reshape(herd_count * SLOTS)
    incoming = (
        jnp.zeros((traits_here, block_count + 1, 128), jnp.float32)
        .at[:, block_target, :]
        .add(returned)
    )
    return result + incoming[:, :block_count, :].reshape(traits_here, animals)


def body(
    sol_u,
    res_u,
    dir_u,
    rec_weight,
    inv_diag_u,
    sol_a,
    res_a,
    dir_a,
    inv_diag_a,
    genotypes,
    allele_freq,
    geno_weight,
    snp_ridge,
    genetic_inv,
    sire,
    dam,
):
    herd_index = lax.axis_index("herd")
    snp_count = genotypes.shape[1] * lax.axis_size("snp")
    genotyped = genotypes.shape[0]
    per_device = dir_a.shape[2]
    geno_scale = 2.0 / math.sqrt(snp_count)
    centered = (genotypes.astype(jnp.float32) - 2.0 * allele_freq) * geno_scale
    partial_rows = lax.dot_general(
        lax.all_gather(dir_a, "herd", axis=2, tiled=True)[:, 0, :],
        centered,
        (((1,), (1,)), ((), ())),
        precision=lax.Precision.HIGHEST,
        preferred_element_type=jnp.float32,
    )
    genomic = lax.psum_scatter(partial_rows, "snp", scatter_dimension=0, tiled=True)
    geno_resid = geno_weight[:, None] * (dir_u[:, :genotyped] - genomic)
    resid_all = lax.all_gather(geno_resid, "snp", axis=0, tiled=True)
    totals_all = jnp.dot(resid_all, centered, precision=lax.Precision.HIGHEST)
    summed = lax.psum(totals_all, "herd")
    snp_back = lax.dynamic_slice_in_dim(summed, herd_index * per_device, per_device, 1)
    image_a = snp_ridge[:, None, None] * dir_a - snp_back[:, None, :]
    own_term = pedigree(dir_u, sire, dam)
    whole_traits = lax.all_gather(own_term, "snp", axis=0, tiled=True)
    mixed_term = jnp.dot(genetic_inv, whole_traits, precision=lax.Precision.HIGHEST)
    image_u = rec_weight * dir_u + mixed_term
    image_u = image_u.at[:, :genotyped].add(geno_resid)
    weighted_u = inv_diag_u * res_u
    weighted_a = inv_diag_a * res_a
    local_norm = jnp.sum(weighted_u * res_u) + jnp.sum(weighted_a * res_a)
    local_curve = jnp.sum(dir_u * image_u) + jnp.sum(dir_a * image_a)
    norm_now = lax.psum(local_norm, ("herd", "snp"))
    curvature = lax.psum(local_curve, ("herd", "snp"))
    step_size = norm_now / curvature
    next_res_u = res_u - step_size * image_u
    next_res_a = res_a - step_size * image_a
    local_next = jnp.sum(inv_diag_u * next_res_u * next_res_u) + jnp.sum(
        inv_diag_a * next_res_a * next_res_a
    )
    norm_next = lax.psum(local_next, ("herd", "snp"))
    next_sol_u = sol_u + step_size * dir_u
    next_sol_a = sol_a + step_size * dir_a
    step_ratio = norm_next / norm_now
    next_dir_u = inv_diag_u * next_res_u + step_ratio * dir_u
    next_dir_a = inv_diag_a * next_res_a + step_ratio * dir_a
    return (next_sol_u, next_res_u, next_dir_u, next_sol_a, next_res_a, next_dir_a)


def solution(mesh):
    placed = (
        P("snp", "herd"),
        P("snp", "herd"),
        P("snp", "herd"),
        P("snp", "herd"),
        P("snp", "herd"),
        P(None, "snp", "herd"),
        P(None, "snp", "herd"),
        P(None, "snp", "herd"),
        P(None, "snp", "herd"),
        P("herd", "snp"),
        P("snp"),
        P("snp"),
        P(),
        P("snp", None),
        P("herd"),
        P("herd"),
    )
    return jax.shard_map(
        body,
        mesh=mesh,
        in_specs=placed,
        out_specs=(
            P("snp", "herd"),
            P("snp", "herd"),
            P("snp", "herd"),
            P(None, "snp", "herd"),
            P(None, "snp", "herd"),
            P(None, "snp", "herd"),
        ),
        check_vma=False,
    )
```

profile of v0, /device:TPU:1, one launch (start us, length us, event | category | flops | bytes accessed | tf_op | source)
XLA Modules:
  0.0 999.3 jit_solution(17570711834181041808)
XLA Ops:
  7.2 1.4 broadcast_select_fusion
  8.5 0.8 fusion.30
  9.3 22.4 %scatter_custom_fusion = s32[4097]{0:T(1024)S(1)} fusion(s32[4096]{0:T(1024)S(1)} %get-tuple-element.41, s32[4096]{0:T(1024)S(1)} %ne.33, s32[]{:T(128)} %constant.113.clone.1), kind=kCustom, calls=%fused_computation.87 | custom fusion | flops 4096 | bytes 16392 | tf_op jit(solution)/shard_map/scatter-max | solution.py:27
  31.7 0.1 broadcast_in_dim_reshape.3
  31.8 0.1 copy.93
  31.9 0.1 reduce_window_sum.11
  32.0 0.1 copy.92
  32.1 0.1 select_reduce_fusion
  32.2 0.1 copy.94
  32.3 35.4 %all_to_all.22 = s32[128,1,2]{2,1,0:T(1,128)S(1)} all-to-all(s32[128,1,2]{2,1,0:T(1,128)S(1)} %copy.94), channel_id=1, replica_groups=mesh['herd'=128,'snp'=4] {'herd'}, dimensions={0} | all-to-all | bytes 2048 | tf_op jit(solution)/shard_map/all_to_all | solution.py:34
  67.7 0.1 reshape.165
  67.9 1.8 gather_fusion
  69.7 0.2 copy.96
  70.0 0.1 copy.95
  70.1 1.0 copy.97
  71.1 6.6 all-to-all-start.1
  77.7 0.6 copy.99
  78.4 26.5 %gather_fusion.1 = s32[4096]{0:T(1024)S(1)} fusion(s32[128,32]{0,1:T(8,128)S(1)} %broadcast_add_fusion, s32[4096]{0:T(1024)S(1)} %get-tuple-element.40), kind=kCustom, calls=%fused_computation.1 | custom fusion | bytes 65536 | tf_op jit(solution)/shard_map/gather | solution.py:44
  105.0 0.6 compare_select_fusion.3
  105.6 14.1 %gather_fusion.3 = f32[4096,4]{1,0:T(8,128)} fusion(f32[4,4096]{0,1:T(8,128)S(1)} %copy.99, s32[4096]{0:T(1024)S(1)} %get-tuple-element.39), kind=kCustom, calls=%fused_computation.3 | custom fusion | bytes 147456 | tf_op jit(solution)/shard_map/gather | solution.py:48
  119.7 8.4 copy.98
  128.1 19.8 %gather_fusion.2 = f32[4096,4]{1,0:T(8,128)} fusion(f32[4,32768]{0,1:T(8,128)} %bitcast.59, s32[4096]{0:T(1024)S(1)} %fusion.33), kind=kCustom, calls=%fused_computation.2 | custom fusion | bytes 147456 | tf_op jit(solution)/shard_map/gather | solution.py:46
  147.9 4.3 fusion.8
  152.2 31.1 %scatter_custom_fusion.2 = f32[4,32769]{0,1:T(8,128)} fusion(s32[4096]{0:T(1024)S(1)} %get-tuple-element.30, f32[]{:T(128)} %constant.111.clone.1, f32[4,4096]{0,1:T(8,128)S(1)} %fusion.8, f32[4096]{0:T(1024)S(1)} %get-tuple-element.28), kind=kCustom, calls=%fused_computation.8 | custom fusion | flops 32768 | bytes 2637844 | tf_op jit(solution)/shard_map/scatter-add | solution.py:62
  183.4 11.2 %slice.50 = f32[4,32768]{0,1:T(8,128)} slice(f32[4,32769]{0,1:T(8,128)} %scatter_custom_fusion.2), slice={[0:4], [0:32768]} | slice | bytes 1048576 | tf_op jit(solution)/shard_map/slice | solution.py:64
  194.6 9.9 copy.101
  204.5 16.3 %all-to-all-start.2 = ((f32[4,128,256]{2,0,1:T(4,128)}), f32[4,128,256]{2,0,1:T(4,128)S(1)}, u32[]{:S(2)}, u32[]{:S(2)}) async-start(f32[4,128,256]{2,0,1:T(4,128)} %copy.101), calls=%async_computation.2 | async-start | bytes 1048576 | tf_op jit(solution)/shard_map/all_to_all | solution.py:65
  220.8 0.0 all-reduce.4.cloned.1.call-start
  220.8 0.1 copy.106
  220.9 1.3 dynamic-slice.8
  222.8 0.6 compare_reduce_fusion
  223.5 119.3 %all_gather.10 = f32[16,1,10240]{0,1,2:T(1,128)S(1)} all-gather(f32[16,1,80]{0,1,2:T(1,128)S(1)} %copy.106), channel_id=1, replica_groups=mesh['herd'=128,'snp'=4] {'herd'}, dimensions={2}, use_global_device_ids=true | all-gather | bytes 660480 | tf_op jit(solution)/shard_map/all_gather | solution.py:102
  342.8 8.3 fusion.13
  351.1 9.4 all-reduce
  360.5 0.5 broadcast.296
  361.0 0.8 reduce.11
  361.8 0.1 all_to_all.17
  362.0 25.9 %scatter_custom_fusion.1 = f32[4,4097]{0,1:T(8,128)} fusion(s32[4096]{0:T(1024)} %get-tuple-element.38, f32[4,4096]{0,1:T(8,128)S(1)} %fusion.8, f32[]{:T(128)} %constant.111.clone.1, f32[4096]{0:T(1024)S(1)} %copy-done.8), kind=kCustom, calls=%fused_computation.16 | custom fusion | flops 32768 | bytes 147984 | tf_op jit(solution)/shard_map/scatter-add | solution.py:55
  387.9 0.9 copy.102
  388.8 1.1 reshape.218
  389.9 1.1 copy.103
  391.0 17.3 %scatter_fusion = f32[4,33,128]{2,0,1:T(4,128)S(1)} fusion(f32[4,33,128]{2,0,1:T(4,128)S(1)} %broadcast_in_dim.105, s32[256]{0:T(256)S(1)} %bitcast.72, f32[256,4,128]{2,1,0:T(4,128)} %copy.103), kind=kCustom, calls=%fused_computation.7 | custom fusion | flops 131072 | bytes 1573888 | tf_op jit(solution)/shard_map/scatter-add | solution.py:72
  408.3 2.0 copy.104
  410.3 4.0 fusion.4
  414.3 2.2 copy.105
  416.6 9.5 all-gather
  426.1 0.1 reshape.244
  426.2 0.3 fusion.2
  426.5 1.4 fusion.44
  427.9 8.1 all-gather.1
  436.0 1.7 fusion.11
  437.7 0.6 fusion.40
  438.4 0.6 fusion.21
  440.3 0.2 scatter-add.29
  440.5 0.6 multiply_reduce_fusion.1
  441.1 337.4 %all-reduce.4.cloned.1.call-done = f32[16,10240]{1,0:T(8,128)} async-done(((f32[16,10240]{1,0:T(8,128)}), f32[16,10240]{1,0:T(8,128)}) %all-reduce.4.cloned.1.call-update) | async-done | bytes 655376 | tf_op jit(solution)/shard_map/psum | solution.py:112
  778.5 0.8 constant_dynamic-slice_fusion
  779.3 0.7 multiply_reduce_fusion.3
  781.3 105.1 %all-reduce.1 = (f32[]{:T(128)}, f32[]{:T(128)}) all-reduce(f32[]{:T(128)S(6)} %add.158, f32[]{:T(128)S(6)} %add.185), channel_id=1, replica_groups=mesh['herd'=128,'snp'=4] {'herd','snp'}, use_global_device_ids=true, to_apply=%region_2.3 | all-reduce | flops 2 | bytes 16 | tf_op jit(solution)/shard_map/psum | solution.py:124
  887.7 1.3 multiply_reduce_fusion
  889.0 1.2 multiply_reduce_fusion.2
  891.5 98.3 %psum.31 = f32[]{:T(128)} all-reduce(f32[]{:T(128)S(6)} %add.187), channel_id=1, replica_groups=mesh['herd'=128,'snp'=4] {'herd','snp'}, use_global_device_ids=true, to_apply=%region_17.18 | all-reduce | flops 1 | bytes 8 | tf_op jit(solution)/shard_map/psum | solution.py:132
  991.1 0.7 multiply_add_fusion
  991.8 0.6 multiply_add_fusion.2
  (57 shorter events, 0.4 us)
Async XLA Ops:
  7.2 419.0 %copy-start = (f32[4,16]{1,0:T(4,128)S(1)}, f32[4,16]{1,0:T(4,128)}, u32[]{:S(2)}) copy-start(f32[4,16]{1,0:T(4,128)} %param.31) | copy-start | bytes 772
  69.7 8.0 copy-start.2
  71.1 48.6 %all-to-all-start.1 = ((f32[4,128,256]{2,0,1:T(4,128)}), f32[4,128,256]{2,0,1:T(4,128)S(1)}, u32[]{:S(2)}, u32[]{:S(2)}) async-start(f32[4,128,256]{2,0,1:T(4,128)} %copy.97), calls=%async_computation.1 | async-start | bytes 1048576 | tf_op jit(solution)/shard_map/all_to_all | solution.py:41
  78.4 27.2 %copy-start.1 = (f32[4,4096]{0,1:T(8,128)}, f32[4,4096]{0,1:T(8,128)S(1)}, u32[]{:S(2)}) copy-start(f32[4,4096]{0,1:T(8,128)S(1)} %copy.99) | copy-start | bytes 196612
  78.4 26.6 %copy-start.11 = (s32[4096]{0:T(1024)S(1)}, s32[4096]{0:T(1024)}, u32[]{:S(2)}) copy-start(s32[4096]{0:T(1024)} %param.33) | copy-start | bytes 49156
  78.4 41.3 %copy-start.6 = (s32[4096]{0:T(1024)S(1)}, s32[4096]{0:T(1024)}, u32[]{:S(2)}) copy-start(s32[4096]{0:T(1024)} %param.32) | copy-start | bytes 49156
  194.6 26.2 %copy-start.7 = (f32[16,1,80]{2,1,0:T(1,128)S(1)}, f32[16,1,80]{2,1,0:T(1,128)}, u32[]{:S(2)}) copy-start(f32[16,1,80]{2,1,0:T(1,128)} %param.25) | copy-start | bytes 15364
  204.5 183.4 %all-to-all-start.2 = ((f32[4,128,256]{2,0,1:T(4,128)}), f32[4,128,256]{2,0,1:T(4,128)S(1)}, u32[]{:S(2)}, u32[]{:S(2)}) async-start(f32[4,128,256]{2,0,1:T(4,128)} %copy.101), calls=%async_computation.2 | async-start | bytes 1048576 | tf_op jit(solution)/shard_map/all_to_all | solution.py:65
  220.8 557.7 %all-reduce.4.cloned.1.call-start = ((), (), s32[]{:S(2)}) async-start(), calls=%async_computation.3 | async-start | bytes 1310720 | tf_op jit(solution)/shard_map/psum | solution.py:112
  223.5 119.3 %copy-start.12 = (f32[10240]{0:T(1024)S(1)}, f32[10240]{0:T(1024)}, u32[]{:S(2)}) copy-start(f32[10240]{0:T(1024)} %param.28) | copy-start | bytes 122884
  223.5 119.3 %copy-start.3 = (bf16[32,10240]{1,0:T(8,128)(2,1)S(1)}, bf16[32,10240]{1,0:T(8,128)(2,1)}, u32[]{:S(2)}) copy-start(bf16[32,10240]{1,0:T(8,128)(2,1)} %param.27) | copy-start | bytes 1966084
  342.8 19.1 %copy-start.8 = (f32[4096]{0:T(1024)S(1)}, f32[4096]{0:T(1024)}, u32[]{:S(2)}) copy-start(f32[4096]{0:T(1024)} %get-tuple-element.47) | copy-start | bytes 49156
  414.3 11.9 %copy-start.9 = (f32[4,4096]{1,0:T(4,128)S(1)}, f32[4,4096]{1,0:T(4,128)}, u32[]{:S(2)}) copy-start(f32[4,4096]{1,0:T(4,128)} %param.21) | copy-start | bytes 196612
  414.3 12.2 %copy-start.16 = (f32[4]{0:T(128)S(1)}, f32[4]{0:T(128)}, u32[]{:S(2)}) copy-start(f32[4]{0:T(128)} %param.29) | copy-start | bytes 52
  416.5 21.2 %copy-start.13 = (f32[16,1,80]{2,1,0:T(1,128)S(1)}, f32[16,1,80]{2,1,0:T(1,128)}, u32[]{:S(2)}) copy-start(f32[16,1,80]{2,1,0:T(1,128)} %param.24) | copy-start | bytes 15364
  416.5 21.2 %copy-start.14 = (f32[16,1,80]{2,1,0:T(1,128)S(1)}, f32[16,1,80]{2,1,0:T(1,128)}, u32[]{:S(2)}) copy-start(f32[16,1,80]{2,1,0:T(1,128)} %param.26) | copy-start | bytes 15364
  416.5 21.8 %copy-start.4 = (f32[4,4096]{1,0:T(4,128)S(1)}, f32[4,4096]{1,0:T(4,128)}, u32[]{:S(2)}) copy-start(f32[4,4096]{1,0:T(4,128)} %param.22) | copy-start | bytes 196612
  416.6 21.8 %copy-start.5 = (f32[4,4096]{1,0:T(4,128)S(1)}, f32[4,4096]{1,0:T(4,128)}, u32[]{:S(2)}) copy-start(f32[4,4096]{1,0:T(4,128)} %param.19) | copy-start | bytes 196612
  416.6 362.7 %copy-start.17 = (f32[16]{0:T(128)S(1)}, f32[16]{0:T(128)}, u32[]{:S(2)}) copy-start(f32[16]{0:T(128)} %param.30) | copy-start | bytes 196
  416.6 574.5 %copy-start.10 = (f32[4,4096]{1,0:T(4,128)S(1)}, f32[4,4096]{1,0:T(4,128)}, u32[]{:S(2)}) copy-start(f32[4,4096]{1,0:T(4,128)} %param.18) | copy-start | bytes 196612
  426.1 565.7 %copy-start.15 = (f32[16,1,80]{2,1,0:T(1,128)S(1)}, f32[16,1,80]{2,1,0:T(1,128)}, u32[]{:S(2)}) copy-start(f32[16,1,80]{2,1,0:T(1,128)} %param.23) | copy-start | bytes 15364
Sparse Core Ops, SparseCore 0:
  437.8 340.6 all-reduce.3
where the time goes:
time: 1000 us; the launch traced here: 999 us
  blocking collectives  385 us (38%)
  waiting for transfers between devices  337 us (34%)
  other arithmetic  117 us (12%)
  local copies, waits for them, and re-layouts  105 us (10%)
  starting transfers between devices  22.9 us (2%)
  between operations  21.7 us (2%)
  matrix products  10.3 us (1%)
    psum x1, waiting for transfers between devices, body(): summed = lax.psum(totals_all, 'herd')  337 us
    all_gather x1, blocking collectives, body(): lax.all_gather(dir_a, 'herd', axis=2, tiled=True)[:, 0, :]  119 us
    psum x1, blocking collectives, body(): norm_now = lax.psum(local_norm, ('herd', 'snp'))  105 us
    psum x1, blocking collectives, body(): norm_next = lax.psum(local_next, ('herd', 'snp'))  98.3 us
    all_to_all x1, blocking collectives, pedigree(): lax.all_to_all(wanted, 'herd', split_axis=0, concat_axis=0, tiled=True)  35.4 us
    scatter-add x1, other arithmetic, pedigree(): outbound = jnp.zeros((traits_here, herd_count * span + 1), jnp.float32).a...  31.1 us
    gather x1, local copies, waits for them, and re-layouts, pedigree(): slot_index = slot_order[owner_herd, block_index]  26.5 us
    scatter-add x1, other arithmetic, pedigree(): dam_terms = jnp.zeros((traits_here, animals + 1), jnp.float32).at[:, dam_...  25.9 us
  transfers between devices with their start and end apart: 3, of which 1 were waited for; matrix products, arithmetic and copies ran while one was open for 8% of the time, Pallas kernels for 0%

commit v1 on v0

v1 whole, which is shorter than its diff:
```python
import functools
import math

import jax
import jax.numpy as jnp
from jax import lax
from jax.experimental import pallas as pl
from jax.experimental.pallas import tpu as pltpu
from jax.sharding import Mesh, PartitionSpec as P

SLOTS = 2
CAP = 64
CHUNK = 512
HERD = ("y", "z", "c")
F32 = jnp.float32
BF16 = jnp.bfloat16
NT = (((1,), (1,)), ((), ()))
TN = (((0,), (0,)), ((), ()))
NN = (((1,), (0,)), ((), ()))


def call(kernel, out, scratch=(), specs=None, flops=10**8, **kw):
    return pl.pallas_call(
        kernel,
        out_shape=out,
        scratch_shapes=list(scratch),
        compiler_params=pltpu.CompilerParams(vmem_limit_bytes=40 * 2**20),
        **kw,
    )


def dot(a, b, dims=NN):
    return lax.dot_general(a, b, dims, preferred_element_type=F32)


def parts(x, n=2):
    out = []
    for _ in range(n):
        p = x.astype(BF16).astype(F32)
        out.append(p)
        x = x - p
    return out


def rows_at(n, cols):
    return lax.broadcasted_iota(jnp.int32, (n, cols), 0)


def weights(sire, dam):
    known = (sire >= 0).astype(jnp.int32) + (dam >= 0).astype(jnp.int32)
    return jnp.where(known == 2, 2.0, jnp.where(known == 1, 4.0 / 3.0, 1.0)).astype(F32)


def dam_place(dam, animals):
    local = dam & (animals - 1)
    block = jnp.where(dam >= 0, local >> 7, -1)
    return block, local & 127


def lists_kernel(dir_ref, g_ref, sire_ref, dam_ref, pay_ref, c_ref, tab_ref, rank_ref, v_ref, acc_ref):
    traits, animals = v_ref.shape
    herd = pay_ref.shape[0]
    blocks = animals // 128
    n = CHUNK
    v_ref[...] = lax.dot_general(
        g_ref[...], dir_ref[...], NN, precision=lax.Precision.HIGHEST, preferred_element_type=F32
    )
    for t in range(traits):
        for b in range(blocks):
            tab_ref[t * blocks + b : t * blocks + b + 1, :] = v_ref[t : t + 1, b * 128 : (b + 1) * 128]
    table = jnp.concatenate([p.astype(BF16) for p in parts(tab_ref[...])], axis=0)
    half = traits * blocks
    before = (rows_at(n, n) < lax.broadcasted_iota(jnp.int32, (n, n), 1)).astype(F32).astype(BF16)
    acc_ref[...] = jnp.zeros(acc_ref.shape, F32)

    def step(k, carry):
        at = pl.ds(pl.multiple_of(k * n, n), n)
        sire = sire_ref[:, at]
        dam = dam_ref[:, at]
        weight = weights(sire, dam)
        block, offset = dam_place(dam, animals)
        hit = (rows_at(128, n) == offset).astype(F32).astype(BF16)
        found = dot(table, hit)
        found = found[:half] + found[half:]
        in_block = rows_at(blocks, n) == block
        own = v_ref[:, at]
        terms = []
        for t in range(traits):
            dam_value = jnp.sum(
                jnp.where(in_block, found[t * blocks : (t + 1) * blocks], 0.0), axis=0, keepdims=True
            )
            terms.append(weight * (own[t : t + 1] - 0.5 * dam_value))
            c_ref[t : t + 1, at] = terms[t]
        owner = sire >> (animals.bit_length() - 1)
        is_owner = rows_at(herd, n) == owner
        owners = is_owner.astype(F32).astype(BF16)
        earlier = dot(owners, before) + carry
        rank = jnp.sum(jnp.where(is_owner, earlier, 0.0), axis=0, keepdims=True).astype(jnp.int32)
        rank = jnp.where(sire >= 0, rank, -1)
        rank_ref[:, at] = rank
        in_slot = rows_at(CAP, n) == rank
        local = (sire & (animals - 1)) + 1
        high = [(local & ~63).astype(F32), weight * 1.5]
        low = [(local & 63).astype(F32), jnp.zeros((1, n), F32)]
        for value in terms:
            hi, lo = parts(value)
            high.append(hi)
            low.append(lo)
        fields = jnp.concatenate(
            [jnp.where(in_slot, f, 0.0).astype(BF16) for f in high + low], axis=0
        )
        acc_ref[...] += dot(owners, fields, NT)
        return carry + jnp.sum(jnp.where(is_owner, 1.0, 0.0), axis=1, keepdims=True)

    count = lax.fori_loop(0, animals // n, step, jnp.zeros((herd, 1), F32))
    width = pay_ref.shape[1]
    overflow = jnp.where(jnp.max(count, axis=0, keepdims=True) > CAP + 0.5, 16.0, 0.0)
    lane = lax.broadcasted_iota(jnp.int32, (herd, width), 1)
    flag = jnp.where((lane >= CAP) & (lane < 2 * CAP), overflow, 0.0)
    pay_ref[...] = acc_ref[:, :width] + acc_ref[:, width:] + flag


def owner_kernel(got_ref, tab_ref, out_ref, inc_ref, over_ref, turned_ref, vals_ref, acc_ref):
    herd = got_ref.shape[0]
    half = tab_ref.shape[0]
    blocks = 32
    traits = half // blocks
    for j in range(got_ref.shape[1] // 128):
        turned_ref[j * 128 : (j + 1) * 128, :] = got_ref[:, j * 128 : (j + 1) * 128].T
    weight_rows = turned_ref[CAP : 2 * CAP, :]
    over_ref[...] = jnp.broadcast_to(jnp.max(weight_rows, keepdims=True), over_ref.shape)
    table = jnp.concatenate([p.astype(BF16) for p in parts(tab_ref[...])], axis=0)
    acc_ref[...] = jnp.zeros(acc_ref.shape, F32)
    group = 8
    n = group * herd

    def flat(first):
        tile = turned_ref[pl.ds(first, group), :]
        return jnp.concatenate([tile[j : j + 1] for j in range(group)], axis=1)

    def step(k, _):
        r = pl.multiple_of(k * group, group)
        place = flat(r).astype(jnp.int32) - 1
        block = place >> 7
        hit = (rows_at(128, n) == (place & 127)).astype(F32).astype(BF16)
        in_block = rows_at(blocks, n) == block
        found = dot(table, hit)
        found = found[:half] + found[half:]
        high, low = [], []
        for t in range(traits):
            value = jnp.sum(
                jnp.where(in_block, found[t * blocks : (t + 1) * blocks], 0.0), axis=0, keepdims=True
            )
            vals_ref[pl.ds(t * CAP + r, group), :] = jnp.concatenate(
                [value[:, j * herd : (j + 1) * herd] for j in range(group)], axis=0
            )
            hi, lo = parts(flat(2 * CAP + t * CAP + r))
            high.append(hi)
            low.append(lo)
        weight = flat(CAP + r)
        weight = jnp.where(weight >= 8.0, weight - 16.0, weight)
        fields = jnp.concatenate(
            [jnp.where(in_block, f, 0.0).astype(BF16) for f in high + low + [weight]], axis=0
        )
        acc_ref[...] += dot(fields, hit, NT)
        return 0

    lax.fori_loop(0, CAP // group, step, 0)
    out_ref[...] = vals_ref[...].T
    weight_sum = acc_ref[2 * half :, :] * (0.25 / 1.5)
    for t in range(traits):
        at = slice(t * blocks, (t + 1) * blocks)
        sums = acc_ref[at, :] + acc_ref[half + t * blocks : half + (t + 1) * blocks, :]
        inc_ref[at, :] = weight_sum * tab_ref[at, :] - 0.5 * sums


def image_kernel(
    got_ref, c_ref, rank_ref, sire_ref, dam_ref, inc_ref, resid_ref,
    dir_ref, rec_ref, res_ref, inv_ref,
    back_ref, ridge_ref, dir_a_ref, res_a_ref, inv_a_ref,
    image_ref, image_a_ref, sums_ref, acc_ref, tab_ref,
):
    traits, animals = c_ref.shape
    herd = got_ref.shape[0]
    blocks = animals // 128
    n = CHUNK
    half = traits * blocks
    table = jnp.concatenate([p.astype(BF16) for p in parts(got_ref[...])], axis=1)
    wide = traits * CAP
    acc_ref[...] = jnp.zeros(acc_ref.shape, F32)

    def step(k, _):
        at = pl.ds(pl.multiple_of(k * n, n), n)
        sire = sire_ref[:, at]
        dam = dam_ref[:, at]
        weight = weights(sire, dam)
        owner = sire >> (animals.bit_length() - 1)
        owners = (rows_at(herd, n) == owner).astype(F32).astype(BF16)
        found = dot(table, owners, TN)
        found = found[:wide] + found[wide:]
        in_slot = rows_at(CAP, n) == rank_ref[:, at]
        block, offset = dam_place(dam, animals)
        in_block = rows_at(blocks, n) == block
        hit = (rows_at(128, n) == offset).astype(F32).astype(BF16)
        high, low = [], []
        for t in range(traits):
            sire_value = jnp.sum(
                jnp.where(in_slot, found[t * CAP : (t + 1) * CAP], 0.0), axis=0, keepdims=True
            )
            scaled = c_ref[t : t + 1, at] - 0.5 * weight * sire_value
            image_ref[t : t + 1, at] = scaled
            hi, lo = parts(scaled)
            high.append(hi)
            low.append(lo)
        fields = jnp.concatenate(
            [jnp.where(in_block, f, 0.0).astype(BF16) for f in high + low], axis=0
        )
        acc_ref[...] += dot(fields, hit, NT)
        return 0

    lax.fori_loop(0, animals // n, step, 0)
    tab_ref[...] = inc_ref[...] - 0.5 * (acc_ref[:half, :] + acc_ref[half:, :])
    for b in range(blocks):
        for t in range(traits):
            at = (slice(t, t + 1), slice(b * 128, (b + 1) * 128))
            image_ref[at] = image_ref[at] + tab_ref[t * blocks + b : t * blocks + b + 1, :]
    image_ref[:, :128] = image_ref[:, :128] + resid_ref[...]
    direction = dir_ref[...]
    image = image_ref[...] + rec_ref[...] * direction
    image_ref[...] = image
    res = res_ref[...]
    inv = inv_ref[...]
    columns = dir_a_ref.shape[1]
    back = jnp.sum(back_ref[...], axis=0)[:, :columns]
    dir_a = dir_a_ref[...]
    image_a = ridge_ref[...] * dir_a - back
    image_a_ref[...] = image_a
    res_a = res_a_ref[...]
    inv_a = inv_a_ref[...]
    weighted, weighted_a = inv * res, inv_a * res_a
    lane = lax.broadcasted_iota(jnp.int32, (1, 128), 1)
    pairs = (
        (weighted * res, weighted_a * res_a),
        (direction * image, dir_a * image_a),
        (weighted * image, weighted_a * image_a),
        (inv * image * image, inv_a * image_a * image_a),
    )
    total = jnp.zeros((1, 128), F32)
    for j, (one, two) in enumerate(pairs):
        value = jnp.sum(one, keepdims=True) + jnp.sum(two, keepdims=True)
        total = jnp.where(lane == j, value, total)
    sums_ref[...] = total


def join_kernel(in_ref, out_ref, *, columns):
    cores, zs, traits, _ = in_ref.shape
    lane = lax.broadcasted_iota(jnp.int32, (traits, 128), 1)
    for k in range(out_ref.shape[1] // 128):
        tile = jnp.zeros((traits, 128), F32)
        for p in range(cores * zs):
            off = p * columns - k * 128
            if off <= -columns or off >= 128:
                continue
            piece = in_ref[p % cores, p // cores]
            if off % 128:
                piece = pltpu.roll(piece, off % 128, 1)
            tile = jnp.where((lane >= off) & (lane < off + columns), piece, tile)
        out_ref[:, k * 128 : (k + 1) * 128] = tile


def part_kernel(in_ref, out_ref, *, columns):
    cores, zs, traits, _ = out_ref.shape
    total = in_ref[0]
    for y in range(1, in_ref.shape[0]):
        total = total + in_ref[y]
    lane = lax.broadcasted_iota(jnp.int32, (traits, 128), 1)
    for p in range(cores * zs):
        first = p * columns
        k, off = first // 128, first % 128
        piece = total[:, k * 128 : (k + 1) * 128]
        if off:
            piece = pltpu.roll(piece, 128 - off, 1)
        if off + columns > 128:
            nxt = pltpu.roll(total[:, (k + 1) * 128 : (k + 2) * 128], 128 - off, 1)
            piece = jnp.where(lane < 128 - off, piece, nxt)
        out_ref[p % cores, p // cores] = jnp.where(lane < columns, piece, 0.0)


def predict_kernel(dir_ref, geno_ref, freq_ref, gw_ref, out_ref, *, scale):
    ys, traits, width = dir_ref.shape
    genotyped = geno_ref.shape[0]
    total = jnp.zeros((3 * traits, genotyped), F32)
    bias = jnp.zeros((traits, 1), F32)
    for y in range(ys):
        at = slice(y * width, (y + 1) * width)
        values = dir_ref[y]
        stack = jnp.concatenate([p.astype(BF16) for p in parts(values, 3)], axis=0)
        total = total + dot(stack, geno_ref[:, at], NT)
        bias = bias + jnp.sum(values * (2.0 * freq_ref[:, at]), axis=1, keepdims=True)
    rows = total[:traits] + total[traits : 2 * traits] + total[2 * traits :]
    out_ref[...] = jnp.zeros(out_ref.shape, F32)
    out_ref[:, :genotyped] = (rows - bias) * scale
    out_ref[:, genotyped : genotyped + 1] = gw_ref[...]


def back_kernel(pred_ref, dir_ref, geno_ref, freq_ref, out_ref, resid_ref, *, scale):
    ys, traits, width = out_ref.shape
    genotyped = geno_ref.shape[0]
    total = pred_ref[0]
    for x in range(1, pred_ref.shape[0]):
        total = total + pred_ref[x]
    lane = lax.broadcasted_iota(jnp.int32, (traits, 128), 1)
    weight = jnp.sum(jnp.where(lane == genotyped, total, 0.0), axis=1, keepdims=True)
    resid = jnp.where(lane < genotyped, weight * (dir_ref[...] - total), 0.0)
    resid_ref[...] = resid
    stack = jnp.concatenate([p.astype(BF16) for p in parts(resid, 3)], axis=0)[:, :genotyped]
    summed = jnp.sum(resid, axis=1, keepdims=True)
    for y in range(ys):
        at = slice(y * width, (y + 1) * width)
        found = dot(stack, geno_ref[:, at])
        found = found[:traits] + found[traits : 2 * traits] + found[2 * traits :]
        out_ref[y] = (found - summed * (2.0 * freq_ref[:, at])) * scale


def update_kernel(
    sums_ref, sol_ref, res_ref, dir_ref, inv_ref, image_ref,
    sol_a_ref, res_a_ref, dir_a_ref, inv_a_ref, image_a_ref,
    nsol_ref, nres_ref, ndir_ref, nsol_a_ref, nres_a_ref, ndir_a_ref,
):
    total = jnp.sum(sums_ref[...], axis=0)
    norm, curve, cross, square = (total[:, j : j + 1] for j in range(4))
    size = norm / curve
    following = norm - 2.0 * size * cross + size * size * square
    ratio = following / norm
    for sol, res, dire, inv, image, nsol, nres, ndir in (
        (sol_ref, res_ref, dir_ref, inv_ref, image_ref, nsol_ref, nres_ref, ndir_ref),
        (sol_a_ref, res_a_ref, dir_a_ref, inv_a_ref, image_a_ref, nsol_a_ref, nres_a_ref, ndir_a_ref),
    ):
        d = dire[...]
        nsol[...] = sol[...] + size * d
        left = res[...] - size * image[...]
        nres[...] = left
        ndir[...] = inv[...] * left + ratio * d


def pedigree_by_blocks(field, sire, dam, herd_count, herd_index):
    traits_here, animals = field.shape
    block_count = animals // 128
    span = SLOTS * 128
    has_sire = sire >= 0
    has_dam = dam >= 0
    sire_known = has_sire.astype(F32)
    dam_known = has_dam.astype(F32)
    owner_herd = jnp.where(has_sire, sire // animals, 0)
    block_index = jnp.where(has_sire, sire % animals // 128, 0)
    offset = jnp.where(has_sire, sire % 128, 0)
    flat_block = jnp.where(
        has_sire, owner_herd * block_count + block_index, herd_count * block_count
    )
    present = jnp.zeros((herd_count * block_count + 1,), jnp.int32).at[flat_block].max(1)
    present = present[:-1].reshape(herd_count, block_count)
    slot_order = jnp.cumsum(present, axis=1) - 1
    slot_range = jnp.arange(SLOTS, dtype=jnp.int32)
    slot_match = (present[:, :, None] == 1) & (slot_order[:, :, None] == slot_range[None, None, :])
    block_ids = jnp.arange(block_count, dtype=jnp.int32)[None, :, None] + 1
    wanted = jnp.sum(jnp.where(slot_match, block_ids, 0), axis=1) - 1
    requests = lax.all_to_all(wanted, HERD, split_axis=0, concat_axis=0, tiled=True)
    live_slot = requests >= 0
    field_tiles = field.reshape(traits_here, block_count, 128)
    outgoing = field_tiles[:, jnp.where(live_slot, requests, 0), :]
    outgoing = jnp.where(live_slot[None, :, :, None], outgoing, 0.0).reshape(
        traits_here, herd_count, span
    )
    fetched = lax.all_to_all(outgoing, HERD, split_axis=1, concat_axis=1, tiled=True).reshape(
        traits_here, herd_count * span
    )
    slot_index = slot_order[owner_herd, block_index]
    buffer_place = owner_herd * span + slot_index * 128 + offset
    sire_values = fetched[:, jnp.where(has_sire, buffer_place, 0)]
    local_dam = jnp.where(has_dam, dam - herd_index * animals, 0)
    dam_values = field[:, local_dam]
    weight = 4.0 / (4.0 - sire_known - dam_known)
    scaled = weight * (field - 0.5 * sire_known * sire_values - 0.5 * dam_known * dam_values)
    dam_target = jnp.where(has_dam, local_dam, animals)
    dam_terms = (
        jnp.zeros((traits_here, animals + 1), F32).at[:, dam_target].add(-0.5 * dam_known * scaled)
    )
    result = scaled + dam_terms[:, :animals]
    sire_target = jnp.where(has_sire, buffer_place, herd_count * span)
    outbound = (
        jnp.zeros((traits_here, herd_count * span + 1), F32)
        .at[:, sire_target]
        .add(-0.5 * sire_known * scaled)
    )
    outbound = outbound[:, :-1].reshape(traits_here, herd_count, span)
    returned = lax.all_to_all(outbound, HERD, split_axis=1, concat_axis=1, tiled=True).reshape(
        traits_here, herd_count * SLOTS, 128
    )
    block_target = jnp.where(live_slot, requests, block_count).reshape(herd_count * SLOTS)
    incoming = (
        jnp.zeros((traits_here, block_count + 1, 128), F32).at[:, block_target, :].add(returned)
    )
    return result + incoming[:, :block_count, :].reshape(traits_here, animals)


def body(
    sol_u, res_u, dir_u, rec_weight, inv_diag_u, sol_a, res_a, dir_a, inv_diag_a,
    genotypes, allele_freq, geno_weight, snp_ridge, genetic_inv, sire, dam,
):
    ny, nz, nc, nx = (lax.axis_size(a) for a in ("y", "z", "c", "x"))
    herd = ny * nz * nc
    herd_index = lax.axis_index(HERD)
    x_index = lax.axis_index("x")
    traits_here, animals = dir_u.shape
    traits, _, columns = dir_a.shape
    genotyped, snps = genotypes.shape
    blocks = animals // 128
    scale = 2.0 / math.sqrt(snps * nx)
    width = snps // ny
    sds = lambda *shape: jax.ShapeDtypeStruct(shape, F32)
    d_a, r_a, s_a, i_a = (a[:, 0, :] for a in (dir_a, res_a, sol_a, inv_diag_a))
    freq = allele_freq[None, :]
    sire_row, dam_row = sire[None, :], dam[None, :]

    dir_all = lax.all_gather(dir_u, "x", axis=0, tiled=True)
    padded = jnp.pad(d_a, ((0, 0), (0, 128 - columns)))
    along_z = lax.all_to_all(
        jnp.broadcast_to(padded[None], (nz, traits, 128)), "z", 0, 0, tiled=True
    )
    both_cores = lax.all_gather(along_z, "c", axis=0)
    joined = call(functools.partial(join_kernel, columns=columns), sds(traits, width))(both_cores)
    dir_block = lax.all_gather(joined, "y", axis=0)

    lists, c_term, table, rank = call(
        lists_kernel,
        (
            sds(herd, (2 + traits_here) * CAP),
            sds(traits_here, animals),
            sds(traits_here * blocks, 128),
            jax.ShapeDtypeStruct((1, animals), jnp.int32),
        ),
        scratch=[
            pltpu.VMEM((traits_here, animals), F32),
            pltpu.VMEM((herd, 2 * (2 + traits_here) * CAP), F32),
        ],
    )(dir_all, genetic_inv, sire_row, dam_row)
    got_lists = lax.all_to_all(lists[:, None, :], HERD, 0, 0, tiled=True)[:, 0, :]

    weight_here = lax.dynamic_update_slice(
        jnp.zeros((traits, 1), F32), geno_weight[:, None], (x_index * traits_here, 0)
    )
    predicted = call(functools.partial(predict_kernel, scale=scale), sds(traits, 128))(
        dir_block, genotypes, freq, weight_here
    )
    all_predicted = lax.all_gather(predicted, "x", axis=0)
    back, resid = call(
        functools.partial(back_kernel, scale=scale), (sds(ny, traits, width), sds(traits, 128))
    )(all_predicted, dir_all[:, :128], genotypes, freq)
    back_y = lax.all_to_all(back, "y", 0, 0, tiled=True)

    values, incoming, over = call(
        owner_kernel,
        (sds(herd, traits_here * CAP), sds(traits_here * blocks, 128), sds(8, 128)),
        scratch=[
            pltpu.VMEM(((2 + traits_here) * CAP, herd), F32),
            pltpu.VMEM((traits_here * CAP, herd), F32),
            pltpu.VMEM((2 * traits_here * blocks + blocks, 128), F32),
        ],
    )(got_lists, table)
    got_values = lax.all_to_all(values[:, None, :], HERD, 0, 0, tiled=True)[:, 0, :]

    pieces = call(
        functools.partial(part_kernel, columns=columns), sds(nc, nz, traits, 128)
    )(back_y)
    back_c = jnp.sum(lax.all_to_all(pieces, "c", 0, 0, tiled=True).reshape(nc, nz, traits, 128), axis=0)
    back_z = lax.all_to_all(back_c, "z", 0, 0, tiled=True)

    own_resid = lax.dynamic_slice_in_dim(resid, x_index * traits_here, traits_here, 0)
    image_u, image_a, sums = call(
        image_kernel,
        (sds(traits_here, animals), sds(traits, columns), sds(1, 128)),
        scratch=[
            pltpu.VMEM((2 * traits_here * blocks, 128), F32),
            pltpu.VMEM((traits_here * blocks, 128), F32),
        ],
    )(
        got_values, c_term, rank, sire_row, dam_row, incoming, own_resid,
        dir_u, rec_weight, res_u, inv_diag_u,
        back_z, snp_ridge[:, None], d_a, r_a, i_a,
    )

    def by_blocks():
        mixed = jnp.dot(genetic_inv, dir_all, precision=lax.Precision.HIGHEST)
        image = rec_weight * dir_u + pedigree_by_blocks(mixed, sire, dam, herd, herd_index)
        image = image.at[:, :genotyped].add(own_resid[:, :genotyped])
        cells = [
            jnp.sum(inv_diag_u * res_u * res_u) + jnp.sum(i_a * r_a * r_a),
            jnp.sum(dir_u * image) + jnp.sum(d_a * image_a),
            jnp.sum(inv_diag_u * res_u * image) + jnp.sum(i_a * r_a * image_a),
            jnp.sum(inv_diag_u * image * image) + jnp.sum(i_a * image_a * image_a),
        ]
        return image, jnp.pad(jnp.stack(cells), (0, 124))[None, :]

    image_u, sums = lax.cond(over[0, 0] >= 8.0, by_blocks, lambda: (image_u, sums))

    near = lax.all_to_all(
        jnp.broadcast_to(sums[None], (ny * nc * nx, 1, 128)), ("y", "c", "x"), 0, 0, tiled=True
    )
    near = jnp.sum(near, axis=0, keepdims=True)
    far = lax.all_to_all(jnp.broadcast_to(near, (nz, 1, 128)), "z", 0, 0, tiled=True)

    u, a = sds(traits_here, animals), sds(traits, columns)
    outs = call(update_kernel, (u, u, u, a, a, a))(
        far, sol_u, res_u, dir_u, inv_diag_u, image_u, s_a, r_a, d_a, i_a, image_a
    )
    return tuple(outs[:3]) + tuple(o[:, None, :] for o in outs[3:])


def solution(mesh):
    herd, nx = mesh.devices.shape
    ny, nc = (4, 2) if herd == 128 else (2, 2)
    grid = Mesh(mesh.devices.reshape(ny, herd // (ny * nc), nc, nx), ("y", "z", "c", "x"))
    u = P("x", HERD)
    a = P(None, "x", HERD)
    return jax.shard_map(
        body,
        mesh=grid,
        in_specs=(
            u, u, u, u, u, a, a, a, a,
            P(HERD, "x"), P("x"), P("x"), P(), P("x", None), P(HERD), P(HERD),
        ),
        out_specs=(u, u, u, a, a, a),
        check_vma=False,
    )
```

time: 1000 us -> 188 us (0.19)
  blocking collectives: 385 us -> 75.8 us
  waiting for transfers between devices: 337 us -> 29.9 us
  other arithmetic: 117 us -> 0.67 us
  local copies, waits for them, and re-layouts: 105 us -> 3.99 us
  starting transfers between devices: 22.9 us -> 55.4 us
  between operations: 21.7 us -> 1.6 us
  Pallas kernels: 0 us -> 19.6 us
  matrix products: 10.3 us -> 0 us
    psum x1 -> x0, waiting for transfers between devices: 337 us -> none  [body(): summed = lax.psum(totals_all, 'herd')]
    psum x2 -> x0, blocking collectives: 203 us -> none  [the longest x1 105 us: body(): norm_now = lax.psum(local_norm, ('herd', 'snp'))]
    all_gather x3 -> x4, blocking collectives: 137 us -> 35 us  [the longest x1 12.4 us: body(): dir_block = lax.all_gather(joined, 'y', axis=0)]
    scatter-add x3 -> x0, other arithmetic: 74.3 us -> none  [the longest x1 31.1 us: pedigree(): outbound = jnp.zeros((traits_here, herd_count * span + 1), jnp.float32).a...]
    gather x5 -> x0, local copies, waits for them, and re-layouts: 62.5 us -> none  [the longest x1 26.5 us: pedigree(): slot_index = slot_order[owner_herd, block_index]]
    all_to_all x2 -> x5, starting transfers between devices: 22.8 us -> 55.4 us  [the longest x1 18.8 us: body(): lax.all_to_all(lists[:, None, :], HERD, 0, 0, tiled=True)[:, 0, :]]
    all_to_all x2 -> x5, waiting for transfers between devices: 0.01 us -> 29.9 us  [the longest x1 16.7 us: body(): lax.all_to_all(values[:, None, :], HERD, 0, 0, tiled=True)[:, 0, :]]
    another operation x3 -> x0, other arithmetic: 23.1 us -> none  [the longest x1 22.4 us: pedigree(): jnp.zeros((herd_count * block_count + 1,), jnp.int32).at[flat_block].max(1)]
  transfers between devices with their start and end apart: 3 -> 5, of which waited for: 1 -> 3; matrix products, arithmetic and copies ran while one was open for 8% -> 2% of each run, Pallas kernels for 0% -> 7%
where the time goes in v1:
time: 188 us; the launch traced here: 187 us
  blocking collectives  75.8 us (40%)
  starting transfers between devices  55.4 us (29%)
  waiting for transfers between devices  29.9 us (16%)
  Pallas kernels  19.6 us (10%)
  local copies, waits for them, and re-layouts  3.99 us (2%)
    all_to_all x1, starting transfers between devices, body(): lax.all_to_all(lists[:, None, :], HERD, 0, 0, tiled=True)[:, 0, :]  18.8 us
    all_to_all x1, waiting for transfers between devices, body(): lax.all_to_all(values[:, None, :], HERD, 0, 0, tiled=True)[:, 0, :]  16.7 us
    all_to_all x1, blocking collectives, body(): lax.all_to_all(jnp.broadcast_to(sums[None], (ny * nc * nx, 1, 128)), ('y'...  15.9 us
    all_to_all x1, starting transfers between devices, body(): lax.all_to_all(jnp.broadcast_to(padded[None], (nz, traits, 128)), 'z', 0,...  15.7 us
    all_to_all x1, blocking collectives, body(): lax.all_to_all(jnp.broadcast_to(near, (nz, 1, 128)), 'z', 0, 0, tiled=True)  14.7 us
    all_to_all x1, starting transfers between devices, body(): lax.all_to_all(values[:, None, :], HERD, 0, 0, tiled=True)[:, 0, :]  13.7 us
    all_gather x1, blocking collectives, body(): dir_block = lax.all_gather(joined, 'y', axis=0)  12.4 us
    all_gather x1, blocking collectives, body(): dir_all = lax.all_gather(dir_u, 'x', axis=0, tiled=True)  10.8 us
  transfers between devices with their start and end apart: 5, of which 3 were waited for; matrix products, arithmetic and copies ran while one was open for 2% of the time, Pallas kernels for 7%

profile of v1, /device:TPU:1, one launch (start us, length us, event | category | flops | bytes accessed | tf_op | source)
XLA Modules:
  0.0 187.0 jit_solution(7108033243470138059)
XLA Ops:
  0.6 0.0 copy-start.14
  0.6 0.0 copy-start
  0.7 0.0 copy-start.1
  0.7 0.8 pad.10
  1.4 0.6 broadcast_in_dim.129
  2.1 15.7 %all-to-all-start.5 = ((f32[16,16,128]{2,1,0:T(8,128)}), f32[16,16,128]{2,1,0:T(8,128)S(1)}, u32[]{:S(2)}, u32[]{:S(2)}) async-start(f32[16,16,128]{2,1,0:T(8,128)} %broadcast_in_dim.129), calls=%async_computation.5 | async-start | bytes 262144 | tf_op jit(solution)/shard_map/all_to_all | solution.py:427
  17.8 10.8 %all-gather.3 = f32[4,4,4096]{2,1,0:T(4,128)S(1)} all-gather(f32[1,4,4096]{2,1,0:T(4,128)} %bitcast.94), channel_id=1, replica_groups=mesh['y'=4,'z'=16,'c'=2,'x'=4] {'x'}, dimensions={0}, use_global_device_ids=true | all-gather | bytes 327680 | tf_op jit(solution)/shard_map/all_gather | solution.py:425
  28.6 0.1 reshape.254.dir_ref
  28.7 6.5 %shard_map.199 = (f32[128,384]{1,0:T(8,128)S(1)}, f32[4,4096]{1,0:T(4,128)S(1)}, f32[128,128]{1,0:T(8,128)S(1)}, s32[1,4096]{1,0:T(1,128)S(1)}) custom-call(f32[16,4096]{1,0:T(8,128)S(1)} %reshape.254.dir_ref, f32[4,16]{1,0:T(4,128)} %g_ref.1, s32[1,4096]{1,0:T(1,128)} %bitcast.96, s32[1,4096]{1,0:T(1,128)} %bitcast.98), custom_call_target="tpu_custom_call" | custom-call | tf_op jit(solution)/shard_map/pallas_call | solution.py:434
  35.3 0.9 copy.185
  36.1 0.0 all-to-all-done.5
  36.1 18.8 %all-to-all-start.3 = ((f32[128,1,384]{2,1,0:T(1,128)}), f32[128,1,384]{2,1,0:T(1,128)S(1)}, u32[]{:S(2)}, u32[]{:S(2)}) async-start(f32[128,1,384]{2,1,0:T(1,128)} %copy.185), calls=%async_computation.3 | async-start | bytes 393216 | tf_op jit(solution)/shard_map/all_to_all | solution.py:447
  55.0 0.0 copy-done.14
  55.0 0.1 copy.187
  55.1 2.5 %all-gather = f32[32,16,128]{2,1,0:T(8,128)S(1)} all-gather(f32[16,16,128]{2,1,0:T(8,128)S(1)} %all-to-all-done.5), channel_id=2, replica_groups=mesh['y'=4,'z'=16,'c'=2,'x'=4] {'c'}, dimensions={0}, use_global_device_ids=true | all-gather | bytes 393216 | tf_op jit(solution)/shard_map/all_gather | solution.py:430
  57.6 0.2 shard_map.201
  57.8 12.4 %all-gather.1 = f32[64,2560]{1,0:T(8,128)S(1)} all-gather(f32[16,2560]{1,0:T(8,128)S(1)} %shard_map.201), channel_id=3, replica_groups=mesh['y'=4,'z'=16,'c'=2,'x'=4] {'y'}, dimensions={0}, use_global_device_ids=true | all-gather | bytes 819200 | tf_op jit(solution)/shard_map/all_gather | solution.py:432
  70.2 0.0 copy-done
  70.2 0.0 copy-done.1
  70.2 0.5 shard_map.202
  70.7 9.3 %all-gather.2 = f32[64,128]{1,0:T(8,128)S(1)} all-gather(f32[16,128]{1,0:T(8,128)S(1)} %shard_map.202), channel_id=4, replica_groups=mesh['y'=4,'z'=16,'c'=2,'x'=4] {'x'}, dimensions={0}, use_global_device_ids=true | all-gather | bytes 40960 | tf_op jit(solution)/shard_map/all_gather | solution.py:455
  80.0 1.4 shard_map.203
  81.4 0.0 all-to-all-done.3
  81.4 0.0 copy-start.15
  81.4 3.6 %all-to-all-start.6 = ((f32[4,16,2560]{2,1,0:T(8,128)}), f32[4,16,2560]{2,1,0:T(8,128)S(1)}, u32[]{:S(2)}, u32[]{:S(2)}) async-start(f32[4,16,2560]{2,1,0:T(8,128)} %get-tuple-element.92), calls=%async_computation.6 | async-start | bytes 1310720 | tf_op jit(solution)/shard_map/all_to_all | solution.py:459
  85.0 0.0 copy-start.4
  85.0 0.0 copy-start.5
  85.0 0.0 copy-start.6
  85.0 0.0 copy-start.7
  85.0 0.0 copy-start.8
  85.1 0.0 copy-start.9
  85.1 0.0 copy-start.10
  85.1 0.0 copy-start.11
  85.1 0.0 copy-start.12
  85.1 0.0 copy-start.13
  85.1 4.2 %shard_map.200 = (f32[128,256]{1,0:T(8,128)S(1)}, f32[128,128]{1,0:T(8,128)S(1)}, f32[8,128]{1,0:T(8,128)S(1)}) custom-call(f32[128,384]{1,0:T(8,128)S(1)} %bitcast.81, f32[128,128]{1,0:T(8,128)S(1)} %get-tuple-element.85.tab_ref), custom_call_target="tpu_custom_call" | custom-call | tf_op jit(solution)/shard_map/pallas_call | solution.py:461
  89.3 0.8 copy.186
  90.1 2.5 %all-to-all-done.6.in_ref = f32[4,16,2560]{2,1,0:T(8,128)S(1)} async-done(((f32[4,16,2560]{2,1,0:T(8,128)}), f32[4,16,2560]{2,1,0:T(8,128)S(1)}, u32[]{:S(2)}, u32[]{:S(2)}) %all-to-all-start.6) | async-done | bytes 655392 | tf_op jit(solution)/shard_map/all_to_all | solution.py:459
  92.6 0.2 shard_map.204
  92.8 10.2 %all_to_all.57 = f32[2,16,16,128]{3,2,1,0:T(8,128)S(1)} all-to-all(f32[2,16,16,128]{3,2,1,0:T(8,128)S(1)} %shard_map.204), channel_id=1, replica_groups=mesh['y'=4,'z'=16,'c'=2,'x'=4] {'c'}, dimensions={0} | all-to-all | bytes 524288 | tf_op jit(solution)/shard_map/all_to_all | solution.py:475
  103.0 13.7 %all-to-all-start.4 = ((f32[128,1,256]{2,1,0:T(1,128)}), f32[128,1,256]{2,1,0:T(1,128)S(1)}, u32[]{:S(2)}, u32[]{:S(2)}) async-start(f32[128,1,256]{2,1,0:T(1,128)} %copy.186), calls=%async_computation.4 | async-start | bytes 262144 | tf_op jit(solution)/shard_map/all_to_all | solution.py:470
  116.7 0.7 reduce_sum.99
  117.4 16.7 %all-to-all-done.4 = f32[128,1,256]{2,1,0:T(1,128)S(1)} async-done(((f32[128,1,256]{2,1,0:T(1,128)}), f32[128,1,256]{2,1,0:T(1,128)S(1)}, u32[]{:S(2)}, u32[]{:S(2)}) %all-to-all-start.4) | async-done | bytes 131104 | tf_op jit(solution)/shard_map/all_to_all | solution.py:470
  134.1 3.5 %all-to-all-start.8 = ((f32[16,16,128]{2,1,0:T(8,128)}), f32[16,16,128]{2,1,0:T(8,128)S(1)}, u32[]{:S(2)}, u32[]{:S(2)}) async-start(f32[16,16,128]{2,1,0:T(8,128)} %reduce_sum.99), calls=%async_computation.8 | async-start | bytes 262144 | tf_op jit(solution)/shard_map/all_to_all | solution.py:476
  137.6 0.0 copy-done.15
  137.7 0.1 copy.188.ridge_ref
  137.7 0.5 slice.40
  138.9 10.6 %all-to-all-done.8.back_ref = f32[16,16,128]{2,1,0:T(8,128)S(1)} async-done(((f32[16,16,128]{2,1,0:T(8,128)}), f32[16,16,128]{2,1,0:T(8,128)S(1)}, u32[]{:S(2)}, u32[]{:S(2)}) %all-to-all-start.8) | async-done | bytes 131104 | tf_op jit(solution)/shard_map/all_to_all | solution.py:476
  149.6 0.0 copy-done.4
  149.6 0.0 copy-done.5
  149.6 0.0 copy-done.6
  149.6 0.0 copy-done.7
  149.6 0.0 copy-done.8
  149.6 0.0 copy-done.9
  149.6 0.0 copy-done.10
  149.6 0.0 copy-done.11
  149.6 0.0 copy-done.12
  149.6 5.0 %shard_map.205 = (f32[4,4096]{1,0:T(4,128)}, f32[16,80]{1,0:T(8,128)S(1)}, f32[1,128]{1,0:T(1,128)S(1)}) custom-call(f32[128,256]{1,0:T(8,128)S(1)} %bitcast.82, f32[4,4096]{1,0:T(4,128)S(1)} %get-tuple-element.88.c_ref, s32[1,4096]{1,0:T(1,128)S(1)} %get-tuple-element.89.rank_ref, s32[1,4096]{1,0:T(1,128)S(1)} %bitcast.97, s32[1,4096]{1,0:T(1,128)S(1)} %bitcast.99, ...), custom_call_target="tpu_custom_call" | custom-call | tf_op jit(solution)/shard_map/pallas_call | solution.py:479
  154.7 0.0 copy-done.13
  154.7 15.9 %all_to_all.58 = f32[32,1,128]{2,1,0:T(1,128)S(1)} all-to-all(f32[32,1,128]{2,1,0:T(1,128)S(1)} %broadcast_in_dim.134), channel_id=1, replica_groups=mesh['y'=4,'z'=16,'c'=2,'x'=4] {'y','c','x'}, dimensions={0} | all-to-all | bytes 32768 | tf_op jit(solution)/shard_map/all_to_all | solution.py:506
  170.6 14.7 %all_to_all.59.sums_ref = f32[16,1,128]{2,1,0:T(1,128)S(1)} all-to-all(f32[16,1,128]{2,1,0:T(1,128)S(1)} %broadcast_in_dim.135), channel_id=1, replica_groups=mesh['y'=4,'z'=16,'c'=2,'x'=4] {'z'}, dimensions={0} | all-to-all | bytes 16384 | tf_op jit(solution)/shard_map/all_to_all | solution.py:510
  185.3 0.0 copy-done.2
  185.3 0.0 copy-done.3
  185.3 1.7 shard_map.206
  (12 shorter events, 0.1 us)
Async XLA Ops:
  0.6 54.4 %copy-start.14 = (f32[4]{0:T(128)S(1)}, f32[4]{0:T(128)}, u32[]{:S(2)}) copy-start(f32[4]{0:T(128)} %param.31) | copy-start | bytes 52
  0.6 69.5 %copy-start = (bf16[32,10240]{1,0:T(8,128)(2,1)S(1)}, bf16[32,10240]{1,0:T(8,128)(2,1)}, u32[]{:S(2)}) copy-start(bf16[32,10240]{1,0:T(8,128)(2,1)} %geno_ref.3) | copy-start | bytes 1966084
  0.7 69.5 %copy-start.1 = (f32[10240]{0:T(1024)S(1)}, f32[10240]{0:T(1024)}, u32[]{:S(2)}) copy-start(f32[10240]{0:T(1024)} %param.30) | copy-start | bytes 122884
  2.1 34.0 %all-to-all-start.5 = ((f32[16,16,128]{2,1,0:T(8,128)}), f32[16,16,128]{2,1,0:T(8,128)S(1)}, u32[]{:S(2)}, u32[]{:S(2)}) async-start(f32[16,16,128]{2,1,0:T(8,128)} %broadcast_in_dim.129), calls=%async_computation.5 | async-start | bytes 262144 | tf_op jit(solution)/shard_map/all_to_all | solution.py:427
  36.1 45.2 %all-to-all-start.3 = ((f32[128,1,384]{2,1,0:T(1,128)}), f32[128,1,384]{2,1,0:T(1,128)S(1)}, u32[]{:S(2)}, u32[]{:S(2)}) async-start(f32[128,1,384]{2,1,0:T(1,128)} %copy.185), calls=%async_computation.3 | async-start | bytes 393216 | tf_op jit(solution)/shard_map/all_to_all | solution.py:447
  81.4 56.3 %copy-start.15 = (f32[16]{0:T(128)S(1)}, f32[16]{0:T(128)}, u32[]{:S(2)}) copy-start(f32[16]{0:T(128)} %param.32) | copy-start | bytes 196
  81.4 11.2 %all-to-all-start.6 = ((f32[4,16,2560]{2,1,0:T(8,128)}), f32[4,16,2560]{2,1,0:T(8,128)S(1)}, u32[]{:S(2)}, u32[]{:S(2)}) async-start(f32[4,16,2560]{2,1,0:T(8,128)} %get-tuple-element.92), calls=%async_computation.6 | async-start | bytes 1310720 | tf_op jit(solution)/shard_map/all_to_all | solution.py:459
  85.0 64.6 %copy-start.4 = (f32[4,4096]{1,0:T(4,128)S(1)}, f32[4,4096]{1,0:T(4,128)}, u32[]{:S(2)}) copy-start(f32[4,4096]{1,0:T(4,128)} %dir_ref.3) | copy-start | bytes 196612
  85.0 64.5 %copy-start.5 = (f32[4,4096]{1,0:T(4,128)S(1)}, f32[4,4096]{1,0:T(4,128)}, u32[]{:S(2)}) copy-start(f32[4,4096]{1,0:T(4,128)} %res_ref.3) | copy-start | bytes 196612
  85.0 64.5 %copy-start.6 = (f32[4,4096]{1,0:T(4,128)S(1)}, f32[4,4096]{1,0:T(4,128)}, u32[]{:S(2)}) copy-start(f32[4,4096]{1,0:T(4,128)} %inv_ref.3) | copy-start | bytes 196612
  85.0 64.5 %copy-start.7 = (s32[4096]{0:T(1024)S(1)}, s32[4096]{0:T(1024)}, u32[]{:S(2)}) copy-start(s32[4096]{0:T(1024)} %param.34) | copy-start | bytes 49156
  85.0 64.5 %copy-start.8 = (s32[4096]{0:T(1024)S(1)}, s32[4096]{0:T(1024)}, u32[]{:S(2)}) copy-start(s32[4096]{0:T(1024)} %param.35) | copy-start | bytes 49156
  85.1 64.5 %copy-start.9 = (f32[4,4096]{1,0:T(4,128)S(1)}, f32[4,4096]{1,0:T(4,128)}, u32[]{:S(2)}) copy-start(f32[4,4096]{1,0:T(4,128)} %rec_ref.1) | copy-start | bytes 196612
  85.1 64.5 %copy-start.10 = (f32[16,1,80]{2,1,0:T(1,128)S(1)}, f32[16,1,80]{2,1,0:T(1,128)}, u32[]{:S(2)}) copy-start(f32[16,1,80]{2,1,0:T(1,128)} %param.27) | copy-start | bytes 15364
  85.1 64.5 %copy-start.11 = (f32[16,1,80]{2,1,0:T(1,128)S(1)}, f32[16,1,80]{2,1,0:T(1,128)}, u32[]{:S(2)}) copy-start(f32[16,1,80]{2,1,0:T(1,128)} %param.26) | copy-start | bytes 15364
  85.1 64.5 %copy-start.12 = (f32[16,1,80]{2,1,0:T(1,128)S(1)}, f32[16,1,80]{2,1,0:T(1,128)}, u32[]{:S(2)}) copy-start(f32[16,1,80]{2,1,0:T(1,128)} %param.28) | copy-start | bytes 15364
  85.1 69.6 %copy-start.13 = (f32[4,16]{1,0:T(4,128)S(1)}, f32[4,16]{1,0:T(4,128)}, u32[]{:S(2)}) copy-start(f32[4,16]{1,0:T(4,128)} %g_ref.1) | copy-start | bytes 772
  103.0 31.1 %all-to-all-start.4 = ((f32[128,1,256]{2,1,0:T(1,128)}), f32[128,1,256]{2,1,0:T(1,128)S(1)}, u32[]{:S(2)}, u32[]{:S(2)}) async-start(f32[128,1,256]{2,1,0:T(1,128)} %copy.186), calls=%async_computation.4 | async-start | bytes 262144 | tf_op jit(solution)/shard_map/all_to_all | solution.py:470
  134.1 15.4 %all-to-all-start.8 = ((f32[16,16,128]{2,1,0:T(8,128)}), f32[16,16,128]{2,1,0:T(8,128)S(1)}, u32[]{:S(2)}, u32[]{:S(2)}) async-start(f32[16,16,128]{2,1,0:T(8,128)} %reduce_sum.99), calls=%async_computation.8 | async-start | bytes 262144 | tf_op jit(solution)/shard_map/all_to_all | solution.py:476
  154.7 30.6 %copy-start.2 = (f32[4,4096]{1,0:T(4,128)S(1)}, f32[4,4096]{1,0:T(4,128)}, u32[]{:S(2)}) copy-start(f32[4,4096]{1,0:T(4,128)} %sol_ref.1) | copy-start | bytes 196612
  154.7 30.6 %copy-start.3 = (f32[16,1,80]{2,1,0:T(1,128)S(1)}, f32[16,1,80]{2,1,0:T(1,128)}, u32[]{:S(2)}) copy-start(f32[16,1,80]{2,1,0:T(1,128)} %param.25) | copy-start | bytes 15364

commit v2 on v1

v2 whole, which is shorter than its diff:
```python
import functools
import math

import jax
import jax.numpy as jnp
from jax import lax
from jax.experimental import pallas as pl
from jax.experimental.pallas import tpu as pltpu
from jax.sharding import Mesh, PartitionSpec as P

SLOTS = 2
CAP = 64
LIST = CAP - 1
CHUNK = 512
HERD = ("y", "z", "c")
F32 = jnp.float32
BF16 = jnp.bfloat16
NT = (((1,), (1,)), ((), ()))
TN = (((0,), (0,)), ((), ()))
NN = (((1,), (0,)), ((), ()))


def call(kernel, out, scratch=(), **kw):
    return pl.pallas_call(
        kernel,
        out_shape=out,
        scratch_shapes=list(scratch),
        compiler_params=pltpu.CompilerParams(vmem_limit_bytes=40 * 2**20),
        **kw,
    )


def dot(a, b, dims=NN):
    return lax.dot_general(a, b, dims, preferred_element_type=F32)


def parts(x, n=2):
    out = []
    for _ in range(n):
        p = x.astype(BF16).astype(F32)
        out.append(p)
        x = x - p
    return out


def rows_at(n, cols):
    return lax.broadcasted_iota(jnp.int32, (n, cols), 0)


def weights(sire, dam):
    known = (sire >= 0).astype(jnp.int32) + (dam >= 0).astype(jnp.int32)
    return jnp.where(known == 2, 2.0, jnp.where(known == 1, 4.0 / 3.0, 1.0)).astype(F32)


def dam_place(dam, animals):
    local = dam & (animals - 1)
    block = jnp.where(dam >= 0, local >> 7, -1)
    return block, local & 127


def one_hot(index, rows):
    return (rows_at(rows, index.shape[1]) == index).astype(F32).astype(BF16)


def pick(found, in_group, t):
    rows = in_group.shape[0]
    return jnp.sum(jnp.where(in_group, found[t * rows : (t + 1) * rows], 0.0), axis=0, keepdims=True)


def table_of(ref):
    return jnp.concatenate([p.astype(BF16) for p in parts(ref[...])], axis=0)


def masked(in_group, fields):
    return jnp.concatenate([jnp.where(in_group, f, 0.0).astype(BF16) for f in fields], axis=0)


def moved(width, pieces, load, rows):
    lane = lax.broadcasted_iota(jnp.int32, (rows, 128), 1)
    for k in range(width // 128):
        tile = jnp.zeros((rows, 128), F32)
        for source, first, at, length in pieces:
            lo, hi = max(at, k * 128), min(at + length, (k + 1) * 128)
            while lo < hi:
                src = first + lo - at
                end = min(hi, lo + 128 - src % 128)
                turn = (lo - src) % 128
                value = load(source, src // 128)
                if turn:
                    value = pltpu.roll(value, turn, 1)
                a, b = lo - k * 128, end - k * 128
                tile = value if (a, b) == (0, 128) else jnp.where((lane >= a) & (lane < b), value, tile)
                lo = end
        yield k, tile


def lists_kernel(dir_ref, dir_a_ref, sire_ref, dam_ref, out_ref, rank_ref, tab_ref, acc_ref, *, shape):
    ny, nz, nc = shape
    traits, animals = dir_ref.shape
    herd = ny * nz * nc
    blocks = animals // 128
    n = CHUNK
    for t in range(traits):
        for b in range(blocks):
            tab_ref[t * blocks + b : t * blocks + b + 1, :] = dir_ref[t : t + 1, b * 128 : (b + 1) * 128]
    table = table_of(tab_ref)
    half = traits * blocks
    before = (rows_at(n, n) < lax.broadcasted_iota(jnp.int32, (n, n), 1)).astype(F32).astype(BF16)
    acc_ref[...] = jnp.zeros(acc_ref.shape, F32)

    def step(k, carry):
        at = pl.ds(pl.multiple_of(k * n, n), n)
        sire = sire_ref[:, at]
        dam = dam_ref[:, at]
        weight = weights(sire, dam)
        block, offset = dam_place(dam, animals)
        found = dot(table, one_hot(offset, 128))
        found = found[:half] + found[half:]
        in_block = rows_at(blocks, n) == block
        own = dir_ref[:, at]
        is_owner = rows_at(herd, n) == owner_row(sire, animals, shape)
        owners = is_owner.astype(F32).astype(BF16)
        earlier = dot(owners, before) + carry
        rank = jnp.sum(jnp.where(is_owner, earlier, 0.0), axis=0, keepdims=True).astype(jnp.int32)
        rank = jnp.where((sire >= 0) & (rank < LIST), rank, -1)
        rank_ref[:, at] = rank
        local = (sire & (animals - 1)) + 1
        high = [(local & ~63).astype(F32), weight * 1.5]
        low = [(local & 63).astype(F32), jnp.zeros((1, n), F32)]
        for t in range(traits):
            hi, lo = parts(weight * (own[t : t + 1] - 0.5 * pick(found, in_block, t)))
            high.append(hi)
            low.append(lo)
        acc_ref[...] += dot(masked(rows_at(CAP, n) == rank, high + low), owners, NT)
        return carry + jnp.sum(jnp.where(is_owner, 1.0, 0.0), axis=1, keepdims=True)

    count = lax.fori_loop(0, animals // n, step, jnp.zeros((herd, 1), F32))
    width = (2 + traits) * CAP
    overflow = jnp.where(jnp.max(count, axis=0, keepdims=True) > LIST + 0.5, 1.0, 0.0)
    lane = lax.broadcasted_iota(jnp.int32, (herd, 128), 1)
    for j in range(width // 128):
        at = slice(j * 128, (j + 1) * 128)
        block = (acc_ref[at, :] + acc_ref[width + j * 128 : width + (j + 1) * 128, :]).T
        if j == 0:
            block = jnp.where(lane == 127, overflow, block)
        out_ref[:, :, at] = block.reshape(nz, ny * nc, 128)
    rows = ny * nc
    columns = dir_a_ref.shape[1]
    for j in range(dir_a_ref.shape[0] // rows):
        piece = dir_a_ref[j * rows : (j + 1) * rows, :]
        for z in range(nz):
            out_ref[z, :, width + j * 128 : width + j * 128 + columns] = piece


def owner_row(sire, animals, shape):
    ny, nz, nc = shape
    owner = sire >> (animals.bit_length() - 1)
    low = nc.bit_length() - 1
    c = owner & (nc - 1)
    z = (owner >> low) & (nz - 1)
    y = owner >> (low + nz.bit_length() - 1)
    return jnp.where(sire >= 0, z * (ny * nc) + y * nc + c, -1)


def forward_kernel(in_ref, out_ref, *, columns, lists):
    nz, near, _ = in_ref.shape
    traits = out_ref.shape[1]
    for g in range(near):
        out_ref[g, :nz, :lists] = in_ref[:, g, :lists]
    pieces = [(z, 0, z * columns, columns) for z in range(nz)]
    for j in range(traits // near):
        first = lists + j * 128
        load = lambda z, _: in_ref[z, :, first : first + 128]
        for k, tile in moved(nz * columns, pieces, load, near):
            for g in range(near):
                out_ref[g, j * near : (j + 1) * near, lists + k * 128 : lists + (k + 1) * 128] = tile


def gather_kernel(
    in_ref, tab_ref, geno_ref, freq_ref, gw_ref, out_ref, turned_ref, weight_ref, over_ref,
    joined_ref, acc_ref, *, shape, columns, lists, scale,
):
    ny, nz, nc = shape
    herd = ny * nz * nc
    traits = in_ref.shape[1]
    half = tab_ref.shape[0]
    blocks = weight_ref.shape[0]
    here = half // blocks
    genotyped = geno_ref.shape[0]
    for j in range(lists // 128):
        at = slice(j * 128, (j + 1) * 128)
        turned_ref[at, :] = in_ref[:, :nz, at].reshape(herd, 128).T
    over_ref[...] = jnp.broadcast_to(jnp.max(turned_ref[127:128, :], keepdims=True), over_ref.shape)
    acc_ref[...] = jnp.zeros(acc_ref.shape, F32)
    group = 8

    def step(k, _):
        r = pl.multiple_of(k * group, group)
        place = flat(turned_ref, r, group).astype(jnp.int32) - 1
        in_block = rows_at(blocks, group * herd) == (place >> 7)
        high, low = [], []
        for t in range(here):
            hi, lo = parts(flat(turned_ref, (2 + t) * CAP + r, group))
            high.append(hi)
            low.append(lo)
        fields = masked(in_block, high + low + [flat(turned_ref, CAP + r, group)])
        acc_ref[...] += dot(fields, one_hot(place & 127, 128), NT)
        return 0

    lax.fori_loop(0, CAP // group, step, 0)
    weight_ref[...] = acc_ref[2 * half :, :] * (0.25 / 1.5)
    out_ref[traits : traits + half, :] = acc_ref[:half, :] + acc_ref[half : 2 * half, :]
    out_ref[traits + half :, :] = tab_ref[...]

    width = nz * nc * columns
    total = jnp.zeros((3 * traits, genotyped), F32)
    bias = jnp.zeros((traits, 1), F32)
    for y in range(ny):
        pieces = [
            (y * nc + c, z * columns, (z * nc + c) * columns, columns) for z in range(nz) for c in range(nc)
        ]
        load = lambda g, k: in_ref[g, :, lists + k * 128 : lists + (k + 1) * 128]
        for k, tile in moved(width, pieces, load, traits):
            joined_ref[:, k * 128 : (k + 1) * 128] = tile
        at = slice(y * width, (y + 1) * width)
        values = joined_ref[...]
        stack = jnp.concatenate([p.astype(BF16) for p in parts(values, 3)], axis=0)
        total = total + dot(stack, geno_ref[:, at], NT)
        bias = bias + jnp.sum(values * (2.0 * freq_ref[:, at]), axis=1, keepdims=True)
    rows = total[:traits] + total[traits : 2 * traits] + total[2 * traits :]
    out_ref[:traits, :] = jnp.zeros((traits, 128), F32)
    out_ref[:traits, :genotyped] = (rows - bias) * scale
    out_ref[:traits, genotyped : genotyped + 1] = gw_ref[...]


def flat(ref, first, group):
    tile = ref[pl.ds(first, group), :]
    return jnp.concatenate([tile[j : j + 1] for j in range(group)], axis=1)


def reply_kernel(
    mix_ref, all_ref, ids_ref, weight_ref, geno_ref, freq_ref,
    out_ref, tab_ref, inc_ref, resid_ref, vals_ref, rows_ref, summed_ref, *, shape, columns, scale,
):
    ny, nz, nc = shape
    herd = ny * nz * nc
    nx = all_ref.shape[0]
    traits = resid_ref.shape[0]
    half = tab_ref.shape[0]
    blocks = weight_ref.shape[0]
    here = half // blocks
    genotyped = geno_ref.shape[0]
    for t in range(here):
        value = jnp.zeros((blocks, 128), F32)
        added = jnp.zeros((blocks, 128), F32)
        for x in range(nx):
            for s in range(here):
                factor = mix_ref[t, x * here + s]
                at = traits + s * blocks
                added = added + factor * all_ref[x, at : at + blocks, :]
                value = value + factor * all_ref[x, half + at : half + at + blocks, :]
        at = slice(t * blocks, (t + 1) * blocks)
        tab_ref[at, :] = value
        inc_ref[at, :] = weight_ref[...] * value - 0.5 * added

    table = table_of(tab_ref)
    group = 8

    def step(k, _):
        r = pl.multiple_of(k * group, group)
        place = flat(ids_ref, r, group).astype(jnp.int32) - 1
        in_block = rows_at(blocks, group * herd) == (place >> 7)
        found = dot(table, one_hot(place & 127, 128))
        found = found[:half] + found[half:]
        for t in range(here):
            value = pick(found, in_block, t)
            vals_ref[pl.ds(t * CAP + r, group), :] = jnp.concatenate(
                [value[:, j * herd : (j + 1) * herd] for j in range(group)], axis=0
            )
        return 0

    lax.fori_loop(0, CAP // group, step, 0)
    values = here * CAP
    for j in range(values // 128):
        at = slice(j * 128, (j + 1) * 128)
        out_ref[:, :nz, at] = vals_ref[at, :].T.reshape(ny * nc, nz, 128)

    for x in range(nx):
        for s in range(here):
            at = traits + half + s * blocks
            rows_ref[x * here + s : x * here + s + 1, :] = all_ref[x, at : at + 1, :]
    total = all_ref[0, :traits, :]
    for x in range(1, nx):
        total = total + all_ref[x, :traits, :]
    lane = lax.broadcasted_iota(jnp.int32, (traits, 128), 1)
    weight = jnp.sum(jnp.where(lane == genotyped, total, 0.0), axis=1, keepdims=True)
    resid = jnp.where(lane < genotyped, weight * (rows_ref[...] - total), 0.0)
    resid_ref[...] = resid
    stack = jnp.concatenate([p.astype(BF16) for p in parts(resid, 3)], axis=0)[:, :genotyped]
    summed = jnp.sum(resid, axis=1, keepdims=True)
    width = nz * nc * columns
    for y in range(ny):
        at = slice(y * width, (y + 1) * width)
        found = dot(stack, geno_ref[:, at])
        found = found[:traits] + found[traits : 2 * traits] + found[2 * traits :]
        summed_ref[...] = (found - summed * (2.0 * freq_ref[:, at])) * scale
        for c in range(nc):
            pieces = [(0, (z * nc + c) * columns, z * columns, columns) for z in range(nz)]
            load = lambda _, k: summed_ref[:, k * 128 : (k + 1) * 128]
            for k, tile in moved(nz * columns, pieces, load, traits):
                out_ref[y * nc + c, :, values + k * 128 : values + (k + 1) * 128] = tile


def backward_kernel(in_ref, out_ref, *, columns, values):
    nz, near, _ = out_ref.shape
    traits = in_ref.shape[1]
    for g in range(near):
        out_ref[:, g, :values] = in_ref[g, :nz, :values]
    total = in_ref[0, :, values:]
    for g in range(1, near):
        total = total + in_ref[g, :, values:]
    load = lambda _, k: total[:, k * 128 : (k + 1) * 128]
    for z in range(nz):
        for _, tile in moved(128, [(0, z * columns, 0, columns)], load, traits):
            for j in range(traits // near):
                first = values + j * 128
                out_ref[z, :, first : first + 128] = tile[j * near : (j + 1) * near]


def dams_kernel(tab_ref, sire_ref, dam_ref, out_ref):
    traits, animals = out_ref.shape
    blocks = animals // 128
    half = traits * blocks
    n = CHUNK
    for t in range(traits):
        for b in range(blocks):
            out_ref[t : t + 1, b * 128 : (b + 1) * 128] = tab_ref[t * blocks + b : t * blocks + b + 1, :]
    table = table_of(tab_ref)

    def step(k, _):
        at = pl.ds(pl.multiple_of(k * n, n), n)
        dam = dam_ref[:, at]
        weight = weights(sire_ref[:, at], dam)
        block, offset = dam_place(dam, animals)
        found = dot(table, one_hot(offset, 128))
        found = found[:half] + found[half:]
        in_block = rows_at(blocks, n) == block
        for t in range(traits):
            out_ref[t : t + 1, at] = weight * (out_ref[t : t + 1, at] - 0.5 * pick(found, in_block, t))
        return 0

    lax.fori_loop(0, animals // n, step, 0)


def image_kernel(
    got_ref, c_ref, rank_ref, sire_ref, dam_ref, inc_ref, resid_ref,
    dir_ref, rec_ref, res_ref, inv_ref, ridge_ref, dir_a_ref, res_a_ref, inv_a_ref,
    image_ref, image_a_ref, sums_ref, acc_ref, tab_ref, *, shape,
):
    traits, animals = c_ref.shape
    ny, nz, nc = shape
    herd, near = ny * nz * nc, ny * nc
    blocks = animals // 128
    n = CHUNK
    half = traits * blocks
    wide = traits * CAP
    table = jnp.concatenate(
        [p.astype(BF16) for p in parts(got_ref[:, :, :wide].reshape(herd, wide))], axis=1
    )
    acc_ref[...] = jnp.zeros(acc_ref.shape, F32)

    def step(k, _):
        at = pl.ds(pl.multiple_of(k * n, n), n)
        sire = sire_ref[:, at]
        dam = dam_ref[:, at]
        weight = weights(sire, dam)
        found = dot(table, one_hot(owner_row(sire, animals, shape), herd), TN)
        found = found[:wide] + found[wide:]
        in_slot = rows_at(CAP, n) == rank_ref[:, at]
        block, offset = dam_place(dam, animals)
        high, low = [], []
        for t in range(traits):
            scaled = c_ref[t : t + 1, at] - 0.5 * weight * pick(found, in_slot, t)
            image_ref[t : t + 1, at] = scaled
            hi, lo = parts(scaled)
            high.append(hi)
            low.append(lo)
        acc_ref[...] += dot(masked(rows_at(blocks, n) == block, high + low), one_hot(offset, 128), NT)
        return 0

    lax.fori_loop(0, animals // n, step, 0)
    tab_ref[...] = inc_ref[...] - 0.5 * (acc_ref[:half, :] + acc_ref[half:, :])
    for b in range(blocks):
        for t in range(traits):
            at = (slice(t, t + 1), slice(b * 128, (b + 1) * 128))
            image_ref[at] = image_ref[at] + tab_ref[t * blocks + b : t * blocks + b + 1, :]
    image_ref[:, :128] = image_ref[:, :128] + resid_ref[...]
    direction = dir_ref[...]
    image = image_ref[...] + rec_ref[...] * direction
    image_ref[...] = image
    res = res_ref[...]
    inv = inv_ref[...]
    columns = dir_a_ref.shape[1]
    sums = jnp.sum(got_ref[:, :, wide:], axis=0)
    tiles = sums.shape[1] // 128
    back = jnp.concatenate([sums[:, j * 128 : (j + 1) * 128] for j in range(tiles)], axis=0)[:, :columns]
    dir_a = dir_a_ref[...]
    image_a = ridge_ref[...] * dir_a - back
    image_a_ref[...] = image_a
    res_a = res_a_ref[...]
    inv_a = inv_a_ref[...]
    weighted, weighted_a = inv * res, inv_a * res_a
    lane = lax.broadcasted_iota(jnp.int32, (1, 128), 1)
    pairs = (
        (weighted * res, weighted_a * res_a),
        (direction * image, dir_a * image_a),
        (weighted * image, weighted_a * image_a),
        (inv * image * image, inv_a * image_a * image_a),
    )
    total = jnp.zeros((1, 128), F32)
    for j, (one, two) in enumerate(pairs):
        value = jnp.sum(one, keepdims=True) + jnp.sum(two, keepdims=True)
        total = jnp.where(lane == j, value, total)
    sums_ref[...] = total


def update_kernel(
    sums_ref, sol_ref, res_ref, dir_ref, inv_ref, image_ref,
    sol_a_ref, res_a_ref, dir_a_ref, inv_a_ref, image_a_ref,
    nsol_ref, nres_ref, ndir_ref, nsol_a_ref, nres_a_ref, ndir_a_ref,
):
    total = jnp.sum(sums_ref[...], axis=0)
    norm, curve, cross, square = (total[:, j : j + 1] for j in range(4))
    size = norm / curve
    following = norm - 2.0 * size * cross + size * size * square
    ratio = following / norm
    for sol, res, dire, inv, image, nsol, nres, ndir in (
        (sol_ref, res_ref, dir_ref, inv_ref, image_ref, nsol_ref, nres_ref, ndir_ref),
        (sol_a_ref, res_a_ref, dir_a_ref, inv_a_ref, image_a_ref, nsol_a_ref, nres_a_ref, ndir_a_ref),
    ):
        d = dire[...]
        nsol[...] = sol[...] + size * d
        left = res[...] - size * image[...]
        nres[...] = left
        ndir[...] = inv[...] * left + ratio * d


def pedigree_by_blocks(field, sire, dam, herd_count, herd_index):
    traits_here, animals = field.shape
    block_count = animals // 128
    span = SLOTS * 128
    has_sire = sire >= 0
    has_dam = dam >= 0
    sire_known = has_sire.astype(F32)
    dam_known = has_dam.astype(F32)
    owner_herd = jnp.where(has_sire, sire // animals, 0)
    block_index = jnp.where(has_sire, sire % animals // 128, 0)
    offset = jnp.where(has_sire, sire % 128, 0)
    flat_block = jnp.where(
        has_sire, owner_herd * block_count + block_index, herd_count * block_count
    )
    present = jnp.zeros((herd_count * block_count + 1,), jnp.int32).at[flat_block].max(1)
    present = present[:-1].reshape(herd_count, block_count)
    slot_order = jnp.cumsum(present, axis=1) - 1
    slot_range = jnp.arange(SLOTS, dtype=jnp.int32)
    slot_match = (present[:, :, None] == 1) & (slot_order[:, :, None] == slot_range[None, None, :])
    block_ids = jnp.arange(block_count, dtype=jnp.int32)[None, :, None] + 1
    wanted = jnp.sum(jnp.where(slot_match, block_ids, 0), axis=1) - 1
    requests = lax.all_to_all(wanted, HERD, split_axis=0, concat_axis=0, tiled=True)
    live_slot = requests >= 0
    field_tiles = field.reshape(traits_here, block_count, 128)
    outgoing = field_tiles[:, jnp.where(live_slot, requests, 0), :]
    outgoing = jnp.where(live_slot[None, :, :, None], outgoing, 0.0).reshape(
        traits_here, herd_count, span
    )
    fetched = lax.all_to_all(outgoing, HERD, split_axis=1, concat_axis=1, tiled=True).reshape(
        traits_here, herd_count * span
    )
    slot_index = slot_order[owner_herd, block_index]
    buffer_place = owner_herd * span + slot_index * 128 + offset
    sire_values = fetched[:, jnp.where(has_sire, buffer_place, 0)]
    local_dam = jnp.where(has_dam, dam - herd_index * animals, 0)
    dam_values = field[:, local_dam]
    weight = 4.0 / (4.0 - sire_known - dam_known)
    scaled = weight * (field - 0.5 * sire_known * sire_values - 0.5 * dam_known * dam_values)
    dam_target = jnp.where(has_dam, local_dam, animals)
    dam_terms = (
        jnp.zeros((traits_here, animals + 1), F32).at[:, dam_target].add(-0.5 * dam_known * scaled)
    )
    result = scaled + dam_terms[:, :animals]
    sire_target = jnp.where(has_sire, buffer_place, herd_count * span)
    outbound = (
        jnp.zeros((traits_here, herd_count * span + 1), F32)
        .at[:, sire_target]
        .add(-0.5 * sire_known * scaled)
    )
    outbound = outbound[:, :-1].reshape(traits_here, herd_count, span)
    returned = lax.all_to_all(outbound, HERD, split_axis=1, concat_axis=1, tiled=True).reshape(
        traits_here, herd_count * SLOTS, 128
    )
    block_target = jnp.where(live_slot, requests, block_count).reshape(herd_count * SLOTS)
    incoming = (
        jnp.zeros((traits_here, block_count + 1, 128), F32).at[:, block_target, :].add(returned)
    )
    return result + incoming[:, :block_count, :].reshape(traits_here, animals)


def body(
    sol_u, res_u, dir_u, rec_weight, inv_diag_u, sol_a, res_a, dir_a, inv_diag_a,
    genotypes, allele_freq, geno_weight, snp_ridge, genetic_inv, sire, dam,
):
    shape = ny, nz, nc = tuple(lax.axis_size(a) for a in HERD)
    nx = lax.axis_size("x")
    herd, near = ny * nz * nc, ny * nc
    herd_index = lax.axis_index(HERD)
    x_index = lax.axis_index("x")
    here, animals = dir_u.shape
    traits, _, columns = dir_a.shape
    genotyped, snps = genotypes.shape
    blocks = animals // 128
    half = here * blocks
    lists, values = (2 + here) * CAP, here * CAP
    spare = traits // near * 128
    scale = 2.0 / math.sqrt(snps * nx)
    sds = lambda *s: jax.ShapeDtypeStruct(s, F32)
    vmem = lambda *s: pltpu.VMEM(s, F32)
    d_a, r_a, s_a, i_a = (a[:, 0, :] for a in (dir_a, res_a, sol_a, inv_diag_a))
    freq = allele_freq[None, :]
    sire_row, dam_row = sire[None, :], dam[None, :]
    weight_here = lax.dynamic_update_slice(
        jnp.zeros((traits, 1), F32), geno_weight[:, None], (x_index * here, 0)
    )

    out_z, rank, table = call(
        functools.partial(lists_kernel, shape=shape),
        (sds(nz, near, lists + spare), jax.ShapeDtypeStruct((1, animals), jnp.int32), sds(half, 128)),
        scratch=[vmem(2 * lists, herd)],
    )(dir_u, d_a, sire_row, dam_row)
    in_z = lax.all_to_all(out_z, "z", 0, 0, tiled=True)
    out_near = call(
        functools.partial(forward_kernel, columns=columns, lists=lists),
        sds(near, traits, lists + nz * columns),
    )(in_z)
    in_near = lax.all_to_all(out_near, ("y", "c"), 0, 0, tiled=True)

    to_x, turned, weight_sum, over = call(
        functools.partial(gather_kernel, shape=shape, columns=columns, lists=lists, scale=scale),
        (sds(traits + 2 * half, 128), sds(lists, herd), sds(blocks, 128), sds(8, 128)),
        scratch=[vmem(traits, nz * nc * columns), vmem(2 * half + blocks, 128)],
    )(in_near, table, genotypes, freq, weight_here)
    from_x = lax.all_gather(to_x, "x", axis=0)

    on_chip = pl.BlockSpec(memory_space=pltpu.VMEM)
    back_near, mixed_table, incoming, resid = call(
        functools.partial(reply_kernel, shape=shape, columns=columns, scale=scale),
        (sds(near, traits, values + nz * columns), sds(half, 128), sds(half, 128), sds(traits, 128)),
        scratch=[vmem(values, herd), vmem(traits, 128), vmem(traits, nz * nc * columns)],
        in_specs=[pl.BlockSpec(memory_space=pltpu.SMEM)] + [on_chip] * 5,
    )(genetic_inv, from_x, turned, weight_sum, genotypes, freq)
    got_near = lax.all_to_all(back_near, ("y", "c"), 0, 0, tiled=True)
    back_z = call(
        functools.partial(backward_kernel, columns=columns, values=values), sds(nz, near, values + spare)
    )(got_near)
    got_z = lax.all_to_all(back_z, "z", 0, 0, tiled=True)

    c_term = call(dams_kernel, sds(here, animals))(mixed_table, sire_row, dam_row)
    own_resid = lax.dynamic_slice_in_dim(resid, x_index * here, here, 0)
    image_u, image_a, sums = call(
        functools.partial(image_kernel, shape=shape),
        (sds(here, animals), sds(traits, columns), sds(1, 128)),
        scratch=[vmem(2 * half, 128), vmem(half, 128)],
    )(
        got_z, c_term, rank, sire_row, dam_row, incoming, own_resid,
        dir_u, rec_weight, res_u, inv_diag_u, snp_ridge[:, None], d_a, r_a, i_a,
    )

    def by_blocks():
        dir_all = from_x[:, traits + half :, :].reshape(traits, animals)
        mixed = jnp.dot(genetic_inv, dir_all, precision=lax.Precision.HIGHEST)
        image = rec_weight * dir_u + pedigree_by_blocks(mixed, sire, dam, herd, herd_index)
        image = image.at[:, :genotyped].add(own_resid[:, :genotyped])
        cells = [
            jnp.sum(inv_diag_u * res_u * res_u) + jnp.sum(i_a * r_a * r_a),
            jnp.sum(dir_u * image) + jnp.sum(d_a * image_a),
            jnp.sum(inv_diag_u * res_u * image) + jnp.sum(i_a * r_a * image_a),
            jnp.sum(inv_diag_u * image * image) + jnp.sum(i_a * image_a * image_a),
        ]
        return image, jnp.pad(jnp.stack(cells), (0, 124))[None, :]

    image_u, sums = lax.cond(over[0, 0] > 0.5, by_blocks, lambda: (image_u, sums))

    close = lax.all_to_all(
        jnp.broadcast_to(sums[None], (near * nx, 1, 128)), ("y", "c", "x"), 0, 0, tiled=True
    )
    close = jnp.sum(close, axis=0, keepdims=True)
    far = lax.all_to_all(jnp.broadcast_to(close, (nz, 1, 128)), "z", 0, 0, tiled=True)

    u, a = sds(here, animals), sds(traits, columns)
    outs = call(update_kernel, (u, u, u, a, a, a))(
        far, sol_u, res_u, dir_u, inv_diag_u, image_u, s_a, r_a, d_a, i_a, image_a
    )
    return tuple(outs[:3]) + tuple(o[:, None, :] for o in outs[3:])


def solution(mesh):
    herd, nx = mesh.devices.shape
    ny, nc = 4, 2
    grid = Mesh(mesh.devices.reshape(ny, herd // (ny * nc), nc, nx), HERD + ("x",))
    u = P("x", HERD)
    a = P(None, "x", HERD)
    return jax.shard_map(
        body,
        mesh=grid,
        in_specs=(
            u, u, u, u, u, a, a, a, a,
            P(HERD, "x"), P("x"), P("x"), P(), P("x", None), P(HERD), P(HERD),
        ),
        out_specs=(u, u, u, a, a, a),
        check_vma=False,
    )
```

time: 188 us -> 162 us (0.86)
  starting transfers between devices: 55.4 us -> 16.9 us
  blocking collectives: 75.8 us -> 94.5 us
  waiting for transfers between devices: 29.9 us -> 22.6 us
  Pallas kernels: 19.6 us -> 24.7 us
  local copies, waits for them, and re-layouts: 3.99 us -> 0.81 us
    all_to_all x3 -> x4, blocking collectives: 40.8 us -> 82.7 us  [the longest x1 30.8 us: body(): in_z = lax.all_to_all(out_z, 'z', 0, 0, tiled=True)]
    all_to_all x5 -> x2, starting transfers between devices: 55.4 us -> 16.9 us  [the longest x1 11.1 us: body(): in_near = lax.all_to_all(out_near, ('y', 'c'), 0, 0, tiled=True)]
    all_gather x4 -> x1, blocking collectives: 35 us -> 11.8 us  [body(): from_x = lax.all_gather(to_x, 'x', axis=0)]
    all_to_all x5 -> x2, waiting for transfers between devices: 29.9 us -> 22.6 us  [the longest x1 12.9 us: body(): in_near = lax.all_to_all(out_near, ('y', 'c'), 0, 0, tiled=True)]
    pallas_call x7, Pallas kernels: 17.9 us -> 23 us  [the longest x1 6.44 us: body(): call(functools.partial(lists_kernel, shape=shape), (sds(nz, near, lists +...]
    broadcast_in_dim x5 -> x2, local copies, waits for them, and re-layouts: 2.31 us -> 0.02 us  [the longest x1 0.01 us: body(): jnp.broadcast_to(sums[None], (near * nx, 1, 128))]
  transfers between devices with their start and end apart: 5 -> 2, of which waited for: 3 -> 2; matrix products, arithmetic and copies ran while one was open for 2% -> 0% of each run, Pallas kernels for 7% -> 1%
where the time goes in v2:
time: 162 us; the launch traced here: 161 us
  blocking collectives  94.5 us (58%)
  Pallas kernels  24.7 us (15%)
  waiting for transfers between devices  22.6 us (14%)
  starting transfers between devices  16.9 us (10%)
    all_to_all x1, blocking collectives, body(): in_z = lax.all_to_all(out_z, 'z', 0, 0, tiled=True)  30.8 us
    all_to_all x1, blocking collectives, body(): lax.all_to_all(jnp.broadcast_to(sums[None], (near * nx, 1, 128)), ('y', '...  18.4 us
    all_to_all x1, blocking collectives, body(): got_near = lax.all_to_all(back_near, ('y', 'c'), 0, 0, tiled=True)  17 us
    all_to_all x1, blocking collectives, body(): lax.all_to_all(jnp.broadcast_to(close, (nz, 1, 128)), 'z', 0, 0, tiled=True)  16.5 us
    all_to_all x1, waiting for transfers between devices, body(): in_near = lax.all_to_all(out_near, ('y', 'c'), 0, 0, tiled=True)  12.9 us
    all_gather x1, blocking collectives, body(): from_x = lax.all_gather(to_x, 'x', axis=0)  11.8 us
    all_to_all x1, starting transfers between devices, body(): in_near = lax.all_to_all(out_near, ('y', 'c'), 0, 0, tiled=True)  11.1 us
    all_to_all x1, waiting for transfers between devices, body(): got_z = lax.all_to_all(back_z, 'z', 0, 0, tiled=True)  9.7 us
  transfers between devices with their start and end apart: 2, of which 2 were waited for; matrix products, arithmetic and copies ran while one was open for 0% of the time, Pallas kernels for 1%

profile of v2, /device:TPU:1, one launch (start us, length us, event | category | flops | bytes accessed | tf_op | source)
XLA Modules:
  0.0 161.0 jit_solution(7333698730368626594)
XLA Ops:
  0.6 0.0 copy-start.14
  0.6 0.0 copy-start
  0.7 0.0 copy-start.1
  0.7 6.4 %shard_map.199 = (f32[16,8,640]{2,1,0:T(8,128)S(1)}, s32[1,4096]{1,0:T(1,128)S(1)}, f32[128,128]{1,0:T(8,128)S(1)}) custom-call(f32[4,4096]{1,0:T(4,128)} %dir_ref.5, f32[16,80]{1,0:T(8,128)} %bitcast.85, s32[1,4096]{1,0:T(1,128)} %bitcast.79, s32[1,4096]{1,0:T(1,128)} %bitcast.82), custom_call_target="tpu_custom_call" | custom-call | tf_op jit(solution)/shard_map/pallas_call | solution.py:534
  7.1 30.8 %all_to_all.47.in_ref = f32[16,8,640]{2,1,0:T(8,128)S(1)} all-to-all(f32[16,8,640]{2,1,0:T(8,128)S(1)} %get-tuple-element.98), channel_id=1, replica_groups=mesh['y'=4,'z'=16,'c'=2,'x'=4] {'z'}, dimensions={0} | all-to-all | bytes 655360 | tf_op jit(solution)/shard_map/all_to_all | solution.py:539
  37.9 1.0 shard_map.200
  39.0 0.0 copy-start.13
  39.0 11.1 %all-to-all-start.4 = ((f32[8,16,1664]{2,1,0:T(8,128)}), f32[8,16,1664]{2,1,0:T(8,128)S(1)}, u32[]{:S(2)}, u32[]{:S(2)}) async-start(f32[8,16,1664]{2,1,0:T(8,128)} %shard_map.200), calls=%async_computation.4 | async-start | bytes 1703936 | tf_op jit(solution)/shard_map/all_to_all | solution.py:544
  50.0 0.0 copy-done.14
  50.0 0.1 copy.177
  50.1 12.9 %all-to-all-done.4.in_ref = f32[8,16,1664]{2,1,0:T(8,128)S(1)} async-done(((f32[8,16,1664]{2,1,0:T(8,128)}), f32[8,16,1664]{2,1,0:T(8,128)S(1)}, u32[]{:S(2)}, u32[]{:S(2)}) %all-to-all-start.4) | async-done | bytes 852000 | tf_op jit(solution)/shard_map/all_to_all | solution.py:544
  63.0 0.0 copy-done
  63.0 0.0 copy-done.1
  63.0 3.7 %shard_map.201 = (f32[272,128]{1,0:T(8,128)S(1)}, f32[384,128]{1,0:T(8,128)S(1)}, f32[32,128]{1,0:T(8,128)S(1)}, f32[8,128]{1,0:T(8,128)S(1)}) custom-call(f32[8,16,1664]{2,1,0:T(8,128)S(1)} %all-to-all-done.4.in_ref, f32[128,128]{1,0:T(8,128)S(1)} %get-tuple-element.99.tab_ref, bf16[32,10240]{1,0:T(8,128)(2,1)S(1)} %copy-done, f32[1,10240]{1,0:T(1,128)S(1)} %bitcast.68, ...), custom_call_target="tpu_custom_call" | custom-call | tf_op jit(solution)/shard_map/pallas_call | solution.py:546
  66.7 11.8 %all-gather = f32[1088,128]{1,0:T(8,128)S(1)} all-gather(f32[272,128]{1,0:T(8,128)S(1)} %get-tuple-element.101), channel_id=2, replica_groups=mesh['y'=4,'z'=16,'c'=2,'x'=4] {'x'}, dimensions={0}, use_global_device_ids=true | all-gather | bytes 696320 | tf_op jit(solution)/shard_map/all_gather | solution.py:551
  78.6 0.0 copy-done.13
  78.6 0.0 copy-start.15
  78.6 0.0 copy-start.5
  78.6 0.0 copy-start.8
  78.6 0.0 copy-start.4
  78.6 0.0 copy-start.6
  78.6 0.0 copy-start.7
  78.6 0.0 copy-start.9
  78.6 0.0 copy-start.10
  78.7 0.0 copy-start.11
  78.7 0.0 copy-start.12
  78.7 4.0 %shard_map.202 = (f32[8,16,1536]{2,1,0:T(8,128)S(1)}, f32[128,128]{1,0:T(8,128)S(1)}, f32[128,128]{1,0:T(8,128)S(1)}, f32[16,128]{1,0:T(8,128)S(1)}) custom-call(f32[4,16]{1,0:T(4,128)S(1)} %copy-done.13, f32[4,272,128]{2,1,0:T(8,128)S(1)} %bitcast.74, f32[384,128]{1,0:T(8,128)S(1)} %get-tuple-element.102.ids_ref, ...), custom_call_target="tpu_custom_call" | custom-call | tf_op jit(solution)/shard_map/pallas_call | solution.py:554
  82.7 17.0 %all_to_all.48.in_ref = f32[8,16,1536]{2,1,0:T(8,128)S(1)} all-to-all(f32[8,16,1536]{2,1,0:T(8,128)S(1)} %get-tuple-element.104), channel_id=1, replica_groups=mesh['y'=4,'z'=16,'c'=2,'x'=4] {'y','c'}, dimensions={0} | all-to-all | bytes 1572864 | tf_op jit(solution)/shard_map/all_to_all | solution.py:560
  99.7 0.8 shard_map.203
  100.5 5.9 %all-to-all-start.6 = ((f32[16,8,512]{2,1,0:T(8,128)}), f32[16,8,512]{2,1,0:T(8,128)S(1)}, u32[]{:S(2)}, u32[]{:S(2)}) async-start(f32[16,8,512]{2,1,0:T(8,128)} %shard_map.203), calls=%async_computation.6 | async-start | bytes 524288 | tf_op jit(solution)/shard_map/all_to_all | solution.py:564
  106.4 0.0 copy-done.15
  106.4 0.1 copy.178.ridge_ref
  106.5 0.5 slice.40
  107.6 0.0 copy-done.5
  107.6 0.0 copy-done.8
  107.7 1.9 %shard_map.204.c_ref = f32[4,4096]{1,0:T(4,128)S(1)} custom-call(f32[128,128]{1,0:T(8,128)S(1)} %get-tuple-element.105.tab_ref, s32[1,4096]{1,0:T(1,128)S(1)} %bitcast.80, s32[1,4096]{1,0:T(1,128)S(1)} %bitcast.83), custom_call_target="tpu_custom_call" | custom-call | tf_op jit(solution)/shard_map/pallas_call | solution.py:566
  109.6 9.7 %all-to-all-done.6.got_ref = f32[16,8,512]{2,1,0:T(8,128)S(1)} async-done(((f32[16,8,512]{2,1,0:T(8,128)}), f32[16,8,512]{2,1,0:T(8,128)S(1)}, u32[]{:S(2)}, u32[]{:S(2)}) %all-to-all-start.6) | async-done | bytes 262176 | tf_op jit(solution)/shard_map/all_to_all | solution.py:564
  119.3 0.0 copy-done.4
  119.3 0.0 copy-done.6
  119.3 0.0 copy-done.7
  119.3 0.0 copy-done.9
  119.3 0.0 copy-done.10
  119.4 0.0 copy-done.11
  119.4 0.0 copy-done.12
  119.4 5.0 %shard_map.205 = (f32[4,4096]{1,0:T(4,128)}, f32[16,80]{1,0:T(8,128)S(1)}, f32[1,128]{1,0:T(1,128)S(1)}) custom-call(f32[16,8,512]{2,1,0:T(8,128)S(1)} %all-to-all-done.6.got_ref, f32[4,4096]{1,0:T(4,128)S(1)} %shard_map.204.c_ref, s32[1,4096]{1,0:T(1,128)S(1)} %get-tuple-element.106.rank_ref, s32[1,4096]{1,0:T(1,128)S(1)} %bitcast.81, ...), custom_call_target="tpu_custom_call" | custom-call | tf_op jit(solution)/shard_map/pallas_call | solution.py:568
  124.4 0.0 copy-start.2
  124.4 0.0 copy-start.3
  124.4 18.4 %all_to_all.49 = f32[32,1,128]{2,1,0:T(1,128)S(1)} all-to-all(f32[32,1,128]{2,1,0:T(1,128)S(1)} %broadcast_in_dim.119), channel_id=1, replica_groups=mesh['y'=4,'z'=16,'c'=2,'x'=4] {'y','c','x'}, dimensions={0} | all-to-all | bytes 32768 | tf_op jit(solution)/shard_map/all_to_all | solution.py:592
  142.9 16.5 %all_to_all.50.sums_ref = f32[16,1,128]{2,1,0:T(1,128)S(1)} all-to-all(f32[16,1,128]{2,1,0:T(1,128)S(1)} %broadcast_in_dim.120), channel_id=1, replica_groups=mesh['y'=4,'z'=16,'c'=2,'x'=4] {'z'}, dimensions={0} | all-to-all | bytes 16384 | tf_op jit(solution)/shard_map/all_to_all | solution.py:596
  159.4 0.0 copy-done.2
  159.4 0.0 copy-done.3
  159.4 1.7 %shard_map.206 = (f32[4,4096]{1,0:T(4,128)}, f32[4,4096]{1,0:T(4,128)}, f32[4,4096]{1,0:T(4,128)}, f32[16,80]{1,0:T(8,128)}, f32[16,80]{1,0:T(8,128)}, /*index=5*/f32[16,80]{1,0:T(8,128)}) custom-call(f32[16,1,128]{2,1,0:T(1,128)S(1)} %all_to_all.50.sums_ref, f32[4,4096]{1,0:T(4,128)S(1)} %copy-done.2, f32[4,4096]{1,0:T(4,128)S(1)} %copy-done.6, ...), custom_call_target="tpu_custom_call" | custom-call | tf_op jit(solution)/shard_map/pallas_call | solution.py:599
  (7 shorter events, 0.1 us)
Async XLA Ops:
  0.6 49.4 %copy-start.14 = (f32[4]{0:T(128)S(1)}, f32[4]{0:T(128)}, u32[]{:S(2)}) copy-start(f32[4]{0:T(128)} %param.31) | copy-start | bytes 52
  0.6 62.4 %copy-start = (bf16[32,10240]{1,0:T(8,128)(2,1)S(1)}, bf16[32,10240]{1,0:T(8,128)(2,1)}, u32[]{:S(2)}) copy-start(bf16[32,10240]{1,0:T(8,128)(2,1)} %geno_ref.3) | copy-start | bytes 1966084
  0.7 62.4 %copy-start.1 = (f32[10240]{0:T(1024)S(1)}, f32[10240]{0:T(1024)}, u32[]{:S(2)}) copy-start(f32[10240]{0:T(1024)} %param.30) | copy-start | bytes 122884
  39.0 39.6 %copy-start.13 = (f32[4,16]{1,0:T(4,128)S(1)}, f32[4,16]{1,0:T(4,128)}, u32[]{:S(2)}) copy-start(f32[4,16]{1,0:T(4,128)} %mix_ref.1) | copy-start | bytes 772
  39.0 24.0 %all-to-all-start.4 = ((f32[8,16,1664]{2,1,0:T(8,128)}), f32[8,16,1664]{2,1,0:T(8,128)S(1)}, u32[]{:S(2)}, u32[]{:S(2)}) async-start(f32[8,16,1664]{2,1,0:T(8,128)} %shard_map.200), calls=%async_computation.4 | async-start | bytes 1703936 | tf_op jit(solution)/shard_map/all_to_all | solution.py:544
  78.6 27.8 %copy-start.15 = (f32[16]{0:T(128)S(1)}, f32[16]{0:T(128)}, u32[]{:S(2)}) copy-start(f32[16]{0:T(128)} %param.32) | copy-start | bytes 196
  78.6 29.1 %copy-start.5 = (s32[4096]{0:T(1024)S(1)}, s32[4096]{0:T(1024)}, u32[]{:S(2)}) copy-start(s32[4096]{0:T(1024)} %param.34) | copy-start | bytes 49156
  78.6 29.1 %copy-start.8 = (s32[4096]{0:T(1024)S(1)}, s32[4096]{0:T(1024)}, u32[]{:S(2)}) copy-start(s32[4096]{0:T(1024)} %param.35) | copy-start | bytes 49156
  78.6 40.7 %copy-start.4 = (f32[4,4096]{1,0:T(4,128)S(1)}, f32[4,4096]{1,0:T(4,128)}, u32[]{:S(2)}) copy-start(f32[4,4096]{1,0:T(4,128)} %dir_ref.5) | copy-start | bytes 196612
  78.6 40.7 %copy-start.6 = (f32[4,4096]{1,0:T(4,128)S(1)}, f32[4,4096]{1,0:T(4,128)}, u32[]{:S(2)}) copy-start(f32[4,4096]{1,0:T(4,128)} %res_ref.3) | copy-start | bytes 196612
  78.6 40.7 %copy-start.7 = (f32[4,4096]{1,0:T(4,128)S(1)}, f32[4,4096]{1,0:T(4,128)}, u32[]{:S(2)}) copy-start(f32[4,4096]{1,0:T(4,128)} %inv_ref.3) | copy-start | bytes 196612
  78.6 40.7 %copy-start.9 = (f32[4,4096]{1,0:T(4,128)S(1)}, f32[4,4096]{1,0:T(4,128)}, u32[]{:S(2)}) copy-start(f32[4,4096]{1,0:T(4,128)} %rec_ref.1) | copy-start | bytes 196612
  78.6 40.7 %copy-start.10 = (f32[16,1,80]{2,1,0:T(1,128)S(1)}, f32[16,1,80]{2,1,0:T(1,128)}, u32[]{:S(2)}) copy-start(f32[16,1,80]{2,1,0:T(1,128)} %param.27) | copy-start | bytes 15364
  78.7 40.7 %copy-start.11 = (f32[16,1,80]{2,1,0:T(1,128)S(1)}, f32[16,1,80]{2,1,0:T(1,128)}, u32[]{:S(2)}) copy-start(f32[16,1,80]{2,1,0:T(1,128)} %param.26) | copy-start | bytes 15364
  78.7 40.7 %copy-start.12 = (f32[16,1,80]{2,1,0:T(1,128)S(1)}, f32[16,1,80]{2,1,0:T(1,128)}, u32[]{:S(2)}) copy-start(f32[16,1,80]{2,1,0:T(1,128)} %param.28) | copy-start | bytes 15364
  100.5 18.8 %all-to-all-start.6 = ((f32[16,8,512]{2,1,0:T(8,128)}), f32[16,8,512]{2,1,0:T(8,128)S(1)}, u32[]{:S(2)}, u32[]{:S(2)}) async-start(f32[16,8,512]{2,1,0:T(8,128)} %shard_map.203), calls=%async_computation.6 | async-start | bytes 524288 | tf_op jit(solution)/shard_map/all_to_all | solution.py:564
  124.4 34.9 %copy-start.2 = (f32[4,4096]{1,0:T(4,128)S(1)}, f32[4,4096]{1,0:T(4,128)}, u32[]{:S(2)}) copy-start(f32[4,4096]{1,0:T(4,128)} %sol_ref.1) | copy-start | bytes 196612
  124.4 34.9 %copy-start.3 = (f32[16,1,80]{2,1,0:T(1,128)S(1)}, f32[16,1,80]{2,1,0:T(1,128)}, u32[]{:S(2)}) copy-start(f32[16,1,80]{2,1,0:T(1,128)} %param.25) | copy-start | bytes 15364

commit v3 on v2

--- a/solution.py
+++ b/solution.py
@@ -16,7 +16,6 @@
 F32 = jnp.float32
 BF16 = jnp.bfloat16
 NT = (((1,), (1,)), ((), ()))
-TN = (((0,), (0,)), ((), ()))
 NN = (((1,), (0,)), ((), ()))
 
 
@@ -52,10 +51,8 @@
     return jnp.where(known == 2, 2.0, jnp.where(known == 1, 4.0 / 3.0, 1.0)).astype(F32)
 
 
-def dam_place(dam, animals):
-    local = dam & (animals - 1)
-    block = jnp.where(dam >= 0, local >> 7, -1)
-    return block, local & 127
+def place_in(local, known):
+    return jnp.where(known, (local >> 7) & 15, -1), ((local >> 11) << 7) + (local & 127)
 
 
 def one_hot(index, rows):
@@ -67,8 +64,18 @@
     return jnp.sum(jnp.where(in_group, found[t * rows : (t + 1) * rows], 0.0), axis=0, keepdims=True)
 
 
-def table_of(ref):
-    return jnp.concatenate([p.astype(BF16) for p in parts(ref[...])], axis=0)
+def side_by_side(table):
+    return jnp.concatenate([p.astype(BF16) for p in parts(table)], axis=1)
+
+
+def look_up(table, index, rows):
+    hit = one_hot(index, rows)
+    return dot(table, jnp.concatenate([hit, hit], axis=0))
+
+
+def both_halves(acc_ref, first, rows):
+    at = slice(first, first + rows)
+    return jnp.concatenate([acc_ref[at, :128], acc_ref[at, 128:]], axis=0)
 
 
 def masked(in_group, fields):
@@ -103,47 +110,51 @@
     for t in range(traits):
         for b in range(blocks):
             tab_ref[t * blocks + b : t * blocks + b + 1, :] = dir_ref[t : t + 1, b * 128 : (b + 1) * 128]
-    table = table_of(tab_ref)
-    half = traits * blocks
+    table = side_by_side(tab_ref[...])
     before = (rows_at(n, n) < lax.broadcasted_iota(jnp.int32, (n, n), 1)).astype(F32).astype(BF16)
     acc_ref[...] = jnp.zeros(acc_ref.shape, F32)
+    short = CAP // 2
 
     def step(k, carry):
         at = pl.ds(pl.multiple_of(k * n, n), n)
         sire = sire_ref[:, at]
         dam = dam_ref[:, at]
         weight = weights(sire, dam)
-        block, offset = dam_place(dam, animals)
-        found = dot(table, one_hot(offset, 128))
-        found = found[:half] + found[half:]
-        in_block = rows_at(blocks, n) == block
+        local_dam = dam & (animals - 1)
+        found = look_up(table, local_dam & 127, 128)
+        in_block = rows_at(blocks, n) == jnp.where(dam >= 0, local_dam >> 7, -1)
         own = dir_ref[:, at]
-        is_owner = rows_at(herd, n) == owner_row(sire, animals, shape)
+        row = owner_row(sire, animals, shape)
+        is_owner = rows_at(herd, n) == row
         owners = is_owner.astype(F32).astype(BF16)
         earlier = dot(owners, before) + carry
         rank = jnp.sum(jnp.where(is_owner, earlier, 0.0), axis=0, keepdims=True).astype(jnp.int32)
         rank = jnp.where((sire >= 0) & (rank < LIST), rank, -1)
         rank_ref[:, at] = rank
         local = (sire & (animals - 1)) + 1
-        high = [(local & ~63).astype(F32), weight * 1.5]
-        low = [(local & 63).astype(F32), jnp.zeros((1, n), F32)]
+        fields = [(local & ~63).astype(F32), (local & 63).astype(F32), weight * 1.5]
         for t in range(traits):
-            hi, lo = parts(weight * (own[t : t + 1] - 0.5 * pick(found, in_block, t)))
-            high.append(hi)
-            low.append(lo)
-        acc_ref[...] += dot(masked(rows_at(CAP, n) == rank, high + low), owners, NT)
-        return carry + jnp.sum(jnp.where(is_owner, 1.0, 0.0), axis=1, keepdims=True)
-
-    count = lax.fori_loop(0, animals // n, step, jnp.zeros((herd, 1), F32))
+            fields += parts(weight * (own[t : t + 1] - 0.5 * pick(found, in_block, t)))
+        in_row = rows_at(short, n) == jnp.where(rank >= 0, rank & (short - 1), -1)
+        target = one_hot((rank >> (short.bit_length() - 1)) * herd + row, 2 * herd)
+        acc_ref[...] += dot(masked(in_row, fields), target, NT)
+        return earlier[:, n - 1 :] + owners[:, n - 1 :].astype(F32)
+
+    count = lax.fori_loop(0, animals // n, step, jnp.zeros((herd, 1), F32), unroll=True)
     width = (2 + traits) * CAP
     overflow = jnp.where(jnp.max(count, axis=0, keepdims=True) > LIST + 0.5, 1.0, 0.0)
     lane = lax.broadcasted_iota(jnp.int32, (herd, 128), 1)
+
+    def slots(f):
+        at = slice(f * short, (f + 1) * short)
+        return jnp.concatenate([acc_ref[at, :herd], acc_ref[at, herd:]], axis=0)
+
+    lines = [slots(0) + slots(1), slots(2)] + [slots(3 + 2 * t) + slots(4 + 2 * t) for t in range(traits)]
     for j in range(width // 128):
-        at = slice(j * 128, (j + 1) * 128)
-        block = (acc_ref[at, :] + acc_ref[width + j * 128 : width + (j + 1) * 128, :]).T
+        block = jnp.concatenate(lines[2 * j : 2 * j + 2], axis=0).T
         if j == 0:
             block = jnp.where(lane == 127, overflow, block)
-        out_ref[:, :, at] = block.reshape(nz, ny * nc, 128)
+        out_ref[:, :, j * 128 : (j + 1) * 128] = block.reshape(nz, ny * nc, 128)
     rows = ny * nc
     columns = dir_a_ref.shape[1]
     for j in range(dir_a_ref.shape[0] // rows):
@@ -177,15 +188,15 @@
 
 
 def gather_kernel(
-    in_ref, tab_ref, geno_ref, freq_ref, gw_ref, out_ref, turned_ref, weight_ref, over_ref,
-    joined_ref, acc_ref, *, shape, columns, lists, scale,
+    in_ref, geno_ref, freq_ref, gw_ref, out_ref, added_ref, turned_ref, weight_ref, over_ref,
+    joined_ref, acc_ref, wide_ref, *, shape, columns, lists, scale,
 ):
     ny, nz, nc = shape
     herd = ny * nz * nc
     traits = in_ref.shape[1]
-    half = tab_ref.shape[0]
     blocks = weight_ref.shape[0]
-    here = half // blocks
+    short = blocks // 2
+    here = added_ref.shape[0] // blocks
     genotyped = geno_ref.shape[0]
     for j in range(lists // 128):
         at = slice(j * 128, (j + 1) * 128)
@@ -197,20 +208,20 @@
     def step(k, _):
         r = pl.multiple_of(k * group, group)
         place = flat(turned_ref, r, group).astype(jnp.int32) - 1
-        in_block = rows_at(blocks, group * herd) == (place >> 7)
-        high, low = [], []
+        row, column = place_in(place, place >= 0)
+        fields = [flat(turned_ref, CAP + r, group)]
         for t in range(here):
-            hi, lo = parts(flat(turned_ref, (2 + t) * CAP + r, group))
-            high.append(hi)
-            low.append(lo)
-        fields = masked(in_block, high + low + [flat(turned_ref, CAP + r, group)])
-        acc_ref[...] += dot(fields, one_hot(place & 127, 128), NT)
+            fields += parts(flat(turned_ref, (2 + t) * CAP + r, group))
+        acc_ref[...] += dot(masked(rows_at(short, group * herd) == row, fields), one_hot(column, 256), NT)
         return 0
 
-    lax.fori_loop(0, CAP // group, step, 0)
-    weight_ref[...] = acc_ref[2 * half :, :] * (0.25 / 1.5)
-    out_ref[traits : traits + half, :] = acc_ref[:half, :] + acc_ref[half : 2 * half, :]
-    out_ref[traits + half :, :] = tab_ref[...]
+    lax.fori_loop(0, CAP // group, step, 0, unroll=True)
+    weight_ref[...] = both_halves(acc_ref, 0, short) * (0.25 / 1.5)
+    for t in range(here):
+        first = (1 + 2 * t) * short
+        added_ref[t * blocks : (t + 1) * blocks, :] = both_halves(acc_ref, first, short) + both_halves(
+            acc_ref, first + short, short
+        )
 
     width = nz * nc * columns
     total = jnp.zeros((3 * traits, genotyped), F32)
@@ -228,9 +239,19 @@
         total = total + dot(stack, geno_ref[:, at], NT)
         bias = bias + jnp.sum(values * (2.0 * freq_ref[:, at]), axis=1, keepdims=True)
     rows = total[:traits] + total[traits : 2 * traits] + total[2 * traits :]
-    out_ref[:traits, :] = jnp.zeros((traits, 128), F32)
-    out_ref[:traits, :genotyped] = (rows - bias) * scale
-    out_ref[:traits, genotyped : genotyped + 1] = gw_ref[...]
+    wide_ref[...] = jnp.zeros((traits, 128), F32)
+    wide_ref[:, :genotyped] = (rows - bias) * scale
+    packed = together([wide_ref[x * here : (x + 1) * here, :] for x in range(traits // here)], genotyped)
+    for x in range(out_ref.shape[0]):
+        out_ref[x, :here, :] = packed
+        out_ref[x, here:, :] = gw_ref[...]
+
+
+def together(groups, width):
+    total = groups[0]
+    for x in range(1, len(groups)):
+        total = total + pltpu.roll(groups[x], x * width, 1)
+    return total
 
 
 def flat(ref, first, group):
@@ -238,40 +259,38 @@
     return jnp.concatenate([tile[j : j + 1] for j in range(group)], axis=1)
 
 
+def mixed(mix_ref, all_ref, t, blocks):
+    total = jnp.zeros((blocks, 128), F32)
+    here = all_ref.shape[1] // blocks
+    for x in range(all_ref.shape[0]):
+        for s in range(here):
+            total = total + mix_ref[t, x * here + s] * all_ref[x, s * blocks : (s + 1) * blocks, :]
+    return total
+
+
 def reply_kernel(
-    mix_ref, all_ref, ids_ref, weight_ref, geno_ref, freq_ref,
-    out_ref, tab_ref, inc_ref, resid_ref, vals_ref, rows_ref, summed_ref, *, shape, columns, scale,
+    mix_ref, all_ref, pred_ref, ids_ref, geno_ref, freq_ref,
+    out_ref, tab_ref, resid_ref, vals_ref, summed_ref, *, shape, columns, scale,
 ):
     ny, nz, nc = shape
     herd = ny * nz * nc
     nx = all_ref.shape[0]
     traits = resid_ref.shape[0]
     half = tab_ref.shape[0]
-    blocks = weight_ref.shape[0]
+    blocks = 32
     here = half // blocks
     genotyped = geno_ref.shape[0]
     for t in range(here):
-        value = jnp.zeros((blocks, 128), F32)
-        added = jnp.zeros((blocks, 128), F32)
-        for x in range(nx):
-            for s in range(here):
-                factor = mix_ref[t, x * here + s]
-                at = traits + s * blocks
-                added = added + factor * all_ref[x, at : at + blocks, :]
-                value = value + factor * all_ref[x, half + at : half + at + blocks, :]
-        at = slice(t * blocks, (t + 1) * blocks)
-        tab_ref[at, :] = value
-        inc_ref[at, :] = weight_ref[...] * value - 0.5 * added
-
-    table = table_of(tab_ref)
+        tab_ref[t * blocks : (t + 1) * blocks, :] = mixed(mix_ref, all_ref, t, blocks)
+
+    table = side_by_side(tab_ref[...])
     group = 8
 
     def step(k, _):
         r = pl.multiple_of(k * group, group)
         place = flat(ids_ref, r, group).astype(jnp.int32) - 1
         in_block = rows_at(blocks, group * herd) == (place >> 7)
-        found = dot(table, one_hot(place & 127, 128))
-        found = found[:half] + found[half:]
+        found = look_up(table, place & 127, 128)
         for t in range(here):
             value = pick(found, in_block, t)
             vals_ref[pl.ds(t * CAP + r, group), :] = jnp.concatenate(
@@ -279,23 +298,26 @@
             )
         return 0
 
-    lax.fori_loop(0, CAP // group, step, 0)
+    lax.fori_loop(0, CAP // group, step, 0, unroll=True)
     values = here * CAP
     for j in range(values // 128):
         at = slice(j * 128, (j + 1) * 128)
         out_ref[:, :nz, at] = vals_ref[at, :].T.reshape(ny * nc, nz, 128)
 
+    total = pred_ref[0]
+    for x in range(1, nx):
+        total = total + pred_ref[x]
+    lane = lax.broadcasted_iota(jnp.int32, (here, 128), 1)
+    own = [
+        jnp.concatenate([all_ref[x, s * blocks : s * blocks + 1, :] for s in range(here)], axis=0)
+        for x in range(nx)
+    ]
+    own = together([jnp.where(lane < genotyped, o, 0.0) for o in own], genotyped)
+    packed = total[here:] * (own - total[:here])
     for x in range(nx):
-        for s in range(here):
-            at = traits + half + s * blocks
-            rows_ref[x * here + s : x * here + s + 1, :] = all_ref[x, at : at + 1, :]
-    total = all_ref[0, :traits, :]
-    for x in range(1, nx):
-        total = total + all_ref[x, :traits, :]
-    lane = lax.broadcasted_iota(jnp.int32, (traits, 128), 1)
-    weight = jnp.sum(jnp.where(lane == genotyped, total, 0.0), axis=1, keepdims=True)
-    resid = jnp.where(lane < genotyped, weight * (rows_ref[...] - total), 0.0)
-    resid_ref[...] = resid
+        rows = pltpu.roll(packed, 128 - x * genotyped, 1) if x else packed
+        resid_ref[x * here : (x + 1) * here, :] = jnp.where(lane < genotyped, rows, 0.0)
+    resid = resid_ref[...]
     stack = jnp.concatenate([p.astype(BF16) for p in parts(resid, 3)], axis=0)[:, :genotyped]
     summed = jnp.sum(resid, axis=1, keepdims=True)
     width = nz * nc * columns
@@ -330,30 +352,28 @@
 def dams_kernel(tab_ref, sire_ref, dam_ref, out_ref):
     traits, animals = out_ref.shape
     blocks = animals // 128
-    half = traits * blocks
     n = CHUNK
     for t in range(traits):
         for b in range(blocks):
             out_ref[t : t + 1, b * 128 : (b + 1) * 128] = tab_ref[t * blocks + b : t * blocks + b + 1, :]
-    table = table_of(tab_ref)
+    table = side_by_side(tab_ref[...])
 
     def step(k, _):
         at = pl.ds(pl.multiple_of(k * n, n), n)
         dam = dam_ref[:, at]
         weight = weights(sire_ref[:, at], dam)
-        block, offset = dam_place(dam, animals)
-        found = dot(table, one_hot(offset, 128))
-        found = found[:half] + found[half:]
-        in_block = rows_at(blocks, n) == block
+        local = dam & (animals - 1)
+        found = look_up(table, local & 127, 128)
+        in_block = rows_at(blocks, n) == jnp.where(dam >= 0, local >> 7, -1)
         for t in range(traits):
             out_ref[t : t + 1, at] = weight * (out_ref[t : t + 1, at] - 0.5 * pick(found, in_block, t))
         return 0
 
-    lax.fori_loop(0, animals // n, step, 0)
+    lax.fori_loop(0, animals // n, step, 0, unroll=True)
 
 
 def image_kernel(
-    got_ref, c_ref, rank_ref, sire_ref, dam_ref, inc_ref, resid_ref,
+    mix_ref, got_ref, c_ref, rank_ref, sire_ref, dam_ref, added_ref, weight_ref, mixed_ref, resid_ref,
     dir_ref, rec_ref, res_ref, inv_ref, ridge_ref, dir_a_ref, res_a_ref, inv_a_ref,
     image_ref, image_a_ref, sums_ref, acc_ref, tab_ref, *, shape,
 ):
@@ -362,11 +382,9 @@
     herd, near = ny * nz * nc, ny * nc
     blocks = animals // 128
     n = CHUNK
-    half = traits * blocks
+    short = blocks // 2
     wide = traits * CAP
-    table = jnp.concatenate(
-        [p.astype(BF16) for p in parts(got_ref[:, :, :wide].reshape(herd, wide))], axis=1
-    )
+    table = side_by_side(got_ref[:, :, :wide].reshape(herd, wide).T)
     acc_ref[...] = jnp.zeros(acc_ref.shape, F32)
 
     def step(k, _):
@@ -374,22 +392,24 @@
         sire = sire_ref[:, at]
         dam = dam_ref[:, at]
         weight = weights(sire, dam)
-        found = dot(table, one_hot(owner_row(sire, animals, shape), herd), TN)
-        found = found[:wide] + found[wide:]
+        found = look_up(table, owner_row(sire, animals, shape), herd)
         in_slot = rows_at(CAP, n) == rank_ref[:, at]
-        block, offset = dam_place(dam, animals)
-        high, low = [], []
+        row, column = place_in(dam & (animals - 1), dam >= 0)
+        fields = []
         for t in range(traits):
             scaled = c_ref[t : t + 1, at] - 0.5 * weight * pick(found, in_slot, t)
             image_ref[t : t + 1, at] = scaled
-            hi, lo = parts(scaled)
-            high.append(hi)
-            low.append(lo)
-        acc_ref[...] += dot(masked(rows_at(blocks, n) == block, high + low), one_hot(offset, 128), NT)
+            fields += parts(scaled)
+        acc_ref[...] += dot(masked(rows_at(short, n) == row, fields), one_hot(column, 256), NT)
         return 0
 
-    lax.fori_loop(0, animals // n, step, 0)
-    tab_ref[...] = inc_ref[...] - 0.5 * (acc_ref[:half, :] + acc_ref[half:, :])
+    lax.fori_loop(0, animals // n, step, 0, unroll=True)
+    for t in range(traits):
+        at = slice(t * blocks, (t + 1) * blocks)
+        first = 2 * t * short
+        down = both_halves(acc_ref, first, short) + both_halves(acc_ref, first + short, short)
+        down = down + mixed(mix_ref, added_ref, t, blocks)
+        tab_ref[at, :] = weight_ref[...] * mixed_ref[at, :] - 0.5 * down
     for b in range(blocks):
         for t in range(traits):
             at = (slice(t, t + 1), slice(b * 128, (b + 1) * 128))
@@ -527,55 +547,60 @@
     d_a, r_a, s_a, i_a = (a[:, 0, :] for a in (dir_a, res_a, sol_a, inv_diag_a))
     freq = allele_freq[None, :]
     sire_row, dam_row = sire[None, :], dam[None, :]
-    weight_here = lax.dynamic_update_slice(
-        jnp.zeros((traits, 1), F32), geno_weight[:, None], (x_index * here, 0)
-    )
+    mine = jnp.arange(128) // genotyped == x_index
+    weight_here = jnp.where(mine[None, :], geno_weight[:, None], 0.0)
 
     out_z, rank, table = call(
         functools.partial(lists_kernel, shape=shape),
         (sds(nz, near, lists + spare), jax.ShapeDtypeStruct((1, animals), jnp.int32), sds(half, 128)),
-        scratch=[vmem(2 * lists, herd)],
+        scratch=[vmem((3 + 2 * here) * CAP // 2, 2 * herd)],
     )(dir_u, d_a, sire_row, dam_row)
     in_z = lax.all_to_all(out_z, "z", 0, 0, tiled=True)
+    all_tables = lax.all_gather(table, "x", axis=0)
+    in_z, all_tables = lax.optimization_barrier((in_z, all_tables))
     out_near = call(
         functools.partial(forward_kernel, columns=columns, lists=lists),
         sds(near, traits, lists + nz * columns),
     )(in_z)
     in_near = lax.all_to_all(out_near, ("y", "c"), 0, 0, tiled=True)
 
-    to_x, turned, weight_sum, over = call(
+    to_x, added, turned, weight_sum, over = call(
         functools.partial(gather_kernel, shape=shape, columns=columns, lists=lists, scale=scale),
-        (sds(traits + 2 * half, 128), sds(lists, herd), sds(blocks, 128), sds(8, 128)),
-        scratch=[vmem(traits, nz * nc * columns), vmem(2 * half + blocks, 128)],
-    )(in_near, table, genotypes, freq, weight_here)
-    from_x = lax.all_gather(to_x, "x", axis=0)
+        (sds(nx, 2 * here, 128), sds(half, 128), sds(lists, herd), sds(blocks, 128), sds(8, 128)),
+        scratch=[vmem(traits, nz * nc * columns), vmem((1 + 2 * here) * blocks // 2, 256), vmem(traits, 128)],
+    )(in_near, genotypes, freq, weight_here)
+    from_x = lax.all_to_all(to_x, "x", 0, 0, tiled=True)
 
     on_chip = pl.BlockSpec(memory_space=pltpu.VMEM)
-    back_near, mixed_table, incoming, resid = call(
+    scalars = pl.BlockSpec(memory_space=pltpu.SMEM)
+    back_near, mixed_table, resid = call(
         functools.partial(reply_kernel, shape=shape, columns=columns, scale=scale),
-        (sds(near, traits, values + nz * columns), sds(half, 128), sds(half, 128), sds(traits, 128)),
-        scratch=[vmem(values, herd), vmem(traits, 128), vmem(traits, nz * nc * columns)],
-        in_specs=[pl.BlockSpec(memory_space=pltpu.SMEM)] + [on_chip] * 5,
-    )(genetic_inv, from_x, turned, weight_sum, genotypes, freq)
+        (sds(near, traits, values + nz * columns), sds(half, 128), sds(traits, 128)),
+        scratch=[vmem(values, herd), vmem(traits, nz * nc * columns)],
+        in_specs=[scalars] + [on_chip] * 5,
+    )(genetic_inv, all_tables, from_x, turned, genotypes, freq)
     got_near = lax.all_to_all(back_near, ("y", "c"), 0, 0, tiled=True)
     back_z = call(
         functools.partial(backward_kernel, columns=columns, values=values), sds(nz, near, values + spare)
     )(got_near)
+    back_z, added = lax.optimization_barrier((back_z, added))
     got_z = lax.all_to_all(back_z, "z", 0, 0, tiled=True)
+    all_added = lax.all_gather(added, "x", axis=0)
 
     c_term = call(dams_kernel, sds(here, animals))(mixed_table, sire_row, dam_row)
     own_resid = lax.dynamic_slice_in_dim(resid, x_index * here, here, 0)
     image_u, image_a, sums = call(
         functools.partial(image_kernel, shape=shape),
         (sds(here, animals), sds(traits, columns), sds(1, 128)),
-        scratch=[vmem(2 * half, 128), vmem(half, 128)],
+        scratch=[vmem(here * blocks, 256), vmem(half, 128)],
+        in_specs=[scalars] + [on_chip] * 17,
     )(
-        got_z, c_term, rank, sire_row, dam_row, incoming, own_resid,
+        genetic_inv, got_z, c_term, rank, sire_row, dam_row, all_added, weight_sum, mixed_table, own_resid,
         dir_u, rec_weight, res_u, inv_diag_u, snp_ridge[:, None], d_a, r_a, i_a,
     )
 
     def by_blocks():
-        dir_all = from_x[:, traits + half :, :].reshape(traits, animals)
+        dir_all = all_tables.reshape(traits, animals)
         mixed = jnp.dot(genetic_inv, dir_all, precision=lax.Precision.HIGHEST)
         image = rec_weight * dir_u + pedigree_by_blocks(mixed, sire, dam, herd, herd_index)
         image = image.at[:, :genotyped].add(own_resid[:, :genotyped])

time: 162 us -> 153 us (0.944)
  starting transfers between devices: 16.9 us -> 32.6 us
  blocking collectives: 94.5 us -> 81.9 us
  Pallas kernels: 24.7 us -> 17.3 us
  waiting for transfers between devices: 22.6 us -> 18.4 us
    all_to_all x1, blocking collectives: 30.8 us -> 8.04 us  [body(): from_x = lax.all_to_all(to_x, 'x', 0, 0, tiled=True)]
    all_to_all x0 -> x1, starting transfers between devices: none -> 15.7 us  [body(): in_z = lax.all_to_all(out_z, 'z', 0, 0, tiled=True)]
    all_to_all x1, waiting for transfers between devices: 9.7 us -> 0.88 us  [body(): got_z = lax.all_to_all(back_z, 'z', 0, 0, tiled=True)]
    all_gather x1 -> x2, blocking collectives: 11.8 us -> 20.6 us  [the longest x1 10.6 us: body(): all_tables = lax.all_gather(table, 'x', axis=0)]
    all_to_all x0 -> x1, waiting for transfers between devices: none -> 4.63 us  [body(): in_z = lax.all_to_all(out_z, 'z', 0, 0, tiled=True)]
    all_to_all x1, blocking collectives: 16.5 us -> 19.7 us  [body(): lax.all_to_all(jnp.broadcast_to(close, (nz, 1, 128)), 'z', 0, 0, tiled=True)]
    pallas_call x1, Pallas kernels: 5.04 us -> 3.18 us  [body(): call(functools.partial(image_kernel, shape=shape), (sds(here, animals), s...]
    all_to_all x1, blocking collectives: 18.4 us -> 16.5 us  [body(): lax.all_to_all(jnp.broadcast_to(sums[None], (near * nx, 1, 128)), ('y', '...]
  transfers between devices with their start and end apart: 2 -> 3, of which waited for: 2 -> 3; matrix products, arithmetic and copies ran while one was open for 0% -> 0% of each run, Pallas kernels for 1% -> 1%
where the time goes in v3:
time: 153 us
  blocking collectives  81.9 us (54%)
  starting transfers between devices  32.6 us (21%)
  waiting for transfers between devices  18.4 us (12%)
  Pallas kernels  17.3 us (11%)
    all_to_all x1, blocking collectives, body(): lax.all_to_all(jnp.broadcast_to(close, (nz, 1, 128)), 'z', 0, 0, tiled=True)  19.7 us
    all_to_all x1, blocking collectives, body(): got_near = lax.all_to_all(back_near, ('y', 'c'), 0, 0, tiled=True)  17.1 us
    all_to_all x1, blocking collectives, body(): lax.all_to_all(jnp.broadcast_to(sums[None], (near * nx, 1, 128)), ('y', '...  16.5 us
    all_to_all x1, starting transfers between devices, body(): in_z = lax.all_to_all(out_z, 'z', 0, 0, tiled=True)  15.7 us
    all_to_all x1, waiting for transfers between devices, body(): in_near = lax.all_to_all(out_near, ('y', 'c'), 0, 0, tiled=True)  12.9 us
    all_to_all x1, starting transfers between devices, body(): in_near = lax.all_to_all(out_near, ('y', 'c'), 0, 0, tiled=True)  11 us
    all_gather x1, blocking collectives, body(): all_tables = lax.all_gather(table, 'x', axis=0)  10.6 us
    all_gather x1, blocking collectives, body(): all_added = lax.all_gather(added, 'x', axis=0)  9.96 us
  transfers between devices with their start and end apart: 3, of which 3 were waited for; matrix products, arithmetic and copies ran while one was open for 0% of the time, Pallas kernels for 1%

profile of v3, /device:TPU:1, one launch (start us, length us, event | category | flops | bytes accessed | tf_op | source)
XLA Modules:
  0.0 152.6 jit_solution(17975674526710329131)
XLA Ops:
  0.6 0.0 copy-start.15
  0.6 0.0 copy-start
  0.7 0.0 copy-start.1
  0.7 4.7 %shard_map.199 = (f32[16,8,640]{2,1,0:T(8,128)}, s32[1,4096]{1,0:T(1,128)S(1)}, f32[128,128]{1,0:T(8,128)S(1)}) custom-call(f32[4,4096]{1,0:T(4,128)} %dir_ref.5, f32[16,80]{1,0:T(8,128)} %bitcast.86, s32[1,4096]{1,0:T(1,128)} %bitcast.80, s32[1,4096]{1,0:T(1,128)} %bitcast.83), custom_call_target="tpu_custom_call" | custom-call | tf_op jit(solution)/shard_map/pallas_call | solution.py:553
  5.4 15.7 %all-to-all-start.3 = ((f32[16,8,640]{2,1,0:T(8,128)}), f32[16,8,640]{2,1,0:T(8,128)S(1)}, u32[]{:S(2)}, u32[]{:S(2)}) async-start(f32[16,8,640]{2,1,0:T(8,128)} %get-tuple-element.102), calls=%async_computation.3 | async-start | bytes 655360 | tf_op jit(solution)/shard_map/all_to_all | solution.py:558
  21.1 10.6 %all-gather = f32[512,128]{1,0:T(8,128)S(1)} all-gather(f32[128,128]{1,0:T(8,128)S(1)} %get-tuple-element.103), channel_id=2, replica_groups=mesh['y'=4,'z'=16,'c'=2,'x'=4] {'x'}, dimensions={0}, use_global_device_ids=true | all-gather | bytes 327680 | tf_op jit(solution)/shard_map/all_gather | solution.py:559
  31.7 4.6 %all-to-all-done.3.in_ref = f32[16,8,640]{2,1,0:T(8,128)S(1)} async-done(((f32[16,8,640]{2,1,0:T(8,128)}), f32[16,8,640]{2,1,0:T(8,128)S(1)}, u32[]{:S(2)}, u32[]{:S(2)}) %all-to-all-start.3) | async-done | bytes 327712 | tf_op jit(solution)/shard_map/all_to_all | solution.py:558
  36.3 0.0 copy-start.13
  36.3 1.0 shard_map.200
  37.4 11.0 %all-to-all-start.4 = ((f32[8,16,1664]{2,1,0:T(8,128)}), f32[8,16,1664]{2,1,0:T(8,128)S(1)}, u32[]{:S(2)}, u32[]{:S(2)}) async-start(f32[8,16,1664]{2,1,0:T(8,128)} %shard_map.200), calls=%async_computation.4 | async-start | bytes 1703936 | tf_op jit(solution)/shard_map/all_to_all | solution.py:565
  48.4 0.0 copy-done.15
  48.4 0.1 broadcast_select_fusion.4.gw_ref
  48.4 12.9 %all-to-all-done.4.in_ref = f32[8,16,1664]{2,1,0:T(8,128)S(1)} async-done(((f32[8,16,1664]{2,1,0:T(8,128)}), f32[8,16,1664]{2,1,0:T(8,128)S(1)}, u32[]{:S(2)}, u32[]{:S(2)}) %all-to-all-start.4) | async-done | bytes 852000 | tf_op jit(solution)/shard_map/all_to_all | solution.py:565
  61.3 0.0 copy-done
  61.3 0.0 copy-done.1
  61.3 2.3 %shard_map.201 = (f32[4,8,128]{2,1,0:T(8,128)S(1)}, f32[128,128]{1,0:T(8,128)S(1)}, f32[384,128]{1,0:T(8,128)S(1)}, f32[32,128]{1,0:T(8,128)S(1)}, f32[8,128]{1,0:T(8,128)S(1)}) custom-call(f32[8,16,1664]{2,1,0:T(8,128)S(1)} %all-to-all-done.4.in_ref, bf16[32,10240]{1,0:T(8,128)(2,1)S(1)} %copy-done, f32[1,10240]{1,0:T(1,128)S(1)} %bitcast.69, ...), custom_call_target="tpu_custom_call" | custom-call | tf_op jit(solution)/shard_map/pallas_call | solution.py:567
  63.6 8.0 %all_to_all.52.pred_ref = f32[4,8,128]{2,1,0:T(8,128)S(1)} all-to-all(f32[4,8,128]{2,1,0:T(8,128)S(1)} %get-tuple-element.107), channel_id=1, replica_groups=mesh['y'=4,'z'=16,'c'=2,'x'=4] {'x'}, dimensions={0} | all-to-all | bytes 32768 | tf_op jit(solution)/shard_map/all_to_all | solution.py:572
  71.7 0.0 copy-done.13
  71.7 0.0 copy-start.14
  71.7 0.0 copy-start.5
  71.7 0.0 copy-start.8
  71.7 2.8 %shard_map.202 = (f32[8,16,1536]{2,1,0:T(8,128)S(1)}, f32[128,128]{1,0:T(8,128)S(1)}, f32[16,128]{1,0:T(8,128)S(1)}) custom-call(f32[4,16]{1,0:T(4,128)S(1)} %copy-done.13, f32[4,128,128]{2,1,0:T(8,128)S(1)} %bitcast.75, f32[4,8,128]{2,1,0:T(8,128)S(1)} %all_to_all.52.pred_ref, f32[384,128]{1,0:T(8,128)S(1)} %get-tuple-element.108.ids_ref, ...), custom_call_target="tpu_custom_call" | custom-call | tf_op jit(solution)/shard_map/pallas_call | solution.py:576
  74.5 0.0 copy-start.4
  74.5 0.0 copy-start.6
  74.5 0.0 copy-start.7
  74.5 0.0 copy-start.9
  74.5 0.0 copy-start.10
  74.5 0.0 copy-start.11
  74.6 0.0 copy-start.12
  74.6 17.1 %all_to_all.53.in_ref = f32[8,16,1536]{2,1,0:T(8,128)S(1)} all-to-all(f32[8,16,1536]{2,1,0:T(8,128)S(1)} %get-tuple-element.109), channel_id=1, replica_groups=mesh['y'=4,'z'=16,'c'=2,'x'=4] {'y','c'}, dimensions={0} | all-to-all | bytes 1572864 | tf_op jit(solution)/shard_map/all_to_all | solution.py:582
  91.6 0.8 shard_map.203
  92.5 5.9 %all-to-all-start.7 = ((f32[16,8,512]{2,1,0:T(8,128)}), f32[16,8,512]{2,1,0:T(8,128)S(1)}, u32[]{:S(2)}, u32[]{:S(2)}) async-start(f32[16,8,512]{2,1,0:T(8,128)} %shard_map.203), calls=%async_computation.7 | async-start | bytes 524288 | tf_op jit(solution)/shard_map/all_to_all | solution.py:587
  98.4 0.0 copy-done.14
  98.4 0.1 copy.170.ridge_ref
  98.5 0.5 slice.37
  99.6 0.0 copy-done.5
  99.7 0.0 copy-done.8
  99.7 0.8 shard_map.204.c_ref
  100.5 10.0 %all-gather.1 = f32[512,128]{1,0:T(8,128)S(1)} all-gather(f32[128,128]{1,0:T(8,128)S(1)} %get-tuple-element.114), channel_id=3, replica_groups=mesh['y'=4,'z'=16,'c'=2,'x'=4] {'x'}, dimensions={0}, use_global_device_ids=true | all-gather | bytes 327680 | tf_op jit(solution)/shard_map/all_gather | solution.py:588
  110.5 0.9 all-to-all-done.7.got_ref
  111.3 0.0 copy-done.4
  111.3 0.0 copy-done.6
  111.3 0.0 copy-done.7
  111.3 0.0 copy-done.9
  111.4 0.0 copy-done.10
  111.4 0.0 copy-done.11
  111.4 0.0 copy-done.12
  111.4 3.2 %shard_map.205 = (f32[4,4096]{1,0:T(4,128)}, f32[16,80]{1,0:T(8,128)S(1)}, f32[1,128]{1,0:T(1,128)S(1)}) custom-call(f32[4,16]{1,0:T(4,128)S(1)} %copy-done.13, f32[16,8,512]{2,1,0:T(8,128)S(1)} %all-to-all-done.7.got_ref, f32[4,4096]{1,0:T(4,128)S(1)} %shard_map.204.c_ref, s32[1,4096]{1,0:T(1,128)S(1)} %get-tuple-element.113.rank_ref, ...), custom_call_target="tpu_custom_call" | custom-call | tf_op jit(solution)/shard_map/pallas_call | solution.py:592
  114.6 0.0 copy-start.2
  114.6 0.0 copy-start.3
  114.6 16.5 %all_to_all.54 = f32[32,1,128]{2,1,0:T(1,128)S(1)} all-to-all(f32[32,1,128]{2,1,0:T(1,128)S(1)} %broadcast_in_dim.140), channel_id=1, replica_groups=mesh['y'=4,'z'=16,'c'=2,'x'=4] {'y','c','x'}, dimensions={0} | all-to-all | bytes 32768 | tf_op jit(solution)/shard_map/all_to_all | solution.py:617
  131.2 19.7 %all_to_all.55.sums_ref = f32[16,1,128]{2,1,0:T(1,128)S(1)} all-to-all(f32[16,1,128]{2,1,0:T(1,128)S(1)} %broadcast_in_dim.141), channel_id=1, replica_groups=mesh['y'=4,'z'=16,'c'=2,'x'=4] {'z'}, dimensions={0} | all-to-all | bytes 16384 | tf_op jit(solution)/shard_map/all_to_all | solution.py:621
  150.9 0.0 copy-done.2
  150.9 0.0 copy-done.3
  150.9 1.7 %shard_map.206 = (f32[4,4096]{1,0:T(4,128)}, f32[4,4096]{1,0:T(4,128)}, f32[4,4096]{1,0:T(4,128)}, f32[16,80]{1,0:T(8,128)}, f32[16,80]{1,0:T(8,128)}, /*index=5*/f32[16,80]{1,0:T(8,128)}) custom-call(f32[16,1,128]{2,1,0:T(1,128)S(1)} %all_to_all.55.sums_ref, f32[4,4096]{1,0:T(4,128)S(1)} %copy-done.2, f32[4,4096]{1,0:T(4,128)S(1)} %copy-done.6, ...), custom_call_target="tpu_custom_call" | custom-call | tf_op jit(solution)/shard_map/pallas_call | solution.py:624
  (6 shorter events, 0.1 us)
Async XLA Ops:
  0.6 47.7 %copy-start.15 = (f32[4]{0:T(128)S(1)}, f32[4]{0:T(128)}, u32[]{:S(2)}) copy-start(f32[4]{0:T(128)} %param.31) | copy-start | bytes 52
  0.6 60.7 %copy-start = (bf16[32,10240]{1,0:T(8,128)(2,1)S(1)}, bf16[32,10240]{1,0:T(8,128)(2,1)}, u32[]{:S(2)}) copy-start(bf16[32,10240]{1,0:T(8,128)(2,1)} %geno_ref.3) | copy-start | bytes 1966084
  0.7 60.7 %copy-start.1 = (f32[10240]{0:T(1024)S(1)}, f32[10240]{0:T(1024)}, u32[]{:S(2)}) copy-start(f32[10240]{0:T(1024)} %param.30) | copy-start | bytes 122884
  5.4 31.0 %all-to-all-start.3 = ((f32[16,8,640]{2,1,0:T(8,128)}), f32[16,8,640]{2,1,0:T(8,128)S(1)}, u32[]{:S(2)}, u32[]{:S(2)}) async-start(f32[16,8,640]{2,1,0:T(8,128)} %get-tuple-element.102), calls=%async_computation.3 | async-start | bytes 655360 | tf_op jit(solution)/shard_map/all_to_all | solution.py:558
  36.3 35.3 %copy-start.13 = (f32[4,16]{1,0:T(4,128)S(1)}, f32[4,16]{1,0:T(4,128)}, u32[]{:S(2)}) copy-start(f32[4,16]{1,0:T(4,128)} %mix_ref.3) | copy-start | bytes 772
  37.4 24.0 %all-to-all-start.4 = ((f32[8,16,1664]{2,1,0:T(8,128)}), f32[8,16,1664]{2,1,0:T(8,128)S(1)}, u32[]{:S(2)}, u32[]{:S(2)}) async-start(f32[8,16,1664]{2,1,0:T(8,128)} %shard_map.200), calls=%async_computation.4 | async-start | bytes 1703936 | tf_op jit(solution)/shard_map/all_to_all | solution.py:565
  71.7 26.7 %copy-start.14 = (f32[16]{0:T(128)S(1)}, f32[16]{0:T(128)}, u32[]{:S(2)}) copy-start(f32[16]{0:T(128)} %param.32) | copy-start | bytes 196
  71.7 28.0 %copy-start.5 = (s32[4096]{0:T(1024)S(1)}, s32[4096]{0:T(1024)}, u32[]{:S(2)}) copy-start(s32[4096]{0:T(1024)} %param.34) | copy-start | bytes 49156
  71.7 28.0 %copy-start.8 = (s32[4096]{0:T(1024)S(1)}, s32[4096]{0:T(1024)}, u32[]{:S(2)}) copy-start(s32[4096]{0:T(1024)} %param.35) | copy-start | bytes 49156
  74.5 36.9 %copy-start.4 = (f32[4,4096]{1,0:T(4,128)S(1)}, f32[4,4096]{1,0:T(4,128)}, u32[]{:S(2)}) copy-start(f32[4,4096]{1,0:T(4,128)} %dir_ref.5) | copy-start | bytes 196612
  74.5 36.8 %copy-start.6 = (f32[4,4096]{1,0:T(4,128)S(1)}, f32[4,4096]{1,0:T(4,128)}, u32[]{:S(2)}) copy-start(f32[4,4096]{1,0:T(4,128)} %res_ref.3) | copy-start | bytes 196612
  74.5 36.8 %copy-start.7 = (f32[4,4096]{1,0:T(4,128)S(1)}, f32[4,4096]{1,0:T(4,128)}, u32[]{:S(2)}) copy-start(f32[4,4096]{1,0:T(4,128)} %inv_ref.3) | copy-start | bytes 196612
  74.5 36.8 %copy-start.9 = (f32[4,4096]{1,0:T(4,128)S(1)}, f32[4,4096]{1,0:T(4,128)}, u32[]{:S(2)}) copy-start(f32[4,4096]{1,0:T(4,128)} %rec_ref.1) | copy-start | bytes 196612
  74.5 36.8 %copy-start.10 = (f32[16,1,80]{2,1,0:T(1,128)S(1)}, f32[16,1,80]{2,1,0:T(1,128)}, u32[]{:S(2)}) copy-start(f32[16,1,80]{2,1,0:T(1,128)} %param.27) | copy-start | bytes 15364
  74.5 36.8 %copy-start.11 = (f32[16,1,80]{2,1,0:T(1,128)S(1)}, f32[16,1,80]{2,1,0:T(1,128)}, u32[]{:S(2)}) copy-start(f32[16,1,80]{2,1,0:T(1,128)} %param.26) | copy-start | bytes 15364
  74.6 36.8 %copy-start.12 = (f32[16,1,80]{2,1,0:T(1,128)S(1)}, f32[16,1,80]{2,1,0:T(1,128)}, u32[]{:S(2)}) copy-start(f32[16,1,80]{2,1,0:T(1,128)} %param.28) | copy-start | bytes 15364
  92.5 18.9 %all-to-all-start.7 = ((f32[16,8,512]{2,1,0:T(8,128)}), f32[16,8,512]{2,1,0:T(8,128)S(1)}, u32[]{:S(2)}, u32[]{:S(2)}) async-start(f32[16,8,512]{2,1,0:T(8,128)} %shard_map.203), calls=%async_computation.7 | async-start | bytes 524288 | tf_op jit(solution)/shard_map/all_to_all | solution.py:587
  114.6 36.3 %copy-start.2 = (f32[4,4096]{1,0:T(4,128)S(1)}, f32[4,4096]{1,0:T(4,128)}, u32[]{:S(2)}) copy-start(f32[4,4096]{1,0:T(4,128)} %sol_ref.1) | copy-start | bytes 196612
  114.6 36.3 %copy-start.3 = (f32[16,1,80]{2,1,0:T(1,128)S(1)}, f32[16,1,80]{2,1,0:T(1,128)}, u32[]{:S(2)}) copy-start(f32[16,1,80]{2,1,0:T(1,128)} %param.25) | copy-start | bytes 15364

commit v4 on v3

--- a/solution.py
+++ b/solution.py
@@ -3,6 +3,7 @@
 
 import jax
 import jax.numpy as jnp
+import numpy as np
 from jax import lax
 from jax.experimental import pallas as pl
 from jax.experimental.pallas import tpu as pltpu
@@ -15,6 +16,7 @@
 HERD = ("y", "z", "c")
 F32 = jnp.float32
 BF16 = jnp.bfloat16
+
 NT = (((1,), (1,)), ((), ()))
 NN = (((1,), (0,)), ((), ()))
 
@@ -24,7 +26,7 @@
         kernel,
         out_shape=out,
         scratch_shapes=list(scratch),
-        compiler_params=pltpu.CompilerParams(vmem_limit_bytes=40 * 2**20),
+        compiler_params=pltpu.CompilerParams(vmem_limit_bytes=20 * 2**20),
         **kw,
     )
 
@@ -56,7 +58,12 @@
 
 
 def one_hot(index, rows):
-    return (rows_at(rows, index.shape[1]) == index).astype(F32).astype(BF16)
+    return jnp.where(counted(rows, index.shape[1]) == index.astype(F32).astype(BF16), jnp.ones((), BF16), jnp.zeros((), BF16))
+
+
+def counted(rows, n):
+    column = rows_at(rows, 128).astype(F32).astype(BF16)
+    return jnp.concatenate([column] * (n // 128), axis=1)
 
 
 def pick(found, in_group, t):
@@ -78,8 +85,9 @@
     return jnp.concatenate([acc_ref[at, :128], acc_ref[at, 128:]], axis=0)
 
 
-def masked(in_group, fields):
-    return jnp.concatenate([jnp.where(in_group, f, 0.0).astype(BF16) for f in fields], axis=0)
+def masked(index, rows, fields):
+    here = counted(rows, index.shape[1]) == index.astype(F32).astype(BF16)
+    return jnp.concatenate([jnp.where(here, f.astype(BF16), jnp.zeros((), BF16)) for f in fields], axis=0)
 
 
 def moved(width, pieces, load, rows):
@@ -110,20 +118,12 @@
     for t in range(traits):
         for b in range(blocks):
             tab_ref[t * blocks + b : t * blocks + b + 1, :] = dir_ref[t : t + 1, b * 128 : (b + 1) * 128]
-    table = side_by_side(tab_ref[...])
     before = (rows_at(n, n) < lax.broadcasted_iota(jnp.int32, (n, n), 1)).astype(F32).astype(BF16)
     acc_ref[...] = jnp.zeros(acc_ref.shape, F32)
-    short = CAP // 2
 
     def step(k, carry):
         at = pl.ds(pl.multiple_of(k * n, n), n)
         sire = sire_ref[:, at]
-        dam = dam_ref[:, at]
-        weight = weights(sire, dam)
-        local_dam = dam & (animals - 1)
-        found = look_up(table, local_dam & 127, 128)
-        in_block = rows_at(blocks, n) == jnp.where(dam >= 0, local_dam >> 7, -1)
-        own = dir_ref[:, at]
         row = owner_row(sire, animals, shape)
         is_owner = rows_at(herd, n) == row
         owners = is_owner.astype(F32).astype(BF16)
@@ -132,105 +132,142 @@
         rank = jnp.where((sire >= 0) & (rank < LIST), rank, -1)
         rank_ref[:, at] = rank
         local = (sire & (animals - 1)) + 1
-        fields = [(local & ~63).astype(F32), (local & 63).astype(F32), weight * 1.5]
-        for t in range(traits):
-            fields += parts(weight * (own[t : t + 1] - 0.5 * pick(found, in_block, t)))
-        in_row = rows_at(short, n) == jnp.where(rank >= 0, rank & (short - 1), -1)
-        target = one_hot((rank >> (short.bit_length() - 1)) * herd + row, 2 * herd)
-        acc_ref[...] += dot(masked(in_row, fields), target, NT)
+        weight = weights(sire, dam_ref[:, at]) * 1.5
+        in_row, target = slot_of(rank, row, herd)
+        fields = masked(in_row, CAP // 2, [(local & ~63).astype(F32), (local & 63).astype(F32), weight])
+        acc_ref[...] += dot(fields, target, NT)
         return earlier[:, n - 1 :] + owners[:, n - 1 :].astype(F32)
 
     count = lax.fori_loop(0, animals // n, step, jnp.zeros((herd, 1), F32), unroll=True)
-    width = (2 + traits) * CAP
     overflow = jnp.where(jnp.max(count, axis=0, keepdims=True) > LIST + 0.5, 1.0, 0.0)
     lane = lax.broadcasted_iota(jnp.int32, (herd, 128), 1)
-
-    def slots(f):
-        at = slice(f * short, (f + 1) * short)
-        return jnp.concatenate([acc_ref[at, :herd], acc_ref[at, herd:]], axis=0)
-
-    lines = [slots(0) + slots(1), slots(2)] + [slots(3 + 2 * t) + slots(4 + 2 * t) for t in range(traits)]
-    for j in range(width // 128):
-        block = jnp.concatenate(lines[2 * j : 2 * j + 2], axis=0).T
-        if j == 0:
-            block = jnp.where(lane == 127, overflow, block)
-        out_ref[:, :, j * 128 : (j + 1) * 128] = block.reshape(nz, ny * nc, 128)
+    ids = slots(acc_ref, 0, herd) + slots(acc_ref, 1, herd)
+    block = jnp.concatenate([ids, slots(acc_ref, 2, herd)], axis=0).T
+    block = jnp.where(lane == 127, overflow, block)
+    out_ref[:, :, :128] = block.reshape(nz, ny * nc, 128)
     rows = ny * nc
     columns = dir_a_ref.shape[1]
     for j in range(dir_a_ref.shape[0] // rows):
         piece = dir_a_ref[j * rows : (j + 1) * rows, :]
         for z in range(nz):
-            out_ref[z, :, width + j * 128 : width + j * 128 + columns] = piece
-
-
-def owner_row(sire, animals, shape):
-    ny, nz, nc = shape
+            out_ref[z, :, 128 + j * 128 : 128 + j * 128 + columns] = piece
+
+
+def slot_of(rank, row, herd):
+    short = CAP // 2
+    return jnp.where(rank >= 0, rank & (short - 1), -1), one_hot((rank >> (short.bit_length() - 1)) * herd + row, 2 * herd)
+
+
+def slots(acc_ref, f, herd):
+    at = slice(f * (CAP // 2), (f + 1) * (CAP // 2))
+    return jnp.concatenate([acc_ref[at, :herd], acc_ref[at, herd:]], axis=0)
+
+
+def owner_parts(sire, animals, shape):
+    _, nz, nc = shape
     owner = sire >> (animals.bit_length() - 1)
     low = nc.bit_length() - 1
     c = owner & (nc - 1)
     z = (owner >> low) & (nz - 1)
     y = owner >> (low + nz.bit_length() - 1)
-    return jnp.where(sire >= 0, z * (ny * nc) + y * nc + c, -1)
+    return y * nc + c, z
+
+
+def owner_row(sire, animals, shape):
+    g, z = owner_parts(sire, animals, shape)
+    return jnp.where(sire >= 0, z * (shape[0] * shape[2]) + g, -1)
+
+
+def mixed(mix_ref, all_ref, t, blocks):
+    total = jnp.zeros((blocks, 128), F32)
+    here = all_ref.shape[1] // blocks
+    for x in range(all_ref.shape[0]):
+        for s in range(here):
+            total = total + mix_ref[t, x * here + s] * all_ref[x, s * blocks : (s + 1) * blocks, :]
+    return total
+
+
+def offspring_kernel(mix_ref, all_ref, sire_ref, dam_ref, rank_ref, tab_ref, c_ref, out_ref, acc_ref, *, shape):
+    ny, nz, nc = shape
+    herd = ny * nz * nc
+    traits, animals = c_ref.shape
+    blocks = animals // 128
+    n = CHUNK
+    for t in range(traits):
+        tab_ref[t * blocks : (t + 1) * blocks, :] = mixed(mix_ref, all_ref, t, blocks)
+    for t in range(traits):
+        for b in range(blocks):
+            c_ref[t : t + 1, b * 128 : (b + 1) * 128] = tab_ref[t * blocks + b : t * blocks + b + 1, :]
+    table = side_by_side(tab_ref[...])
+    acc_ref[...] = jnp.zeros(acc_ref.shape, F32)
+
+    def step(k, _):
+        at = pl.ds(pl.multiple_of(k * n, n), n)
+        sire = sire_ref[:, at]
+        dam = dam_ref[:, at]
+        weight = weights(sire, dam)
+        local = dam & (animals - 1)
+        found = look_up(table, local & 127, 128)
+        in_block = rows_at(blocks, n) == jnp.where(dam >= 0, local >> 7, -1)
+        fields = []
+        for t in range(traits):
+            value = weight * (c_ref[t : t + 1, at] - 0.5 * pick(found, in_block, t))
+            c_ref[t : t + 1, at] = value
+            fields += parts(value)
+        g, z = owner_parts(sire, animals, shape)
+        in_row, target = slot_of(rank_ref[:, at], g * nz + z, herd)
+        acc_ref[...] += dot(masked(in_row, CAP // 2, fields), target, NT)
+        return 0
+
+    lax.fori_loop(0, animals // n, step, 0, unroll=True)
+    lines = [slots(acc_ref, 2 * t, herd) + slots(acc_ref, 2 * t + 1, herd) for t in range(traits)]
+    for j in range(traits * CAP // 128):
+        block = jnp.concatenate(lines[2 * j : 2 * j + 2], axis=0).T
+        out_ref[:, :, j * 128 : (j + 1) * 128] = block.reshape(ny * nc, nz, 128)
 
 
 def forward_kernel(in_ref, out_ref, *, columns, lists):
     nz, near, _ = in_ref.shape
-    traits = out_ref.shape[1]
+    ny, traits, _ = out_ref.shape
+    cores = near // ny
     for g in range(near):
-        out_ref[g, :nz, :lists] = in_ref[:, g, :lists]
+        at = g % cores * lists
+        out_ref[g // cores, :nz, at : at + lists] = in_ref[:, g, :lists]
     pieces = [(z, 0, z * columns, columns) for z in range(nz)]
     for j in range(traits // near):
         first = lists + j * 128
         load = lambda z, _: in_ref[z, :, first : first + 128]
         for k, tile in moved(nz * columns, pieces, load, near):
-            for g in range(near):
-                out_ref[g, j * near : (j + 1) * near, lists + k * 128 : lists + (k + 1) * 128] = tile
-
-
-def gather_kernel(
-    in_ref, geno_ref, freq_ref, gw_ref, out_ref, added_ref, turned_ref, weight_ref, over_ref,
-    joined_ref, acc_ref, wide_ref, *, shape, columns, lists, scale,
+            at = cores * lists + k * 128
+            for y in range(ny):
+                out_ref[y, j * near : (j + 1) * near, at : at + 128] = tile
+
+
+def predict_kernel(
+    core_ref, in_ref, geno_ref, freq_ref, gw_ref, out_ref, lists_ref, turned_ref, over_ref,
+    joined_ref, wide_ref, *, shape, columns, lists, scale,
 ):
     ny, nz, nc = shape
     herd = ny * nz * nc
-    traits = in_ref.shape[1]
-    blocks = weight_ref.shape[0]
-    short = blocks // 2
-    here = added_ref.shape[0] // blocks
+    traits = in_ref.shape[2]
+    here = gw_ref.shape[0]
     genotyped = geno_ref.shape[0]
-    for j in range(lists // 128):
-        at = slice(j * 128, (j + 1) * 128)
-        turned_ref[at, :] = in_ref[:, :nz, at].reshape(herd, 128).T
+    mine = lax.broadcasted_iota(jnp.int32, (nz, lists), 0) * 0 + core_ref[0]
+    for g in range(ny * nc):
+        rows = in_ref[g % nc, g // nc, :nz, :lists]
+        for c in range(1, nc):
+            rows = jnp.where(mine == c, in_ref[g % nc, g // nc, :nz, c * lists : (c + 1) * lists], rows)
+        lists_ref[g] = rows
+    turned_ref[...] = lists_ref[...].reshape(herd, lists).T
     over_ref[...] = jnp.broadcast_to(jnp.max(turned_ref[127:128, :], keepdims=True), over_ref.shape)
-    acc_ref[...] = jnp.zeros(acc_ref.shape, F32)
-    group = 8
-
-    def step(k, _):
-        r = pl.multiple_of(k * group, group)
-        place = flat(turned_ref, r, group).astype(jnp.int32) - 1
-        row, column = place_in(place, place >= 0)
-        fields = [flat(turned_ref, CAP + r, group)]
-        for t in range(here):
-            fields += parts(flat(turned_ref, (2 + t) * CAP + r, group))
-        acc_ref[...] += dot(masked(rows_at(short, group * herd) == row, fields), one_hot(column, 256), NT)
-        return 0
-
-    lax.fori_loop(0, CAP // group, step, 0, unroll=True)
-    weight_ref[...] = both_halves(acc_ref, 0, short) * (0.25 / 1.5)
-    for t in range(here):
-        first = (1 + 2 * t) * short
-        added_ref[t * blocks : (t + 1) * blocks, :] = both_halves(acc_ref, first, short) + both_halves(
-            acc_ref, first + short, short
-        )
-
     width = nz * nc * columns
     total = jnp.zeros((3 * traits, genotyped), F32)
     bias = jnp.zeros((traits, 1), F32)
     for y in range(ny):
         pieces = [
-            (y * nc + c, z * columns, (z * nc + c) * columns, columns) for z in range(nz) for c in range(nc)
+            (c, z * columns, (z * nc + c) * columns, columns) for z in range(nz) for c in range(nc)
         ]
-        load = lambda g, k: in_ref[g, :, lists + k * 128 : lists + (k + 1) * 128]
+        load = lambda c, k: in_ref[c, y, :, nc * lists + k * 128 : nc * lists + (k + 1) * 128]
         for k, tile in moved(width, pieces, load, traits):
             joined_ref[:, k * 128 : (k + 1) * 128] = tile
         at = slice(y * width, (y + 1) * width)
@@ -259,18 +296,9 @@
     return jnp.concatenate([tile[j : j + 1] for j in range(group)], axis=1)
 
 
-def mixed(mix_ref, all_ref, t, blocks):
-    total = jnp.zeros((blocks, 128), F32)
-    here = all_ref.shape[1] // blocks
-    for x in range(all_ref.shape[0]):
-        for s in range(here):
-            total = total + mix_ref[t, x * here + s] * all_ref[x, s * blocks : (s + 1) * blocks, :]
-    return total
-
-
 def reply_kernel(
-    mix_ref, all_ref, pred_ref, ids_ref, geno_ref, freq_ref,
-    out_ref, tab_ref, resid_ref, vals_ref, summed_ref, *, shape, columns, scale,
+    tab_ref, add_ref, all_ref, pred_ref, ids_ref, geno_ref, freq_ref,
+    out_ref, resid_ref, vals_ref, summed_ref, *, shape, columns, scale,
 ):
     ny, nz, nc = shape
     herd = ny * nz * nc
@@ -280,9 +308,6 @@
     blocks = 32
     here = half // blocks
     genotyped = geno_ref.shape[0]
-    for t in range(here):
-        tab_ref[t * blocks : (t + 1) * blocks, :] = mixed(mix_ref, all_ref, t, blocks)
-
     table = side_by_side(tab_ref[...])
     group = 8
 
@@ -303,6 +328,8 @@
     for j in range(values // 128):
         at = slice(j * 128, (j + 1) * 128)
         out_ref[:, :nz, at] = vals_ref[at, :].T.reshape(ny * nc, nz, 128)
+    out_ref[:, :nz, values : 2 * values] = add_ref[...]
+    values = 2 * values
 
     total = pred_ref[0]
     for x in range(1, nx):
@@ -349,33 +376,17 @@
                 out_ref[z, :, first : first + 128] = tile[j * near : (j + 1) * near]
 
 
-def dams_kernel(tab_ref, sire_ref, dam_ref, out_ref):
-    traits, animals = out_ref.shape
-    blocks = animals // 128
-    n = CHUNK
-    for t in range(traits):
-        for b in range(blocks):
-            out_ref[t : t + 1, b * 128 : (b + 1) * 128] = tab_ref[t * blocks + b : t * blocks + b + 1, :]
-    table = side_by_side(tab_ref[...])
-
-    def step(k, _):
-        at = pl.ds(pl.multiple_of(k * n, n), n)
-        dam = dam_ref[:, at]
-        weight = weights(sire_ref[:, at], dam)
-        local = dam & (animals - 1)
-        found = look_up(table, local & 127, 128)
-        in_block = rows_at(blocks, n) == jnp.where(dam >= 0, local >> 7, -1)
-        for t in range(traits):
-            out_ref[t : t + 1, at] = weight * (out_ref[t : t + 1, at] - 0.5 * pick(found, in_block, t))
-        return 0
-
-    lax.fori_loop(0, animals // n, step, 0, unroll=True)
+def order_kernel(in_ref, out_ref, swapped_ref):
+    near, nz, lists = in_ref.shape
+    for g in range(near):
+        swapped_ref[:, g, :] = in_ref[g]
+    out_ref[...] = swapped_ref[...].reshape(near * nz, lists).T
 
 
 def image_kernel(
-    mix_ref, got_ref, c_ref, rank_ref, sire_ref, dam_ref, added_ref, weight_ref, mixed_ref, resid_ref,
+    got_ref, c_ref, rank_ref, sire_ref, dam_ref, lists_ref, mixed_ref, resid_ref,
     dir_ref, rec_ref, res_ref, inv_ref, ridge_ref, dir_a_ref, res_a_ref, inv_a_ref,
-    image_ref, image_a_ref, sums_ref, acc_ref, tab_ref, *, shape,
+    image_ref, image_a_ref, sums_ref, acc_ref, tab_ref, turned_ref, weight_ref, *, shape,
 ):
     traits, animals = c_ref.shape
     ny, nz, nc = shape
@@ -385,7 +396,27 @@
     short = blocks // 2
     wide = traits * CAP
     table = side_by_side(got_ref[:, :, :wide].reshape(herd, wide).T)
+    for j in range(wide // 128):
+        first = wide + j * 128
+        turned_ref[j * 128 : (j + 1) * 128, :] = got_ref[:, :, first : first + 128].reshape(herd, 128).T
     acc_ref[...] = jnp.zeros(acc_ref.shape, F32)
+    weight_ref[...] = jnp.zeros(weight_ref.shape, F32)
+    group = 8
+
+    def add(k, _):
+        r = pl.multiple_of(k * group, group)
+        place = flat(lists_ref, r, group).astype(jnp.int32) - 1
+        row, column = place_in(place, place >= 0)
+        fields = []
+        for t in range(traits):
+            fields += parts(flat(turned_ref, t * CAP + r, group))
+        fields = masked(row, short, fields + [flat(lists_ref, CAP + r, group)])
+        sums = dot(fields, one_hot(column, 256), NT)
+        acc_ref[...] += sums[: 2 * traits * short]
+        weight_ref[...] += sums[2 * traits * short :]
+        return 0
+
+    lax.fori_loop(0, CAP // group, add, 0, unroll=True)
 
     def step(k, _):
         at = pl.ds(pl.multiple_of(k * n, n), n)
@@ -400,7 +431,7 @@
             scaled = c_ref[t : t + 1, at] - 0.5 * weight * pick(found, in_slot, t)
             image_ref[t : t + 1, at] = scaled
             fields += parts(scaled)
-        acc_ref[...] += dot(masked(rows_at(short, n) == row, fields), one_hot(column, 256), NT)
+        acc_ref[...] += dot(masked(row, short, fields), one_hot(column, 256), NT)
         return 0
 
     lax.fori_loop(0, animals // n, step, 0, unroll=True)
@@ -408,8 +439,7 @@
         at = slice(t * blocks, (t + 1) * blocks)
         first = 2 * t * short
         down = both_halves(acc_ref, first, short) + both_halves(acc_ref, first + short, short)
-        down = down + mixed(mix_ref, added_ref, t, blocks)
-        tab_ref[at, :] = weight_ref[...] * mixed_ref[at, :] - 0.5 * down
+        tab_ref[at, :] = (0.25 / 1.5) * both_halves(weight_ref, 0, short) * mixed_ref[at, :] - 0.5 * down
     for b in range(blocks):
         for t in range(traits):
             at = (slice(t, t + 1), slice(b * 128, (b + 1) * 128))
@@ -421,7 +451,7 @@
     res = res_ref[...]
     inv = inv_ref[...]
     columns = dir_a_ref.shape[1]
-    sums = jnp.sum(got_ref[:, :, wide:], axis=0)
+    sums = jnp.sum(got_ref[:, :, 2 * wide :], axis=0)
     tiles = sums.shape[1] // 128
     back = jnp.concatenate([sums[:, j * 128 : (j + 1) * 128] for j in range(tiles)], axis=0)[:, :columns]
     dir_a = dir_a_ref[...]
@@ -532,14 +562,13 @@
     shape = ny, nz, nc = tuple(lax.axis_size(a) for a in HERD)
     nx = lax.axis_size("x")
     herd, near = ny * nz * nc, ny * nc
-    herd_index = lax.axis_index(HERD)
     x_index = lax.axis_index("x")
     here, animals = dir_u.shape
     traits, _, columns = dir_a.shape
     genotyped, snps = genotypes.shape
     blocks = animals // 128
     half = here * blocks
-    lists, values = (2 + here) * CAP, here * CAP
+    lists, values = 2 * CAP, here * CAP
     spare = traits // near * 128
     scale = 2.0 / math.sqrt(snps * nx)
     sds = lambda *s: jax.ShapeDtypeStruct(s, F32)
@@ -553,56 +582,83 @@
     out_z, rank, table = call(
         functools.partial(lists_kernel, shape=shape),
         (sds(nz, near, lists + spare), jax.ShapeDtypeStruct((1, animals), jnp.int32), sds(half, 128)),
-        scratch=[vmem((3 + 2 * here) * CAP // 2, 2 * herd)],
+        scratch=[vmem(3 * CAP // 2, 2 * herd)],
     )(dir_u, d_a, sire_row, dam_row)
     in_z = lax.all_to_all(out_z, "z", 0, 0, tiled=True)
     all_tables = lax.all_gather(table, "x", axis=0)
     in_z, all_tables = lax.optimization_barrier((in_z, all_tables))
     out_near = call(
         functools.partial(forward_kernel, columns=columns, lists=lists),
-        sds(near, traits, lists + nz * columns),
+        sds(ny, traits, nc * lists + nz * columns),
     )(in_z)
-    in_near = lax.all_to_all(out_near, ("y", "c"), 0, 0, tiled=True)
-
-    to_x, added, turned, weight_sum, over = call(
-        functools.partial(gather_kernel, shape=shape, columns=columns, lists=lists, scale=scale),
-        (sds(nx, 2 * here, 128), sds(half, 128), sds(lists, herd), sds(blocks, 128), sds(8, 128)),
-        scratch=[vmem(traits, nz * nc * columns), vmem((1 + 2 * here) * blocks // 2, 256), vmem(traits, 128)],
-    )(in_near, genotypes, freq, weight_here)
-    from_x = lax.all_to_all(to_x, "x", 0, 0, tiled=True)
+    out_near, all_tables = lax.optimization_barrier((out_near, all_tables))
+    in_y = lax.all_to_all(out_near, "y", 0, 0, tiled=True)
 
     on_chip = pl.BlockSpec(memory_space=pltpu.VMEM)
     scalars = pl.BlockSpec(memory_space=pltpu.SMEM)
-    back_near, mixed_table, resid = call(
+    mixed_table, c_term, add = call(
+        functools.partial(offspring_kernel, shape=shape),
+        (sds(half, 128), sds(here, animals), sds(near, nz, values)),
+        scratch=[vmem(here * CAP, 2 * herd)],
+        in_specs=[scalars] + [on_chip] * 4,
+    )(genetic_inv, all_tables, sire_row, dam_row, rank)
+    in_y, mixed_table, c_term, add = lax.optimization_barrier((in_y, mixed_table, c_term, add))
+    in_near = lax.all_gather(in_y, "c", axis=0)
+
+    to_x, asked, turned, over = call(
+        functools.partial(predict_kernel, shape=shape, columns=columns, lists=lists, scale=scale),
+        (sds(nx, 2 * here, 128), sds(near, nz, lists), sds(lists, herd), sds(8, 128)),
+        scratch=[vmem(traits, nz * nc * columns), vmem(traits, 128)],
+        in_specs=[scalars] + [on_chip] * 4,
+    )(lax.axis_index("c").reshape(1), in_near, genotypes, freq, weight_here)
+    from_x = lax.all_to_all(to_x, "x", 0, 0, tiled=True)
+
+    back_near, resid = call(
         functools.partial(reply_kernel, shape=shape, columns=columns, scale=scale),
-        (sds(near, traits, values + nz * columns), sds(half, 128), sds(traits, 128)),
+        (sds(near, traits, 2 * values + nz * columns), sds(traits, 128)),
         scratch=[vmem(values, herd), vmem(traits, nz * nc * columns)],
-        in_specs=[scalars] + [on_chip] * 5,
-    )(genetic_inv, all_tables, from_x, turned, genotypes, freq)
+    )(mixed_table, add, all_tables, from_x, turned, genotypes, freq)
     got_near = lax.all_to_all(back_near, ("y", "c"), 0, 0, tiled=True)
     back_z = call(
-        functools.partial(backward_kernel, columns=columns, values=values), sds(nz, near, values + spare)
+        functools.partial(backward_kernel, columns=columns, values=2 * values),
+        sds(nz, near, 2 * values + spare),
     )(got_near)
-    back_z, added = lax.optimization_barrier((back_z, added))
+    back_z, asked = lax.optimization_barrier((back_z, asked))
     got_z = lax.all_to_all(back_z, "z", 0, 0, tiled=True)
-    all_added = lax.all_gather(added, "x", axis=0)
-
-    c_term = call(dams_kernel, sds(here, animals))(mixed_table, sire_row, dam_row)
+    ordered = call(order_kernel, sds(lists, herd), scratch=[vmem(nz, near, lists)])(asked)
+    too_long = over[0, 0] > 0.5
+    got_z, ordered, too_long = lax.optimization_barrier((got_z, ordered, too_long))
+
     own_resid = lax.dynamic_slice_in_dim(resid, x_index * here, here, 0)
     image_u, image_a, sums = call(
         functools.partial(image_kernel, shape=shape),
         (sds(here, animals), sds(traits, columns), sds(1, 128)),
-        scratch=[vmem(here * blocks, 256), vmem(half, 128)],
-        in_specs=[scalars] + [on_chip] * 17,
+        scratch=[vmem(here * blocks, 256), vmem(half, 128), vmem(values, herd), vmem(blocks // 2, 256)],
     )(
-        genetic_inv, got_z, c_term, rank, sire_row, dam_row, all_added, weight_sum, mixed_table, own_resid,
+        got_z, c_term, rank, sire_row, dam_row, ordered, mixed_table, own_resid,
         dir_u, rec_weight, res_u, inv_diag_u, snp_ridge[:, None], d_a, r_a, i_a,
     )
 
-    def by_blocks():
+    u, a = sds(here, animals), sds(traits, columns)
+
+    def reduced(sums):
+        close = lax.all_to_all(
+            jnp.broadcast_to(sums[None], (near * nx, 1, 128)), ("y", "c", "x"), 0, 0, tiled=True
+        )
+        close = jnp.sum(close, axis=0, keepdims=True)
+        return lax.all_to_all(jnp.broadcast_to(close, (nz, 1, 128)), "z", 0, 0, tiled=True)
+
+    def finish(image, far):
+        return tuple(
+            call(update_kernel, (u, u, u, a, a, a))(
+                far, sol_u, res_u, dir_u, inv_diag_u, image, s_a, r_a, d_a, i_a, image_a
+            )
+        )
+
+    def by_blocks(_):
         dir_all = all_tables.reshape(traits, animals)
         mixed = jnp.dot(genetic_inv, dir_all, precision=lax.Precision.HIGHEST)
-        image = rec_weight * dir_u + pedigree_by_blocks(mixed, sire, dam, herd, herd_index)
+        image = rec_weight * dir_u + pedigree_by_blocks(mixed, sire, dam, herd, lax.axis_index(HERD))
         image = image.at[:, :genotyped].add(own_resid[:, :genotyped])
         cells = [
             jnp.sum(inv_diag_u * res_u * res_u) + jnp.sum(i_a * r_a * r_a),
@@ -610,21 +666,12 @@
             jnp.sum(inv_diag_u * res_u * image) + jnp.sum(i_a * r_a * image_a),
             jnp.sum(inv_diag_u * image * image) + jnp.sum(i_a * image_a * image_a),
         ]
-        return image, jnp.pad(jnp.stack(cells), (0, 124))[None, :]
-
-    image_u, sums = lax.cond(over[0, 0] > 0.5, by_blocks, lambda: (image_u, sums))
-
-    close = lax.all_to_all(
-        jnp.broadcast_to(sums[None], (near * nx, 1, 128)), ("y", "c", "x"), 0, 0, tiled=True
-    )
-    close = jnp.sum(close, axis=0, keepdims=True)
-    far = lax.all_to_all(jnp.broadcast_to(close, (nz, 1, 128)), "z", 0, 0, tiled=True)
-
-    u, a = sds(here, animals), sds(traits, columns)
-    outs = call(update_kernel, (u, u, u, a, a, a))(
-        far, sol_u, res_u, dir_u, inv_diag_u, image_u, s_a, r_a, d_a, i_a, image_a
-    )
-    return tuple(outs[:3]) + tuple(o[:, None, :] for o in outs[3:])
+        return finish(image, reduced(jnp.pad(jnp.stack(cells), (0, 124))[None, :]))
+
+    far, too_long = lax.optimization_barrier((reduced(sums), too_long))
+    outs = finish(image_u, far)
+    outs = lax.cond(too_long, by_blocks, lambda done: done, outs)
+    return outs[:3] + tuple(o[:, None, :] for o in outs[3:])
 
 
 def solution(mesh):

time: 153 us -> 146 us (0.954)
  blocking collectives: 81.9 us -> 61.3 us
  waiting for transfers between devices: 18.4 us -> 33.5 us
  Pallas kernels: 17.3 us -> 13.8 us
    all_to_all x2 -> x1, blocking collectives: 36.3 us -> 16.3 us  [reduced(): lax.all_to_all(jnp.broadcast_to(sums[None], (near * nx, 1, 128)), ('y', '...]
    all_to_all x1, waiting for transfers between devices: 0.88 us -> 16.7 us  [body(): got_z = lax.all_to_all(back_z, 'z', 0, 0, tiled=True)]
    all_to_all x1, waiting for transfers between devices: 4.63 us -> 1.96 us  [body(): in_z = lax.all_to_all(out_z, 'z', 0, 0, tiled=True)]
    all_to_all x1 -> x2, waiting for transfers between devices: 12.9 us -> 14.9 us  [the longest x1 11.2 us: reduced(): lax.all_to_all(jnp.broadcast_to(close, (nz, 1, 128)), 'z', 0, 0, tiled=True)]
    all_gather x1, blocking collectives: 9.96 us -> 8.25 us  [body(): in_near = lax.all_gather(in_y, 'c', axis=0)]
    all_to_all x1 -> x2, starting transfers between devices: 11 us -> 10.2 us  [the longest x1 6.02 us: reduced(): lax.all_to_all(jnp.broadcast_to(close, (nz, 1, 128)), 'z', 0, 0, tiled=True)]
    pallas_call x4 -> x5, Pallas kernels: 5.59 us -> 5.11 us  [the longest x1 2.46 us: body(): call(functools.partial(offspring_kernel, shape=shape), (sds(half, 128), s...]
  transfers between devices with their start and end apart: 3 -> 4, of which waited for: 3 -> 4; matrix products, arithmetic and copies ran while one was open for 0% -> 0% of each run, Pallas kernels for 1% -> 2%
where the time goes in v4:
time: 146 us; the launch traced here: 145 us
  blocking collectives  61.3 us (42%)
  waiting for transfers between devices  33.5 us (23%)
  starting transfers between devices  33.4 us (23%)
  Pallas kernels  13.8 us (9%)
  between operations  1.53 us (1%)
    all_to_all x1, blocking collectives, body(): got_near = lax.all_to_all(back_near, ('y', 'c'), 0, 0, tiled=True)  18.2 us
    all_to_all x1, waiting for transfers between devices, body(): got_z = lax.all_to_all(back_z, 'z', 0, 0, tiled=True)  16.7 us
    all_to_all x1, blocking collectives, reduced(): lax.all_to_all(jnp.broadcast_to(sums[None], (near * nx, 1, 128)), ('y', '...  16.3 us
    all_to_all x1, starting transfers between devices, body(): in_z = lax.all_to_all(out_z, 'z', 0, 0, tiled=True)  15.7 us
    all_to_all x1, waiting for transfers between devices, reduced(): lax.all_to_all(jnp.broadcast_to(close, (nz, 1, 128)), 'z', 0, 0, tiled=True)  11.2 us
    all_gather x1, blocking collectives, body(): all_tables = lax.all_gather(table, 'x', axis=0)  10.6 us
    all_gather x1, blocking collectives, body(): in_near = lax.all_gather(in_y, 'c', axis=0)  8.25 us
    all_to_all x1, blocking collectives, body(): from_x = lax.all_to_all(to_x, 'x', 0, 0, tiled=True)  8.03 us
  transfers between devices with their start and end apart: 4, of which 4 were waited for; matrix products, arithmetic and copies ran while one was open for 0% of the time, Pallas kernels for 2%

profile of v4, /device:TPU:1, one launch (start us, length us, event | category | flops | bytes accessed | tf_op | source)
XLA Modules:
  0.0 144.9 jit_solution(16888976858877745103)
XLA Ops:
  0.6 0.0 copy-start.6
  0.6 0.0 copy-start.5
  0.7 0.0 copy-start.15
  0.7 0.0 copy-start.13
  0.7 0.0 copy-start
  0.7 0.0 copy-start.1
  0.7 3.2 %shard_map.199 = (f32[16,8,384]{2,1,0:T(8,128)}, s32[1,4096]{1,0:T(1,128)S(1)}, f32[128,128]{1,0:T(8,128)S(1)}) custom-call(f32[4,4096]{1,0:T(4,128)} %dir_ref.5, f32[16,80]{1,0:T(8,128)} %bitcast.81, s32[1,4096]{1,0:T(1,128)} %bitcast.75, s32[1,4096]{1,0:T(1,128)} %bitcast.78), custom_call_target="tpu_custom_call" | custom-call | tf_op jit(solution)/shard_map/pallas_call | solution.py:582
  3.9 15.7 %all-to-all-start.5 = ((f32[16,8,384]{2,1,0:T(8,128)}), f32[16,8,384]{2,1,0:T(8,128)S(1)}, u32[]{:S(2)}, u32[]{:S(2)}) async-start(f32[16,8,384]{2,1,0:T(8,128)} %get-tuple-element.138), calls=%async_computation.5 | async-start | bytes 393216 | tf_op jit(solution)/shard_map/all_to_all | solution.py:587
  19.7 10.6 %all-gather = f32[512,128]{1,0:T(8,128)S(1)} all-gather(f32[128,128]{1,0:T(8,128)S(1)} %get-tuple-element.139), channel_id=2, replica_groups=mesh['y'=4,'z'=16,'c'=2,'x'=4] {'x'}, dimensions={0}, use_global_device_ids=true | all-gather | bytes 327680 | tf_op jit(solution)/shard_map/all_gather | solution.py:588
  30.3 2.0 %all-to-all-done.5.in_ref = f32[16,8,384]{2,1,0:T(8,128)S(1)} async-done(((f32[16,8,384]{2,1,0:T(8,128)}), f32[16,8,384]{2,1,0:T(8,128)S(1)}, u32[]{:S(2)}, u32[]{:S(2)}) %all-to-all-start.5) | async-done | bytes 196640 | tf_op jit(solution)/shard_map/all_to_all | solution.py:587
  32.2 0.9 shard_map.200
  33.1 4.2 %all-to-all-start.6 = ((f32[4,16,1536]{2,1,0:T(8,128)}), f32[4,16,1536]{2,1,0:T(8,128)S(1)}, u32[]{:S(2)}, u32[]{:S(2)}) async-start(f32[4,16,1536]{2,1,0:T(8,128)} %shard_map.200), calls=%async_computation.6 | async-start | bytes 786432 | tf_op jit(solution)/shard_map/all_to_all | solution.py:595
  37.3 0.0 copy-done.15
  37.3 0.1 broadcast_select_fusion.4.gw_ref
  37.4 0.0 copy-done.6
  37.4 0.0 copy-done.5
  37.4 0.0 copy-done.13
  37.4 2.5 %shard_map.201 = (f32[128,128]{1,0:T(8,128)S(1)}, f32[4,4096]{1,0:T(4,128)S(1)}, f32[8,16,256]{2,1,0:T(8,128)S(1)}) custom-call(f32[4,16]{1,0:T(4,128)S(1)} %copy-done.13, f32[4,128,128]{2,1,0:T(8,128)S(1)} %bitcast.69, s32[1,4096]{1,0:T(1,128)S(1)} %bitcast.76, s32[1,4096]{1,0:T(1,128)S(1)} %bitcast.79, s32[1,4096]{1,0:T(1,128)S(1)} %get-tuple-element.144.rank_ref), custom_call_target="tpu_custom_call" | custom-call | tf_op jit(solution)/shard_map/pallas_call | solution.py:599
  39.8 3.7 %all-to-all-done.6 = f32[4,16,1536]{2,1,0:T(8,128)S(1)} async-done(((f32[4,16,1536]{2,1,0:T(8,128)}), f32[4,16,1536]{2,1,0:T(8,128)S(1)}, u32[]{:S(2)}, u32[]{:S(2)}) %all-to-all-start.6) | async-done | bytes 393248 | tf_op jit(solution)/shard_map/all_to_all | solution.py:595
  43.5 8.2 %all-gather.1 = f32[8,16,1536]{2,1,0:T(8,128)S(1)} all-gather(f32[4,16,1536]{2,1,0:T(8,128)S(1)} %all-to-all-done.6), channel_id=3, replica_groups=mesh['y'=4,'z'=16,'c'=2,'x'=4] {'c'}, dimensions={0}, use_global_device_ids=true | all-gather | bytes 1179648 | tf_op jit(solution)/shard_map/all_gather | solution.py:606
  51.8 0.0 copy-done
  51.8 0.0 copy-done.1
  51.8 0.8 shard_map.202
  52.6 8.0 %all_to_all.62.pred_ref = f32[4,8,128]{2,1,0:T(8,128)S(1)} all-to-all(f32[4,8,128]{2,1,0:T(8,128)S(1)} %get-tuple-element.151), channel_id=1, replica_groups=mesh['y'=4,'z'=16,'c'=2,'x'=4] {'x'}, dimensions={0} | all-to-all | bytes 32768 | tf_op jit(solution)/shard_map/all_to_all | solution.py:614
  60.6 1.6 %shard_map.203 = (f32[8,16,1792]{2,1,0:T(8,128)S(1)}, f32[16,128]{1,0:T(8,128)S(1)}) custom-call(f32[128,128]{1,0:T(8,128)S(1)} %get-tuple-element.148.tab_ref.mixed_ref, f32[8,16,256]{2,1,0:T(8,128)S(1)} %get-tuple-element.149.add_ref, f32[4,128,128]{2,1,0:T(8,128)S(1)} %bitcast.70, f32[4,8,128]{2,1,0:T(8,128)S(1)} %all_to_all.62.pred_ref, ...), custom_call_target="tpu_custom_call" | custom-call | tf_op jit(solution)/shard_map/pallas_call | solution.py:616
  62.2 0.0 copy-start.14
  62.2 0.0 copy-start.2
  62.3 0.0 copy-start.3
  62.3 0.0 copy-start.4
  62.3 0.0 copy-start.7
  62.3 0.0 copy-start.9
  62.3 0.0 copy-start.10
  62.3 0.0 copy-start.11
  62.3 18.2 %all_to_all.63.in_ref = f32[8,16,1792]{2,1,0:T(8,128)S(1)} all-to-all(f32[8,16,1792]{2,1,0:T(8,128)S(1)} %get-tuple-element.153), channel_id=1, replica_groups=mesh['y'=4,'z'=16,'c'=2,'x'=4] {'y','c'}, dimensions={0} | all-to-all | bytes 1835008 | tf_op jit(solution)/shard_map/all_to_all | solution.py:621
  80.5 0.0 copy-start.8
  80.5 0.0 copy-start.12
  80.5 0.9 shard_map.204
  81.4 7.4 %all-to-all-start.9 = ((f32[16,8,768]{2,1,0:T(8,128)}), f32[16,8,768]{2,1,0:T(8,128)S(1)}, u32[]{:S(2)}, u32[]{:S(2)}) async-start(f32[16,8,768]{2,1,0:T(8,128)} %shard_map.204), calls=%async_computation.9 | async-start | bytes 786432 | tf_op jit(solution)/shard_map/all_to_all | solution.py:627
  88.8 0.0 copy-done.14
  88.8 0.1 copy.151.ridge_ref
  88.9 0.5 slice.37
  90.1 0.1 shard_map.205.lists_ref
  90.2 16.7 %all-to-all-done.9.got_ref = f32[16,8,768]{2,1,0:T(8,128)S(1)} async-done(((f32[16,8,768]{2,1,0:T(8,128)}), f32[16,8,768]{2,1,0:T(8,128)S(1)}, u32[]{:S(2)}, u32[]{:S(2)}) %all-to-all-start.9) | async-done | bytes 393248 | tf_op jit(solution)/shard_map/all_to_all | solution.py:627
  106.9 0.0 copy-done.2
  106.9 0.0 copy-done.3
  106.9 0.0 copy-done.4
  106.9 0.0 copy-done.7
  106.9 0.0 copy-done.9
  106.9 0.0 copy-done.10
  106.9 0.0 copy-done.11
  106.9 3.0 %shard_map.206 = (f32[4,4096]{1,0:T(4,128)S(1)}, f32[16,80]{1,0:T(8,128)S(1)}, f32[1,128]{1,0:T(1,128)S(1)}) custom-call(f32[16,8,768]{2,1,0:T(8,128)S(1)} %all-to-all-done.9.got_ref, f32[4,4096]{1,0:T(4,128)S(1)} %get-tuple-element.159.c_ref, s32[1,4096]{1,0:T(1,128)S(1)} %get-tuple-element.144.rank_ref, s32[1,4096]{1,0:T(1,128)S(1)} %bitcast.77, ...), custom_call_target="tpu_custom_call" | custom-call | tf_op jit(solution)/shard_map/pallas_call | solution.py:633
  110.0 16.3 %all_to_all.64 = f32[32,1,128]{2,1,0:T(1,128)S(1)} all-to-all(f32[32,1,128]{2,1,0:T(1,128)S(1)} %broadcast_in_dim.161), channel_id=1, replica_groups=mesh['y'=4,'z'=16,'c'=2,'x'=4] {'y','c','x'}, dimensions={0} | all-to-all | bytes 32768 | tf_op jit(solution)/shard_map/all_to_all | solution.py:645
  126.3 0.6 broadcast_in_dim.162
  126.9 6.0 %all-to-all-start.11 = ((f32[16,1,128]{2,1,0:T(1,128)}), f32[16,1,128]{2,1,0:T(1,128)S(1)}, u32[]{:S(2)}, u32[]{:S(2)}) async-start(f32[16,1,128]{2,1,0:T(1,128)} %broadcast_in_dim.162), calls=%async_computation.11 | async-start | bytes 16384 | tf_op jit(solution)/shard_map/all_to_all | solution.py:649
  132.9 11.2 %all-to-all-done.11.sums_ref = f32[16,1,128]{2,1,0:T(1,128)S(1)} async-done(((f32[16,1,128]{2,1,0:T(1,128)}), f32[16,1,128]{2,1,0:T(1,128)S(1)}, u32[]{:S(2)}, u32[]{:S(2)}) %all-to-all-start.11) | async-done | bytes 8224 | tf_op jit(solution)/shard_map/all_to_all | solution.py:649
  144.1 0.0 copy-done.8
  144.1 0.0 copy-done.12
  144.1 0.8 shard_map.207
  (5 shorter events, 0.1 us)
Async XLA Ops:
  0.6 36.7 %copy-start.6 = (s32[4096]{0:T(1024)S(1)}, s32[4096]{0:T(1024)}, u32[]{:S(2)}) copy-start(s32[4096]{0:T(1024)} %param.35) | copy-start | bytes 49156
  0.6 36.7 %copy-start.5 = (s32[4096]{0:T(1024)S(1)}, s32[4096]{0:T(1024)}, u32[]{:S(2)}) copy-start(s32[4096]{0:T(1024)} %param.34) | copy-start | bytes 49156
  0.7 36.6 %copy-start.15 = (f32[4]{0:T(128)S(1)}, f32[4]{0:T(128)}, u32[]{:S(2)}) copy-start(f32[4]{0:T(128)} %param.31) | copy-start | bytes 52
  0.7 36.7 %copy-start.13 = (f32[4,16]{1,0:T(4,128)S(1)}, f32[4,16]{1,0:T(4,128)}, u32[]{:S(2)}) copy-start(f32[4,16]{1,0:T(4,128)} %mix_ref.1) | copy-start | bytes 772
  0.7 51.1 %copy-start = (bf16[32,10240]{1,0:T(8,128)(2,1)S(1)}, bf16[32,10240]{1,0:T(8,128)(2,1)}, u32[]{:S(2)}) copy-start(bf16[32,10240]{1,0:T(8,128)(2,1)} %geno_ref.3) | copy-start | bytes 1966084
  0.7 51.1 %copy-start.1 = (f32[10240]{0:T(1024)S(1)}, f32[10240]{0:T(1024)}, u32[]{:S(2)}) copy-start(f32[10240]{0:T(1024)} %param.30) | copy-start | bytes 122884
  3.9 28.3 %all-to-all-start.5 = ((f32[16,8,384]{2,1,0:T(8,128)}), f32[16,8,384]{2,1,0:T(8,128)S(1)}, u32[]{:S(2)}, u32[]{:S(2)}) async-start(f32[16,8,384]{2,1,0:T(8,128)} %get-tuple-element.138), calls=%async_computation.5 | async-start | bytes 393216 | tf_op jit(solution)/shard_map/all_to_all | solution.py:587
  33.1 10.4 %all-to-all-start.6 = ((f32[4,16,1536]{2,1,0:T(8,128)}), f32[4,16,1536]{2,1,0:T(8,128)S(1)}, u32[]{:S(2)}, u32[]{:S(2)}) async-start(f32[4,16,1536]{2,1,0:T(8,128)} %shard_map.200), calls=%async_computation.6 | async-start | bytes 786432 | tf_op jit(solution)/shard_map/all_to_all | solution.py:595
  62.2 26.6 %copy-start.14 = (f32[16]{0:T(128)S(1)}, f32[16]{0:T(128)}, u32[]{:S(2)}) copy-start(f32[16]{0:T(128)} %param.32) | copy-start | bytes 196
  62.2 44.6 %copy-start.2 = (f32[4,4096]{1,0:T(4,128)S(1)}, f32[4,4096]{1,0:T(4,128)}, u32[]{:S(2)}) copy-start(f32[4,4096]{1,0:T(4,128)} %dir_ref.5) | copy-start | bytes 196612
  62.3 44.6 %copy-start.3 = (f32[4,4096]{1,0:T(4,128)S(1)}, f32[4,4096]{1,0:T(4,128)}, u32[]{:S(2)}) copy-start(f32[4,4096]{1,0:T(4,128)} %res_ref.3) | copy-start | bytes 196612
  62.3 44.6 %copy-start.4 = (f32[4,4096]{1,0:T(4,128)S(1)}, f32[4,4096]{1,0:T(4,128)}, u32[]{:S(2)}) copy-start(f32[4,4096]{1,0:T(4,128)} %inv_ref.3) | copy-start | bytes 196612
  62.3 44.6 %copy-start.7 = (f32[4,4096]{1,0:T(4,128)S(1)}, f32[4,4096]{1,0:T(4,128)}, u32[]{:S(2)}) copy-start(f32[4,4096]{1,0:T(4,128)} %rec_ref.1) | copy-start | bytes 196612
  62.3 44.6 %copy-start.9 = (f32[16,1,80]{2,1,0:T(1,128)S(1)}, f32[16,1,80]{2,1,0:T(1,128)}, u32[]{:S(2)}) copy-start(f32[16,1,80]{2,1,0:T(1,128)} %param.27) | copy-start | bytes 15364
  62.3 44.6 %copy-start.10 = (f32[16,1,80]{2,1,0:T(1,128)S(1)}, f32[16,1,80]{2,1,0:T(1,128)}, u32[]{:S(2)}) copy-start(f32[16,1,80]{2,1,0:T(1,128)} %param.26) | copy-start | bytes 15364
  62.3 44.6 %copy-start.11 = (f32[16,1,80]{2,1,0:T(1,128)S(1)}, f32[16,1,80]{2,1,0:T(1,128)}, u32[]{:S(2)}) copy-start(f32[16,1,80]{2,1,0:T(1,128)} %param.28) | copy-start | bytes 15364
  80.5 63.6 %copy-start.8 = (f32[4,4096]{1,0:T(4,128)S(1)}, f32[4,4096]{1,0:T(4,128)}, u32[]{:S(2)}) copy-start(f32[4,4096]{1,0:T(4,128)} %sol_ref.1) | copy-start | bytes 196612
  80.5 63.6 %copy-start.12 = (f32[16,1,80]{2,1,0:T(1,128)S(1)}, f32[16,1,80]{2,1,0:T(1,128)}, u32[]{:S(2)}) copy-start(f32[16,1,80]{2,1,0:T(1,128)} %param.25) | copy-start | bytes 15364
  81.4 25.5 %all-to-all-start.9 = ((f32[16,8,768]{2,1,0:T(8,128)}), f32[16,8,768]{2,1,0:T(8,128)S(1)}, u32[]{:S(2)}, u32[]{:S(2)}) async-start(f32[16,8,768]{2,1,0:T(8,128)} %shard_map.204), calls=%async_computation.9 | async-start | bytes 786432 | tf_op jit(solution)/shard_map/all_to_all | solution.py:627
  126.9 17.2 %all-to-all-start.11 = ((f32[16,1,128]{2,1,0:T(1,128)}), f32[16,1,128]{2,1,0:T(1,128)S(1)}, u32[]{:S(2)}, u32[]{:S(2)}) async-start(f32[16,1,128]{2,1,0:T(1,128)} %broadcast_in_dim.162), calls=%async_computation.11 | async-start | bytes 16384 | tf_op jit(solution)/shard_map/all_to_all | solution.py:649

commit v5 on v4

--- a/solution.py
+++ b/solution.py
@@ -585,13 +585,21 @@
         scratch=[vmem(3 * CAP // 2, 2 * herd)],
     )(dir_u, d_a, sire_row, dam_row)
     in_z = lax.all_to_all(out_z, "z", 0, 0, tiled=True)
-    all_tables = lax.all_gather(table, "x", axis=0)
-    in_z, all_tables = lax.optimization_barrier((in_z, all_tables))
+    from_others = [
+        lax.ppermute(table, "x", [(i, (i + k) % nx) for i in range(nx)]) for k in range(1, nx)
+    ]
     out_near = call(
         functools.partial(forward_kernel, columns=columns, lists=lists),
         sds(ny, traits, nc * lists + nz * columns),
     )(in_z)
-    out_near, all_tables = lax.optimization_barrier((out_near, all_tables))
+    out_near, place = lax.optimization_barrier((out_near, x_index))
+    all_tables = []
+    for j in range(nx):
+        chosen = table
+        for k in range(1, nx):
+            chosen = jnp.where(place == (j + k) % nx, from_others[k - 1], chosen)
+        all_tables.append(chosen)
+    all_tables = jnp.stack(all_tables)
     in_y = lax.all_to_all(out_near, "y", 0, 0, tiled=True)
 
     on_chip = pl.BlockSpec(memory_space=pltpu.VMEM)

time: 146 us -> 144 us (0.986)
  blocking collectives: 61.3 us -> 50.7 us
  starting transfers between devices: 33.4 us -> 42.3 us
    all_gather x1 -> x0, blocking collectives: 10.6 us -> none  [body(): all_tables = lax.all_gather(table, 'x', axis=0)]
    ppermute x0 -> x3, starting transfers between devices: none -> 10.5 us  [body(): lax.ppermute(table, 'x', [(i, (i + k) % nx) for i in range(nx)])]
    all_to_all x1, starting transfers between devices: 7.43 us -> 5.7 us  [body(): got_z = lax.all_to_all(back_z, 'z', 0, 0, tiled=True)]
  transfers between devices with their start and end apart: 4 -> 7, of which waited for: 4 -> 4; matrix products, arithmetic and copies ran while one was open for 0% -> 1% of each run, Pallas kernels for 2% -> 2%
where the time goes in v5:
time: 144 us; the launch traced here: 143 us
  blocking collectives  50.7 us (35%)
  starting transfers between devices  42.3 us (29%)
  waiting for transfers between devices  32.8 us (23%)
  Pallas kernels  13.8 us (10%)
  between operations  1.57 us (1%)
    all_to_all x1, blocking collectives, body(): got_near = lax.all_to_all(back_near, ('y', 'c'), 0, 0, tiled=True)  18.1 us
    all_to_all x1, waiting for transfers between devices, body(): got_z = lax.all_to_all(back_z, 'z', 0, 0, tiled=True)  16.7 us
    all_to_all x1, blocking collectives, reduced(): lax.all_to_all(jnp.broadcast_to(sums[None], (near * nx, 1, 128)), ('y', '...  16.3 us
    all_to_all x1, starting transfers between devices, body(): in_z = lax.all_to_all(out_z, 'z', 0, 0, tiled=True)  15.9 us
    all_to_all x1, waiting for transfers between devices, reduced(): lax.all_to_all(jnp.broadcast_to(close, (nz, 1, 128)), 'z', 0, 0, tiled=True)  11.2 us
    ppermute x3, starting transfers between devices, body(): lax.ppermute(table, 'x', [(i, (i + k) % nx) for i in range(nx)])  10.5 us
    all_gather x1, blocking collectives, body(): in_near = lax.all_gather(in_y, 'c', axis=0)  8.25 us
    all_to_all x1, blocking collectives, body(): from_x = lax.all_to_all(to_x, 'x', 0, 0, tiled=True)  8.03 us
  transfers between devices with their start and end apart: 7, of which 4 were waited for; matrix products, arithmetic and copies ran while one was open for 1% of the time, Pallas kernels for 2%

profile of v5, /device:TPU:1, one launch (start us, length us, event | category | flops | bytes accessed | tf_op | source)
XLA Modules:
  0.0 143.2 jit_solution(1075283750906589758)
XLA Ops:
  0.6 0.0 copy-start.6
  0.6 0.0 copy-start.5
  0.7 0.0 copy-start.13
  0.7 3.2 %shard_map.199 = (f32[16,8,384]{2,1,0:T(8,128)}, s32[1,4096]{1,0:T(1,128)S(1)}, f32[128,128]{1,0:T(8,128)S(1)}) custom-call(f32[4,4096]{1,0:T(4,128)} %dir_ref.5, f32[16,80]{1,0:T(8,128)} %bitcast.85, s32[1,4096]{1,0:T(1,128)} %bitcast.79, s32[1,4096]{1,0:T(1,128)} %bitcast.82), custom_call_target="tpu_custom_call" | custom-call | tf_op jit(solution)/shard_map/pallas_call | solution.py:582
  3.8 0.0 copy-start
  3.8 0.0 copy-start.1
  3.9 15.9 %all-to-all-start.5 = ((f32[16,8,384]{2,1,0:T(8,128)}), f32[16,8,384]{2,1,0:T(8,128)S(1)}, u32[]{:S(2)}, u32[]{:S(2)}) async-start(f32[16,8,384]{2,1,0:T(8,128)} %get-tuple-element.136), calls=%async_computation.5 | async-start | bytes 393216 | tf_op jit(solution)/shard_map/all_to_all | solution.py:587
  19.7 3.1 %collective-permute-start.2 = (f32[128,128]{1,0:T(8,128)S(1)}, f32[128,128]{1,0:T(8,128)S(1)}, u32[]{:S(2)}, u32[]{:S(2)}) collective-permute-start(f32[128,128]{1,0:T(8,128)S(1)} %get-tuple-element.139), channel_id=1, source_target_pairs={{0,1},{1,2},{2,3},{3,0},{4,5},{5,6},{6,7},{7,4},{8,9},{9,10},{10,1... | collective-permute-start | bytes 196616 | tf_op jit(solution)/shard_map/ppermute | solution.py:589
  22.9 4.4 %collective-permute-start.1 = (f32[128,128]{1,0:T(8,128)S(1)}, f32[128,128]{1,0:T(8,128)S(1)}, u32[]{:S(2)}, u32[]{:S(2)}) collective-permute-start(f32[128,128]{1,0:T(8,128)S(1)} %get-tuple-element.139), channel_id=1, source_target_pairs={{0,2},{1,3},{2,0},{3,1},{4,6},{5,7},{6,4},{7,5},{8,10},{9,11},{10,... | collective-permute-start | bytes 196616 | tf_op jit(solution)/shard_map/ppermute | solution.py:589
  27.2 3.1 %collective-permute-start = (f32[128,128]{1,0:T(8,128)S(1)}, f32[128,128]{1,0:T(8,128)S(1)}, u32[]{:S(2)}, u32[]{:S(2)}) collective-permute-start(f32[128,128]{1,0:T(8,128)S(1)} %get-tuple-element.139), channel_id=1, source_target_pairs={{0,3},{1,0},{2,1},{3,2},{4,7},{5,4},{6,5},{7,6},{8,11},{9,8},{10,9... | collective-permute-start | bytes 196616 | tf_op jit(solution)/shard_map/ppermute | solution.py:589
  30.3 0.7 broadcast_select_fusion.4.gw_ref
  31.0 1.2 all-to-all-done.5.in_ref
  32.3 0.9 shard_map.200
  33.1 4.2 %all-to-all-start.6 = ((f32[4,16,1536]{2,1,0:T(8,128)}), f32[4,16,1536]{2,1,0:T(8,128)S(1)}, u32[]{:S(2)}, u32[]{:S(2)}) async-start(f32[4,16,1536]{2,1,0:T(8,128)} %shard_map.200), calls=%async_computation.6 | async-start | bytes 786432 | tf_op jit(solution)/shard_map/all_to_all | solution.py:603
  37.3 0.0 collective-permute-done.2
  37.3 0.0 collective-permute-done.1
  37.3 0.0 collective-permute-done
  37.4 0.0 copy-done.6
  37.4 0.0 copy-done.5
  37.4 0.0 copy-done.13
  37.4 2.5 %shard_map.201 = (f32[128,128]{1,0:T(8,128)S(1)}, f32[4,4096]{1,0:T(4,128)S(1)}, f32[8,16,256]{2,1,0:T(8,128)S(1)}) custom-call(f32[4,16]{1,0:T(4,128)S(1)} %copy-done.13, f32[4,128,128]{2,1,0:T(8,128)S(1)} %pad_maximum_fusion.all_ref, s32[1,4096]{1,0:T(1,128)S(1)} %bitcast.80, s32[1,4096]{1,0:T(1,128)S(1)} %bitcast.83, ...), custom_call_target="tpu_custom_call" | custom-call | tf_op jit(solution)/shard_map/pallas_call | solution.py:607
  39.9 3.6 %all-to-all-done.6 = f32[4,16,1536]{2,1,0:T(8,128)S(1)} async-done(((f32[4,16,1536]{2,1,0:T(8,128)}), f32[4,16,1536]{2,1,0:T(8,128)S(1)}, u32[]{:S(2)}, u32[]{:S(2)}) %all-to-all-start.6) | async-done | bytes 393248 | tf_op jit(solution)/shard_map/all_to_all | solution.py:603
  43.6 8.2 %all-gather = f32[8,16,1536]{2,1,0:T(8,128)S(1)} all-gather(f32[4,16,1536]{2,1,0:T(8,128)S(1)} %all-to-all-done.6), channel_id=2, replica_groups=mesh['y'=4,'z'=16,'c'=2,'x'=4] {'c'}, dimensions={0}, use_global_device_ids=true | all-gather | bytes 1179648 | tf_op jit(solution)/shard_map/all_gather | solution.py:614
  51.8 0.0 copy-done
  51.8 0.0 copy-done.1
  51.8 0.8 shard_map.202
  52.6 8.0 %all_to_all.62.pred_ref = f32[4,8,128]{2,1,0:T(8,128)S(1)} all-to-all(f32[4,8,128]{2,1,0:T(8,128)S(1)} %get-tuple-element.147), channel_id=1, replica_groups=mesh['y'=4,'z'=16,'c'=2,'x'=4] {'x'}, dimensions={0} | all-to-all | bytes 32768 | tf_op jit(solution)/shard_map/all_to_all | solution.py:622
  60.7 1.6 %shard_map.203 = (f32[8,16,1792]{2,1,0:T(8,128)S(1)}, f32[16,128]{1,0:T(8,128)S(1)}) custom-call(f32[128,128]{1,0:T(8,128)S(1)} %get-tuple-element.144.tab_ref.mixed_ref, f32[8,16,256]{2,1,0:T(8,128)S(1)} %get-tuple-element.145.add_ref, f32[4,128,128]{2,1,0:T(8,128)S(1)} %pad_maximum_fusion.all_ref, f32[4,8,128]{2,1,0:T(8,128)S(1)} %all_to_all.62.pred_ref, ...), custom_call_target="tpu_custom_call" | custom-call | tf_op jit(solution)/shard_map/pallas_call | solution.py:624
  62.3 0.0 copy-start.14
  62.3 0.0 copy-start.2
  62.3 0.0 copy-start.3
  62.3 0.0 copy-start.4
  62.4 0.0 copy-start.7
  62.4 0.0 copy-start.9
  62.4 0.0 copy-start.10
  62.4 0.0 copy-start.11
  62.4 18.1 %all_to_all.63.in_ref = f32[8,16,1792]{2,1,0:T(8,128)S(1)} all-to-all(f32[8,16,1792]{2,1,0:T(8,128)S(1)} %get-tuple-element.149), channel_id=1, replica_groups=mesh['y'=4,'z'=16,'c'=2,'x'=4] {'y','c'}, dimensions={0} | all-to-all | bytes 1835008 | tf_op jit(solution)/shard_map/all_to_all | solution.py:629
  80.5 0.0 copy-start.8
  80.5 0.0 copy-start.12
  80.5 0.9 shard_map.204
  81.4 5.7 %all-to-all-start.9 = ((f32[16,8,768]{2,1,0:T(8,128)}), f32[16,8,768]{2,1,0:T(8,128)S(1)}, u32[]{:S(2)}, u32[]{:S(2)}) async-start(f32[16,8,768]{2,1,0:T(8,128)} %shard_map.204), calls=%async_computation.9 | async-start | bytes 786432 | tf_op jit(solution)/shard_map/all_to_all | solution.py:635
  87.1 0.0 copy-done.14
  87.1 0.1 copy.151.ridge_ref
  87.2 0.5 slice.37
  88.4 0.1 shard_map.205.lists_ref
  88.5 16.7 %all-to-all-done.9.got_ref = f32[16,8,768]{2,1,0:T(8,128)S(1)} async-done(((f32[16,8,768]{2,1,0:T(8,128)}), f32[16,8,768]{2,1,0:T(8,128)S(1)}, u32[]{:S(2)}, u32[]{:S(2)}) %all-to-all-start.9) | async-done | bytes 393248 | tf_op jit(solution)/shard_map/all_to_all | solution.py:635
  105.2 0.0 copy-done.2
  105.2 0.0 copy-done.3
  105.2 0.0 copy-done.4
  105.2 0.0 copy-done.7
  105.2 0.0 copy-done.9
  105.2 0.0 copy-done.10
  105.2 0.0 copy-done.11
  105.2 3.0 %shard_map.206 = (f32[4,4096]{1,0:T(4,128)S(1)}, f32[16,80]{1,0:T(8,128)S(1)}, f32[1,128]{1,0:T(1,128)S(1)}) custom-call(f32[16,8,768]{2,1,0:T(8,128)S(1)} %all-to-all-done.9.got_ref, f32[4,4096]{1,0:T(4,128)S(1)} %get-tuple-element.155.c_ref, s32[1,4096]{1,0:T(1,128)S(1)} %get-tuple-element.140.rank_ref, s32[1,4096]{1,0:T(1,128)S(1)} %bitcast.81, ...), custom_call_target="tpu_custom_call" | custom-call | tf_op jit(solution)/shard_map/pallas_call | solution.py:641
  108.3 16.3 %all_to_all.64 = f32[32,1,128]{2,1,0:T(1,128)S(1)} all-to-all(f32[32,1,128]{2,1,0:T(1,128)S(1)} %broadcast_in_dim.161), channel_id=1, replica_groups=mesh['y'=4,'z'=16,'c'=2,'x'=4] {'y','c','x'}, dimensions={0} | all-to-all | bytes 32768 | tf_op jit(solution)/shard_map/all_to_all | solution.py:653
  124.6 0.6 broadcast_in_dim.162
  125.2 6.0 %all-to-all-start.11 = ((f32[16,1,128]{2,1,0:T(1,128)}), f32[16,1,128]{2,1,0:T(1,128)S(1)}, u32[]{:S(2)}, u32[]{:S(2)}) async-start(f32[16,1,128]{2,1,0:T(1,128)} %broadcast_in_dim.162), calls=%async_computation.11 | async-start | bytes 16384 | tf_op jit(solution)/shard_map/all_to_all | solution.py:657
  131.2 11.2 %all-to-all-done.11.sums_ref = f32[16,1,128]{2,1,0:T(1,128)S(1)} async-done(((f32[16,1,128]{2,1,0:T(1,128)}), f32[16,1,128]{2,1,0:T(1,128)S(1)}, u32[]{:S(2)}, u32[]{:S(2)}) %all-to-all-start.11) | async-done | bytes 8224 | tf_op jit(solution)/shard_map/all_to_all | solution.py:657
  142.4 0.0 copy-done.8
  142.4 0.0 copy-done.12
  142.4 0.8 shard_map.207
  (7 shorter events, 0.1 us)
Async XLA Ops:
  0.6 36.8 %copy-start.6 = (s32[4096]{0:T(1024)S(1)}, s32[4096]{0:T(1024)}, u32[]{:S(2)}) copy-start(s32[4096]{0:T(1024)} %param.35) | copy-start | bytes 49156
  0.6 36.8 %copy-start.5 = (s32[4096]{0:T(1024)S(1)}, s32[4096]{0:T(1024)}, u32[]{:S(2)}) copy-start(s32[4096]{0:T(1024)} %param.34) | copy-start | bytes 49156
  0.7 36.8 %copy-start.13 = (f32[4,16]{1,0:T(4,128)S(1)}, f32[4,16]{1,0:T(4,128)}, u32[]{:S(2)}) copy-start(f32[4,16]{1,0:T(4,128)} %mix_ref.1) | copy-start | bytes 772
  3.8 48.0 %copy-start = (bf16[32,10240]{1,0:T(8,128)(2,1)S(1)}, bf16[32,10240]{1,0:T(8,128)(2,1)}, u32[]{:S(2)}) copy-start(bf16[32,10240]{1,0:T(8,128)(2,1)} %geno_ref.3) | copy-start | bytes 1966084
  3.8 48.0 %copy-start.1 = (f32[10240]{0:T(1024)S(1)}, f32[10240]{0:T(1024)}, u32[]{:S(2)}) copy-start(f32[10240]{0:T(1024)} %param.30) | copy-start | bytes 122884
  3.9 28.4 %all-to-all-start.5 = ((f32[16,8,384]{2,1,0:T(8,128)}), f32[16,8,384]{2,1,0:T(8,128)S(1)}, u32[]{:S(2)}, u32[]{:S(2)}) async-start(f32[16,8,384]{2,1,0:T(8,128)} %get-tuple-element.136), calls=%async_computation.5 | async-start | bytes 393216 | tf_op jit(solution)/shard_map/all_to_all | solution.py:587
  19.7 17.6 %collective-permute-start.2 = (f32[128,128]{1,0:T(8,128)S(1)}, f32[128,128]{1,0:T(8,128)S(1)}, u32[]{:S(2)}, u32[]{:S(2)}) collective-permute-start(f32[128,128]{1,0:T(8,128)S(1)} %get-tuple-element.139), channel_id=1, source_target_pairs={{0,1},{1,2},{2,3},{3,0},{4,5},{5,6},{6,7},{7,4},{8,9},{9,10},{10,1... | collective-permute-start | bytes 196616 | tf_op jit(solution)/shard_map/ppermute | solution.py:589
  22.9 14.5 %collective-permute-start.1 = (f32[128,128]{1,0:T(8,128)S(1)}, f32[128,128]{1,0:T(8,128)S(1)}, u32[]{:S(2)}, u32[]{:S(2)}) collective-permute-start(f32[128,128]{1,0:T(8,128)S(1)} %get-tuple-element.139), channel_id=1, source_target_pairs={{0,2},{1,3},{2,0},{3,1},{4,6},{5,7},{6,4},{7,5},{8,10},{9,11},{10,... | collective-permute-start | bytes 196616 | tf_op jit(solution)/shard_map/ppermute | solution.py:589
  27.2 10.1 %collective-permute-start = (f32[128,128]{1,0:T(8,128)S(1)}, f32[128,128]{1,0:T(8,128)S(1)}, u32[]{:S(2)}, u32[]{:S(2)}) collective-permute-start(f32[128,128]{1,0:T(8,128)S(1)} %get-tuple-element.139), channel_id=1, source_target_pairs={{0,3},{1,0},{2,1},{3,2},{4,7},{5,4},{6,5},{7,6},{8,11},{9,8},{10,9... | collective-permute-start | bytes 196616 | tf_op jit(solution)/shard_map/ppermute | solution.py:589
  33.1 10.4 %all-to-all-start.6 = ((f32[4,16,1536]{2,1,0:T(8,128)}), f32[4,16,1536]{2,1,0:T(8,128)S(1)}, u32[]{:S(2)}, u32[]{:S(2)}) async-start(f32[4,16,1536]{2,1,0:T(8,128)} %shard_map.200), calls=%async_computation.6 | async-start | bytes 786432 | tf_op jit(solution)/shard_map/all_to_all | solution.py:603
  62.3 24.8 %copy-start.14 = (f32[16]{0:T(128)S(1)}, f32[16]{0:T(128)}, u32[]{:S(2)}) copy-start(f32[16]{0:T(128)} %param.32) | copy-start | bytes 196
  62.3 42.9 %copy-start.2 = (f32[4,4096]{1,0:T(4,128)S(1)}, f32[4,4096]{1,0:T(4,128)}, u32[]{:S(2)}) copy-start(f32[4,4096]{1,0:T(4,128)} %dir_ref.5) | copy-start | bytes 196612
  62.3 42.9 %copy-start.3 = (f32[4,4096]{1,0:T(4,128)S(1)}, f32[4,4096]{1,0:T(4,128)}, u32[]{:S(2)}) copy-start(f32[4,4096]{1,0:T(4,128)} %res_ref.3) | copy-start | bytes 196612
  62.3 42.8 %copy-start.4 = (f32[4,4096]{1,0:T(4,128)S(1)}, f32[4,4096]{1,0:T(4,128)}, u32[]{:S(2)}) copy-start(f32[4,4096]{1,0:T(4,128)} %inv_ref.3) | copy-start | bytes 196612
  62.4 42.8 %copy-start.7 = (f32[4,4096]{1,0:T(4,128)S(1)}, f32[4,4096]{1,0:T(4,128)}, u32[]{:S(2)}) copy-start(f32[4,4096]{1,0:T(4,128)} %rec_ref.1) | copy-start | bytes 196612
  62.4 42.8 %copy-start.9 = (f32[16,1,80]{2,1,0:T(1,128)S(1)}, f32[16,1,80]{2,1,0:T(1,128)}, u32[]{:S(2)}) copy-start(f32[16,1,80]{2,1,0:T(1,128)} %param.27) | copy-start | bytes 15364
  62.4 42.8 %copy-start.10 = (f32[16,1,80]{2,1,0:T(1,128)S(1)}, f32[16,1,80]{2,1,0:T(1,128)}, u32[]{:S(2)}) copy-start(f32[16,1,80]{2,1,0:T(1,128)} %param.26) | copy-start | bytes 15364
  62.4 42.8 %copy-start.11 = (f32[16,1,80]{2,1,0:T(1,128)S(1)}, f32[16,1,80]{2,1,0:T(1,128)}, u32[]{:S(2)}) copy-start(f32[16,1,80]{2,1,0:T(1,128)} %param.28) | copy-start | bytes 15364
  80.5 61.9 %copy-start.8 = (f32[4,4096]{1,0:T(4,128)S(1)}, f32[4,4096]{1,0:T(4,128)}, u32[]{:S(2)}) copy-start(f32[4,4096]{1,0:T(4,128)} %sol_ref.1) | copy-start | bytes 196612
  80.5 61.9 %copy-start.12 = (f32[16,1,80]{2,1,0:T(1,128)S(1)}, f32[16,1,80]{2,1,0:T(1,128)}, u32[]{:S(2)}) copy-start(f32[16,1,80]{2,1,0:T(1,128)} %param.25) | copy-start | bytes 15364
  81.4 23.8 %all-to-all-start.9 = ((f32[16,8,768]{2,1,0:T(8,128)}), f32[16,8,768]{2,1,0:T(8,128)S(1)}, u32[]{:S(2)}, u32[]{:S(2)}) async-start(f32[16,8,768]{2,1,0:T(8,128)} %shard_map.204), calls=%async_computation.9 | async-start | bytes 786432 | tf_op jit(solution)/shard_map/all_to_all | solution.py:635
  125.2 17.3 %all-to-all-start.11 = ((f32[16,1,128]{2,1,0:T(1,128)}), f32[16,1,128]{2,1,0:T(1,128)S(1)}, u32[]{:S(2)}, u32[]{:S(2)}) async-start(f32[16,1,128]{2,1,0:T(1,128)} %broadcast_in_dim.162), calls=%async_computation.11 | async-start | bytes 16384 | tf_op jit(solution)/shard_map/all_to_all | solution.py:657

commit v6 on v5

--- a/solution.py
+++ b/solution.py
@@ -403,22 +403,16 @@
     weight_ref[...] = jnp.zeros(weight_ref.shape, F32)
     group = 8
 
-    def add(k, _):
+    def add(k):
         r = pl.multiple_of(k * group, group)
         place = flat(lists_ref, r, group).astype(jnp.int32) - 1
         row, column = place_in(place, place >= 0)
         fields = []
         for t in range(traits):
             fields += parts(flat(turned_ref, t * CAP + r, group))
-        fields = masked(row, short, fields + [flat(lists_ref, CAP + r, group)])
-        sums = dot(fields, one_hot(column, 256), NT)
-        acc_ref[...] += sums[: 2 * traits * short]
-        weight_ref[...] += sums[2 * traits * short :]
-        return 0
-
-    lax.fori_loop(0, CAP // group, add, 0, unroll=True)
-
-    def step(k, _):
+        return masked(row, short, fields + [flat(lists_ref, CAP + r, group)]), one_hot(column, 256)
+
+    def step(k):
         at = pl.ds(pl.multiple_of(k * n, n), n)
         sire = sire_ref[:, at]
         dam = dam_ref[:, at]
@@ -431,10 +425,18 @@
             scaled = c_ref[t : t + 1, at] - 0.5 * weight * pick(found, in_slot, t)
             image_ref[t : t + 1, at] = scaled
             fields += parts(scaled)
-        acc_ref[...] += dot(masked(row, short, fields), one_hot(column, 256), NT)
+        fields.append(jnp.zeros((1, n), F32))
+        return masked(row, short, fields), one_hot(column, 256)
+
+    def both(k, _):
+        fields, hits = zip(add(k), step(k))
+        sums = dot(jnp.concatenate(fields, axis=1), jnp.concatenate(hits, axis=1), NT)
+        acc_ref[...] += sums[: 2 * traits * short]
+        weight_ref[...] += sums[2 * traits * short :]
         return 0
 
-    lax.fori_loop(0, animals // n, step, 0, unroll=True)
+    assert animals // n == CAP // group
+    lax.fori_loop(0, animals // n, both, 0, unroll=True)
     for t in range(traits):
         at = slice(t * blocks, (t + 1) * blocks)
         first = 2 * t * short

time: 144 us -> 145 us (level)
  no operation moved by 1% of the time
where the time goes in v6:
time: 145 us; the launch traced here: 144 us
  blocking collectives  50.7 us (35%)
  starting transfers between devices  42.3 us (29%)
  waiting for transfers between devices  32.8 us (23%)
  Pallas kernels  14.7 us (10%)
  between operations  1.57 us (1%)
    all_to_all x1, blocking collectives, body(): got_near = lax.all_to_all(back_near, ('y', 'c'), 0, 0, tiled=True)  18.1 us
    all_to_all x1, waiting for transfers between devices, body(): got_z = lax.all_to_all(back_z, 'z', 0, 0, tiled=True)  16.7 us
    all_to_all x1, blocking collectives, reduced(): lax.all_to_all(jnp.broadcast_to(sums[None], (near * nx, 1, 128)), ('y', '...  16.3 us
    all_to_all x1, starting transfers between devices, body(): in_z = lax.all_to_all(out_z, 'z', 0, 0, tiled=True)  15.9 us
    all_to_all x1, waiting for transfers between devices, reduced(): lax.all_to_all(jnp.broadcast_to(close, (nz, 1, 128)), 'z', 0, 0, tiled=True)  11.2 us
    ppermute x3, starting transfers between devices, body(): lax.ppermute(table, 'x', [(i, (i + k) % nx) for i in range(nx)])  10.5 us
    all_gather x1, blocking collectives, body(): in_near = lax.all_gather(in_y, 'c', axis=0)  8.25 us
    all_to_all x1, blocking collectives, body(): from_x = lax.all_to_all(to_x, 'x', 0, 0, tiled=True)  8.03 us
  transfers between devices with their start and end apart: 7, of which 4 were waited for; matrix products, arithmetic and copies ran while one was open for 1% of the time, Pallas kernels for 2%

profile of v6, /device:TPU:1, one launch (start us, length us, event | category | flops | bytes accessed | tf_op | source)
XLA Modules:
  0.0 144.2 jit_solution(16533481725680042991)
XLA Ops:
  0.6 0.0 copy-start.6
  0.6 0.0 copy-start.5
  0.7 0.0 copy-start.13
  0.7 3.2 %shard_map.199 = (f32[16,8,384]{2,1,0:T(8,128)}, s32[1,4096]{1,0:T(1,128)S(1)}, f32[128,128]{1,0:T(8,128)S(1)}) custom-call(f32[4,4096]{1,0:T(4,128)} %dir_ref.5, f32[16,80]{1,0:T(8,128)} %bitcast.85, s32[1,4096]{1,0:T(1,128)} %bitcast.79, s32[1,4096]{1,0:T(1,128)} %bitcast.82), custom_call_target="tpu_custom_call" | custom-call | tf_op jit(solution)/shard_map/pallas_call | solution.py:584
  3.8 0.0 copy-start
  3.8 0.0 copy-start.1
  3.9 15.9 %all-to-all-start.5 = ((f32[16,8,384]{2,1,0:T(8,128)}), f32[16,8,384]{2,1,0:T(8,128)S(1)}, u32[]{:S(2)}, u32[]{:S(2)}) async-start(f32[16,8,384]{2,1,0:T(8,128)} %get-tuple-element.136), calls=%async_computation.5 | async-start | bytes 393216 | tf_op jit(solution)/shard_map/all_to_all | solution.py:589
  19.7 3.1 %collective-permute-start.2 = (f32[128,128]{1,0:T(8,128)S(1)}, f32[128,128]{1,0:T(8,128)S(1)}, u32[]{:S(2)}, u32[]{:S(2)}) collective-permute-start(f32[128,128]{1,0:T(8,128)S(1)} %get-tuple-element.139), channel_id=1, source_target_pairs={{0,1},{1,2},{2,3},{3,0},{4,5},{5,6},{6,7},{7,4},{8,9},{9,10},{10,1... | collective-permute-start | bytes 196616 | tf_op jit(solution)/shard_map/ppermute | solution.py:591
  22.9 4.4 %collective-permute-start.1 = (f32[128,128]{1,0:T(8,128)S(1)}, f32[128,128]{1,0:T(8,128)S(1)}, u32[]{:S(2)}, u32[]{:S(2)}) collective-permute-start(f32[128,128]{1,0:T(8,128)S(1)} %get-tuple-element.139), channel_id=1, source_target_pairs={{0,2},{1,3},{2,0},{3,1},{4,6},{5,7},{6,4},{7,5},{8,10},{9,11},{10,... | collective-permute-start | bytes 196616 | tf_op jit(solution)/shard_map/ppermute | solution.py:591
  27.2 3.1 %collective-permute-start = (f32[128,128]{1,0:T(8,128)S(1)}, f32[128,128]{1,0:T(8,128)S(1)}, u32[]{:S(2)}, u32[]{:S(2)}) collective-permute-start(f32[128,128]{1,0:T(8,128)S(1)} %get-tuple-element.139), channel_id=1, source_target_pairs={{0,3},{1,0},{2,1},{3,2},{4,7},{5,4},{6,5},{7,6},{8,11},{9,8},{10,9... | collective-permute-start | bytes 196616 | tf_op jit(solution)/shard_map/ppermute | solution.py:591
  30.3 0.7 broadcast_select_fusion.4.gw_ref
  31.0 1.2 all-to-all-done.5.in_ref
  32.3 0.9 shard_map.200
  33.1 4.2 %all-to-all-start.6 = ((f32[4,16,1536]{2,1,0:T(8,128)}), f32[4,16,1536]{2,1,0:T(8,128)S(1)}, u32[]{:S(2)}, u32[]{:S(2)}) async-start(f32[4,16,1536]{2,1,0:T(8,128)} %shard_map.200), calls=%async_computation.6 | async-start | bytes 786432 | tf_op jit(solution)/shard_map/all_to_all | solution.py:605
  37.3 0.0 collective-permute-done.2
  37.3 0.0 collective-permute-done.1
  37.3 0.0 collective-permute-done
  37.4 0.0 copy-done.6
  37.4 0.0 copy-done.5
  37.4 0.0 copy-done.13
  37.4 2.5 %shard_map.201 = (f32[128,128]{1,0:T(8,128)S(1)}, f32[4,4096]{1,0:T(4,128)S(1)}, f32[8,16,256]{2,1,0:T(8,128)S(1)}) custom-call(f32[4,16]{1,0:T(4,128)S(1)} %copy-done.13, f32[4,128,128]{2,1,0:T(8,128)S(1)} %pad_maximum_fusion.all_ref, s32[1,4096]{1,0:T(1,128)S(1)} %bitcast.80, s32[1,4096]{1,0:T(1,128)S(1)} %bitcast.83, ...), custom_call_target="tpu_custom_call" | custom-call | tf_op jit(solution)/shard_map/pallas_call | solution.py:609
  39.9 3.6 %all-to-all-done.6 = f32[4,16,1536]{2,1,0:T(8,128)S(1)} async-done(((f32[4,16,1536]{2,1,0:T(8,128)}), f32[4,16,1536]{2,1,0:T(8,128)S(1)}, u32[]{:S(2)}, u32[]{:S(2)}) %all-to-all-start.6) | async-done | bytes 393248 | tf_op jit(solution)/shard_map/all_to_all | solution.py:605
  43.6 8.2 %all-gather = f32[8,16,1536]{2,1,0:T(8,128)S(1)} all-gather(f32[4,16,1536]{2,1,0:T(8,128)S(1)} %all-to-all-done.6), channel_id=2, replica_groups=mesh['y'=4,'z'=16,'c'=2,'x'=4] {'c'}, dimensions={0}, use_global_device_ids=true | all-gather | bytes 1179648 | tf_op jit(solution)/shard_map/all_gather | solution.py:616
  51.8 0.0 copy-done
  51.8 0.0 copy-done.1
  51.8 0.8 shard_map.202
  52.6 8.0 %all_to_all.62.pred_ref = f32[4,8,128]{2,1,0:T(8,128)S(1)} all-to-all(f32[4,8,128]{2,1,0:T(8,128)S(1)} %get-tuple-element.147), channel_id=1, replica_groups=mesh['y'=4,'z'=16,'c'=2,'x'=4] {'x'}, dimensions={0} | all-to-all | bytes 32768 | tf_op jit(solution)/shard_map/all_to_all | solution.py:624
  60.7 1.6 %shard_map.203 = (f32[8,16,1792]{2,1,0:T(8,128)S(1)}, f32[16,128]{1,0:T(8,128)S(1)}) custom-call(f32[128,128]{1,0:T(8,128)S(1)} %get-tuple-element.144.tab_ref.mixed_ref, f32[8,16,256]{2,1,0:T(8,128)S(1)} %get-tuple-element.145.add_ref, f32[4,128,128]{2,1,0:T(8,128)S(1)} %pad_maximum_fusion.all_ref, f32[4,8,128]{2,1,0:T(8,128)S(1)} %all_to_all.62.pred_ref, ...), custom_call_target="tpu_custom_call" | custom-call | tf_op jit(solution)/shard_map/pallas_call | solution.py:626
  62.3 0.0 copy-start.14
  62.3 0.0 copy-start.2
  62.3 0.0 copy-start.3
  62.3 0.0 copy-start.4
  62.4 0.0 copy-start.7
  62.4 0.0 copy-start.9
  62.4 0.0 copy-start.10
  62.4 0.0 copy-start.11
  62.4 18.1 %all_to_all.63.in_ref = f32[8,16,1792]{2,1,0:T(8,128)S(1)} all-to-all(f32[8,16,1792]{2,1,0:T(8,128)S(1)} %get-tuple-element.149), channel_id=1, replica_groups=mesh['y'=4,'z'=16,'c'=2,'x'=4] {'y','c'}, dimensions={0} | all-to-all | bytes 1835008 | tf_op jit(solution)/shard_map/all_to_all | solution.py:631
  80.5 0.0 copy-start.8
  80.5 0.0 copy-start.12
  80.5 0.9 shard_map.204
  81.4 5.7 %all-to-all-start.9 = ((f32[16,8,768]{2,1,0:T(8,128)}), f32[16,8,768]{2,1,0:T(8,128)S(1)}, u32[]{:S(2)}, u32[]{:S(2)}) async-start(f32[16,8,768]{2,1,0:T(8,128)} %shard_map.204), calls=%async_computation.9 | async-start | bytes 786432 | tf_op jit(solution)/shard_map/all_to_all | solution.py:637
  87.1 0.0 copy-done.14
  87.1 0.1 copy.151.ridge_ref
  87.2 0.5 slice.37
  88.4 0.1 shard_map.205.lists_ref
  88.5 16.7 %all-to-all-done.9.got_ref = f32[16,8,768]{2,1,0:T(8,128)S(1)} async-done(((f32[16,8,768]{2,1,0:T(8,128)}), f32[16,8,768]{2,1,0:T(8,128)S(1)}, u32[]{:S(2)}, u32[]{:S(2)}) %all-to-all-start.9) | async-done | bytes 393248 | tf_op jit(solution)/shard_map/all_to_all | solution.py:637
  105.2 0.0 copy-done.2
  105.2 0.0 copy-done.3
  105.2 0.0 copy-done.4
  105.2 0.0 copy-done.7
  105.2 0.0 copy-done.9
  105.2 0.0 copy-done.10
  105.2 0.0 copy-done.11
  105.2 3.9 %shard_map.206 = (f32[4,4096]{1,0:T(4,128)S(1)}, f32[16,80]{1,0:T(8,128)S(1)}, f32[1,128]{1,0:T(1,128)S(1)}) custom-call(f32[16,8,768]{2,1,0:T(8,128)S(1)} %all-to-all-done.9.got_ref, f32[4,4096]{1,0:T(4,128)S(1)} %get-tuple-element.155.c_ref, s32[1,4096]{1,0:T(1,128)S(1)} %get-tuple-element.140.rank_ref, s32[1,4096]{1,0:T(1,128)S(1)} %bitcast.81, ...), custom_call_target="tpu_custom_call" | custom-call | tf_op jit(solution)/shard_map/pallas_call | solution.py:643
  109.2 16.3 %all_to_all.64 = f32[32,1,128]{2,1,0:T(1,128)S(1)} all-to-all(f32[32,1,128]{2,1,0:T(1,128)S(1)} %broadcast_in_dim.161), channel_id=1, replica_groups=mesh['y'=4,'z'=16,'c'=2,'x'=4] {'y','c','x'}, dimensions={0} | all-to-all | bytes 32768 | tf_op jit(solution)/shard_map/all_to_all | solution.py:655
  125.5 0.6 broadcast_in_dim.162
  126.1 6.0 %all-to-all-start.11 = ((f32[16,1,128]{2,1,0:T(1,128)}), f32[16,1,128]{2,1,0:T(1,128)S(1)}, u32[]{:S(2)}, u32[]{:S(2)}) async-start(f32[16,1,128]{2,1,0:T(1,128)} %broadcast_in_dim.162), calls=%async_computation.11 | async-start | bytes 16384 | tf_op jit(solution)/shard_map/all_to_all | solution.py:659
  132.1 11.2 %all-to-all-done.11.sums_ref = f32[16,1,128]{2,1,0:T(1,128)S(1)} async-done(((f32[16,1,128]{2,1,0:T(1,128)}), f32[16,1,128]{2,1,0:T(1,128)S(1)}, u32[]{:S(2)}, u32[]{:S(2)}) %all-to-all-start.11) | async-done | bytes 8224 | tf_op jit(solution)/shard_map/all_to_all | solution.py:659
  143.4 0.0 copy-done.8
  143.4 0.0 copy-done.12
  143.4 0.8 shard_map.207
  (7 shorter events, 0.1 us)
Async XLA Ops:
  0.6 36.8 %copy-start.6 = (s32[4096]{0:T(1024)S(1)}, s32[4096]{0:T(1024)}, u32[]{:S(2)}) copy-start(s32[4096]{0:T(1024)} %param.35) | copy-start | bytes 49156
  0.6 36.8 %copy-start.5 = (s32[4096]{0:T(1024)S(1)}, s32[4096]{0:T(1024)}, u32[]{:S(2)}) copy-start(s32[4096]{0:T(1024)} %param.34) | copy-start | bytes 49156
  0.7 36.8 %copy-start.13 = (f32[4,16]{1,0:T(4,128)S(1)}, f32[4,16]{1,0:T(4,128)}, u32[]{:S(2)}) copy-start(f32[4,16]{1,0:T(4,128)} %mix_ref.1) | copy-start | bytes 772
  3.8 48.0 %copy-start = (bf16[32,10240]{1,0:T(8,128)(2,1)S(1)}, bf16[32,10240]{1,0:T(8,128)(2,1)}, u32[]{:S(2)}) copy-start(bf16[32,10240]{1,0:T(8,128)(2,1)} %geno_ref.3) | copy-start | bytes 1966084
  3.8 48.0 %copy-start.1 = (f32[10240]{0:T(1024)S(1)}, f32[10240]{0:T(1024)}, u32[]{:S(2)}) copy-start(f32[10240]{0:T(1024)} %param.30) | copy-start | bytes 122884
  3.9 28.4 %all-to-all-start.5 = ((f32[16,8,384]{2,1,0:T(8,128)}), f32[16,8,384]{2,1,0:T(8,128)S(1)}, u32[]{:S(2)}, u32[]{:S(2)}) async-start(f32[16,8,384]{2,1,0:T(8,128)} %get-tuple-element.136), calls=%async_computation.5 | async-start | bytes 393216 | tf_op jit(solution)/shard_map/all_to_all | solution.py:589
  19.7 17.6 %collective-permute-start.2 = (f32[128,128]{1,0:T(8,128)S(1)}, f32[128,128]{1,0:T(8,128)S(1)}, u32[]{:S(2)}, u32[]{:S(2)}) collective-permute-start(f32[128,128]{1,0:T(8,128)S(1)} %get-tuple-element.139), channel_id=1, source_target_pairs={{0,1},{1,2},{2,3},{3,0},{4,5},{5,6},{6,7},{7,4},{8,9},{9,10},{10,1... | collective-permute-start | bytes 196616 | tf_op jit(solution)/shard_map/ppermute | solution.py:591
  22.9 14.5 %collective-permute-start.1 = (f32[128,128]{1,0:T(8,128)S(1)}, f32[128,128]{1,0:T(8,128)S(1)}, u32[]{:S(2)}, u32[]{:S(2)}) collective-permute-start(f32[128,128]{1,0:T(8,128)S(1)} %get-tuple-element.139), channel_id=1, source_target_pairs={{0,2},{1,3},{2,0},{3,1},{4,6},{5,7},{6,4},{7,5},{8,10},{9,11},{10,... | collective-permute-start | bytes 196616 | tf_op jit(solution)/shard_map/ppermute | solution.py:591
  27.2 10.1 %collective-permute-start = (f32[128,128]{1,0:T(8,128)S(1)}, f32[128,128]{1,0:T(8,128)S(1)}, u32[]{:S(2)}, u32[]{:S(2)}) collective-permute-start(f32[128,128]{1,0:T(8,128)S(1)} %get-tuple-element.139), channel_id=1, source_target_pairs={{0,3},{1,0},{2,1},{3,2},{4,7},{5,4},{6,5},{7,6},{8,11},{9,8},{10,9... | collective-permute-start | bytes 196616 | tf_op jit(solution)/shard_map/ppermute | solution.py:591
  33.1 10.4 %all-to-all-start.6 = ((f32[4,16,1536]{2,1,0:T(8,128)}), f32[4,16,1536]{2,1,0:T(8,128)S(1)}, u32[]{:S(2)}, u32[]{:S(2)}) async-start(f32[4,16,1536]{2,1,0:T(8,128)} %shard_map.200), calls=%async_computation.6 | async-start | bytes 786432 | tf_op jit(solution)/shard_map/all_to_all | solution.py:605
  62.3 24.8 %copy-start.14 = (f32[16]{0:T(128)S(1)}, f32[16]{0:T(128)}, u32[]{:S(2)}) copy-start(f32[16]{0:T(128)} %param.32) | copy-start | bytes 196
  62.3 42.9 %copy-start.2 = (f32[4,4096]{1,0:T(4,128)S(1)}, f32[4,4096]{1,0:T(4,128)}, u32[]{:S(2)}) copy-start(f32[4,4096]{1,0:T(4,128)} %dir_ref.5) | copy-start | bytes 196612
  62.3 42.9 %copy-start.3 = (f32[4,4096]{1,0:T(4,128)S(1)}, f32[4,4096]{1,0:T(4,128)}, u32[]{:S(2)}) copy-start(f32[4,4096]{1,0:T(4,128)} %res_ref.3) | copy-start | bytes 196612
  62.3 42.8 %copy-start.4 = (f32[4,4096]{1,0:T(4,128)S(1)}, f32[4,4096]{1,0:T(4,128)}, u32[]{:S(2)}) copy-start(f32[4,4096]{1,0:T(4,128)} %inv_ref.3) | copy-start | bytes 196612
  62.4 42.8 %copy-start.7 = (f32[4,4096]{1,0:T(4,128)S(1)}, f32[4,4096]{1,0:T(4,128)}, u32[]{:S(2)}) copy-start(f32[4,4096]{1,0:T(4,128)} %rec_ref.1) | copy-start | bytes 196612
  62.4 42.8 %copy-start.9 = (f32[16,1,80]{2,1,0:T(1,128)S(1)}, f32[16,1,80]{2,1,0:T(1,128)}, u32[]{:S(2)}) copy-start(f32[16,1,80]{2,1,0:T(1,128)} %param.27) | copy-start | bytes 15364
  62.4 42.8 %copy-start.10 = (f32[16,1,80]{2,1,0:T(1,128)S(1)}, f32[16,1,80]{2,1,0:T(1,128)}, u32[]{:S(2)}) copy-start(f32[16,1,80]{2,1,0:T(1,128)} %param.26) | copy-start | bytes 15364
  62.4 42.8 %copy-start.11 = (f32[16,1,80]{2,1,0:T(1,128)S(1)}, f32[16,1,80]{2,1,0:T(1,128)}, u32[]{:S(2)}) copy-start(f32[16,1,80]{2,1,0:T(1,128)} %param.28) | copy-start | bytes 15364
  80.5 62.8 %copy-start.8 = (f32[4,4096]{1,0:T(4,128)S(1)}, f32[4,4096]{1,0:T(4,128)}, u32[]{:S(2)}) copy-start(f32[4,4096]{1,0:T(4,128)} %sol_ref.1) | copy-start | bytes 196612
  80.5 62.8 %copy-start.12 = (f32[16,1,80]{2,1,0:T(1,128)S(1)}, f32[16,1,80]{2,1,0:T(1,128)}, u32[]{:S(2)}) copy-start(f32[16,1,80]{2,1,0:T(1,128)} %param.25) | copy-start | bytes 15364
  81.4 23.8 %all-to-all-start.9 = ((f32[16,8,768]{2,1,0:T(8,128)}), f32[16,8,768]{2,1,0:T(8,128)S(1)}, u32[]{:S(2)}, u32[]{:S(2)}) async-start(f32[16,8,768]{2,1,0:T(8,128)} %shard_map.204), calls=%async_computation.9 | async-start | bytes 786432 | tf_op jit(solution)/shard_map/all_to_all | solution.py:637
  126.1 17.3 %all-to-all-start.11 = ((f32[16,1,128]{2,1,0:T(1,128)}), f32[16,1,128]{2,1,0:T(1,128)S(1)}, u32[]{:S(2)}, u32[]{:S(2)}) async-start(f32[16,1,128]{2,1,0:T(1,128)} %broadcast_in_dim.162), calls=%async_computation.11 | async-start | bytes 16384 | tf_op jit(solution)/shard_map/all_to_all | solution.py:659

commit v7 on v5

--- a/solution.py
+++ b/solution.py
@@ -386,7 +386,7 @@
 def image_kernel(
     got_ref, c_ref, rank_ref, sire_ref, dam_ref, lists_ref, mixed_ref, resid_ref,
     dir_ref, rec_ref, res_ref, inv_ref, ridge_ref, dir_a_ref, res_a_ref, inv_a_ref,
-    image_ref, image_a_ref, sums_ref, acc_ref, tab_ref, turned_ref, weight_ref, *, shape,
+    image_ref, image_a_ref, sums_ref, acc_ref, tab_ref, turned_ref, weight_ref, dams_ref, *, shape,
 ):
     traits, animals = c_ref.shape
     ny, nz, nc = shape
@@ -401,6 +401,7 @@
         turned_ref[j * 128 : (j + 1) * 128, :] = got_ref[:, :, first : first + 128].reshape(herd, 128).T
     acc_ref[...] = jnp.zeros(acc_ref.shape, F32)
     weight_ref[...] = jnp.zeros(weight_ref.shape, F32)
+    dams_ref[...] = jnp.zeros(dams_ref.shape, F32)
     group = 8
 
     def add(k, _):
@@ -431,7 +432,7 @@
             scaled = c_ref[t : t + 1, at] - 0.5 * weight * pick(found, in_slot, t)
             image_ref[t : t + 1, at] = scaled
             fields += parts(scaled)
-        acc_ref[...] += dot(masked(row, short, fields), one_hot(column, 256), NT)
+        dams_ref[...] += dot(masked(row, short, fields), one_hot(column, 256), NT)
         return 0
 
     lax.fori_loop(0, animals // n, step, 0, unroll=True)
@@ -439,6 +440,7 @@
         at = slice(t * blocks, (t + 1) * blocks)
         first = 2 * t * short
         down = both_halves(acc_ref, first, short) + both_halves(acc_ref, first + short, short)
+        down = down + both_halves(dams_ref, first, short) + both_halves(dams_ref, first + short, short)
         tab_ref[at, :] = (0.25 / 1.5) * both_halves(weight_ref, 0, short) * mixed_ref[at, :] - 0.5 * down
     for b in range(blocks):
         for t in range(traits):
@@ -641,7 +643,9 @@
     image_u, image_a, sums = call(
         functools.partial(image_kernel, shape=shape),
         (sds(here, animals), sds(traits, columns), sds(1, 128)),
-        scratch=[vmem(here * blocks, 256), vmem(half, 128), vmem(values, herd), vmem(blocks // 2, 256)],
+        scratch=[vmem(here * blocks, 256), vmem(half, 128), vmem(values, herd), vmem(blocks // 2, 256),
+            vmem(here * blocks, 256),
+        ],
     )(
         got_z, c_term, rank, sire_row, dam_row, ordered, mixed_table, own_resid,
         dir_u, rec_weight, res_u, inv_diag_u, snp_ridge[:, None], d_a, r_a, i_a,

time: 144 us -> 144 us (level)
  no operation moved by 1% of the time
where the time goes in v7:
time: 144 us; the launch traced here: 143 us
  blocking collectives  50.7 us (35%)
  starting transfers between devices  42.3 us (29%)
  waiting for transfers between devices  32.8 us (23%)
  Pallas kernels  13.8 us (10%)
  between operations  1.57 us (1%)
    all_to_all x1, blocking collectives, body(): got_near = lax.all_to_all(back_near, ('y', 'c'), 0, 0, tiled=True)  18.1 us
    all_to_all x1, waiting for transfers between devices, body(): got_z = lax.all_to_all(back_z, 'z', 0, 0, tiled=True)  16.7 us
    all_to_all x1, blocking collectives, reduced(): lax.all_to_all(jnp.broadcast_to(sums[None], (near * nx, 1, 128)), ('y', '...  16.3 us
    all_to_all x1, starting transfers between devices, body(): in_z = lax.all_to_all(out_z, 'z', 0, 0, tiled=True)  15.9 us
    all_to_all x1, waiting for transfers between devices, reduced(): lax.all_to_all(jnp.broadcast_to(close, (nz, 1, 128)), 'z', 0, 0, tiled=True)  11.2 us
    ppermute x3, starting transfers between devices, body(): lax.ppermute(table, 'x', [(i, (i + k) % nx) for i in range(nx)])  10.5 us
    all_gather x1, blocking collectives, body(): in_near = lax.all_gather(in_y, 'c', axis=0)  8.25 us
    all_to_all x1, blocking collectives, body(): from_x = lax.all_to_all(to_x, 'x', 0, 0, tiled=True)  8.03 us
  transfers between devices with their start and end apart: 7, of which 4 were waited for; matrix products, arithmetic and copies ran while one was open for 1% of the time, Pallas kernels for 2%

profile of v7, /device:TPU:1, one launch (start us, length us, event | category | flops | bytes accessed | tf_op | source)
XLA Modules:
  0.0 143.2 jit_solution(1075283750906589758)
XLA Ops:
  0.6 0.0 copy-start.6
  0.6 0.0 copy-start.5
  0.7 0.0 copy-start.13
  0.7 3.2 %shard_map.199 = (f32[16,8,384]{2,1,0:T(8,128)}, s32[1,4096]{1,0:T(1,128)S(1)}, f32[128,128]{1,0:T(8,128)S(1)}) custom-call(f32[4,4096]{1,0:T(4,128)} %dir_ref.5, f32[16,80]{1,0:T(8,128)} %bitcast.85, s32[1,4096]{1,0:T(1,128)} %bitcast.79, s32[1,4096]{1,0:T(1,128)} %bitcast.82), custom_call_target="tpu_custom_call" | custom-call | tf_op jit(solution)/shard_map/pallas_call | solution.py:584
  3.8 0.0 copy-start
  3.8 0.0 copy-start.1
  3.9 15.9 %all-to-all-start.5 = ((f32[16,8,384]{2,1,0:T(8,128)}), f32[16,8,384]{2,1,0:T(8,128)S(1)}, u32[]{:S(2)}, u32[]{:S(2)}) async-start(f32[16,8,384]{2,1,0:T(8,128)} %get-tuple-element.136), calls=%async_computation.5 | async-start | bytes 393216 | tf_op jit(solution)/shard_map/all_to_all | solution.py:589
  19.7 3.1 %collective-permute-start.2 = (f32[128,128]{1,0:T(8,128)S(1)}, f32[128,128]{1,0:T(8,128)S(1)}, u32[]{:S(2)}, u32[]{:S(2)}) collective-permute-start(f32[128,128]{1,0:T(8,128)S(1)} %get-tuple-element.139), channel_id=1, source_target_pairs={{0,1},{1,2},{2,3},{3,0},{4,5},{5,6},{6,7},{7,4},{8,9},{9,10},{10,1... | collective-permute-start | bytes 196616 | tf_op jit(solution)/shard_map/ppermute | solution.py:591
  22.9 4.4 %collective-permute-start.1 = (f32[128,128]{1,0:T(8,128)S(1)}, f32[128,128]{1,0:T(8,128)S(1)}, u32[]{:S(2)}, u32[]{:S(2)}) collective-permute-start(f32[128,128]{1,0:T(8,128)S(1)} %get-tuple-element.139), channel_id=1, source_target_pairs={{0,2},{1,3},{2,0},{3,1},{4,6},{5,7},{6,4},{7,5},{8,10},{9,11},{10,... | collective-permute-start | bytes 196616 | tf_op jit(solution)/shard_map/ppermute | solution.py:591
  27.2 3.1 %collective-permute-start = (f32[128,128]{1,0:T(8,128)S(1)}, f32[128,128]{1,0:T(8,128)S(1)}, u32[]{:S(2)}, u32[]{:S(2)}) collective-permute-start(f32[128,128]{1,0:T(8,128)S(1)} %get-tuple-element.139), channel_id=1, source_target_pairs={{0,3},{1,0},{2,1},{3,2},{4,7},{5,4},{6,5},{7,6},{8,11},{9,8},{10,9... | collective-permute-start | bytes 196616 | tf_op jit(solution)/shard_map/ppermute | solution.py:591
  30.3 0.7 broadcast_select_fusion.4.gw_ref
  31.0 1.2 all-to-all-done.5.in_ref
  32.3 0.9 shard_map.200
  33.1 4.2 %all-to-all-start.6 = ((f32[4,16,1536]{2,1,0:T(8,128)}), f32[4,16,1536]{2,1,0:T(8,128)S(1)}, u32[]{:S(2)}, u32[]{:S(2)}) async-start(f32[4,16,1536]{2,1,0:T(8,128)} %shard_map.200), calls=%async_computation.6 | async-start | bytes 786432 | tf_op jit(solution)/shard_map/all_to_all | solution.py:605
  37.3 0.0 collective-permute-done.2
  37.3 0.0 collective-permute-done.1
  37.3 0.0 collective-permute-done
  37.4 0.0 copy-done.6
  37.4 0.0 copy-done.5
  37.4 0.0 copy-done.13
  37.4 2.5 %shard_map.201 = (f32[128,128]{1,0:T(8,128)S(1)}, f32[4,4096]{1,0:T(4,128)S(1)}, f32[8,16,256]{2,1,0:T(8,128)S(1)}) custom-call(f32[4,16]{1,0:T(4,128)S(1)} %copy-done.13, f32[4,128,128]{2,1,0:T(8,128)S(1)} %pad_maximum_fusion.all_ref, s32[1,4096]{1,0:T(1,128)S(1)} %bitcast.80, s32[1,4096]{1,0:T(1,128)S(1)} %bitcast.83, ...), custom_call_target="tpu_custom_call" | custom-call | tf_op jit(solution)/shard_map/pallas_call | solution.py:609
  39.9 3.6 %all-to-all-done.6 = f32[4,16,1536]{2,1,0:T(8,128)S(1)} async-done(((f32[4,16,1536]{2,1,0:T(8,128)}), f32[4,16,1536]{2,1,0:T(8,128)S(1)}, u32[]{:S(2)}, u32[]{:S(2)}) %all-to-all-start.6) | async-done | bytes 393248 | tf_op jit(solution)/shard_map/all_to_all | solution.py:605
  43.6 8.2 %all-gather = f32[8,16,1536]{2,1,0:T(8,128)S(1)} all-gather(f32[4,16,1536]{2,1,0:T(8,128)S(1)} %all-to-all-done.6), channel_id=2, replica_groups=mesh['y'=4,'z'=16,'c'=2,'x'=4] {'c'}, dimensions={0}, use_global_device_ids=true | all-gather | bytes 1179648 | tf_op jit(solution)/shard_map/all_gather | solution.py:616
  51.8 0.0 copy-done
  51.8 0.0 copy-done.1
  51.8 0.8 shard_map.202
  52.6 8.0 %all_to_all.62.pred_ref = f32[4,8,128]{2,1,0:T(8,128)S(1)} all-to-all(f32[4,8,128]{2,1,0:T(8,128)S(1)} %get-tuple-element.147), channel_id=1, replica_groups=mesh['y'=4,'z'=16,'c'=2,'x'=4] {'x'}, dimensions={0} | all-to-all | bytes 32768 | tf_op jit(solution)/shard_map/all_to_all | solution.py:624
  60.7 1.6 %shard_map.203 = (f32[8,16,1792]{2,1,0:T(8,128)S(1)}, f32[16,128]{1,0:T(8,128)S(1)}) custom-call(f32[128,128]{1,0:T(8,128)S(1)} %get-tuple-element.144.tab_ref.mixed_ref, f32[8,16,256]{2,1,0:T(8,128)S(1)} %get-tuple-element.145.add_ref, f32[4,128,128]{2,1,0:T(8,128)S(1)} %pad_maximum_fusion.all_ref, f32[4,8,128]{2,1,0:T(8,128)S(1)} %all_to_all.62.pred_ref, ...), custom_call_target="tpu_custom_call" | custom-call | tf_op jit(solution)/shard_map/pallas_call | solution.py:626
  62.3 0.0 copy-start.14
  62.3 0.0 copy-start.2
  62.3 0.0 copy-start.3
  62.3 0.0 copy-start.4
  62.4 0.0 copy-start.7
  62.4 0.0 copy-start.9
  62.4 0.0 copy-start.10
  62.4 0.0 copy-start.11
  62.4 18.1 %all_to_all.63.in_ref = f32[8,16,1792]{2,1,0:T(8,128)S(1)} all-to-all(f32[8,16,1792]{2,1,0:T(8,128)S(1)} %get-tuple-element.149), channel_id=1, replica_groups=mesh['y'=4,'z'=16,'c'=2,'x'=4] {'y','c'}, dimensions={0} | all-to-all | bytes 1835008 | tf_op jit(solution)/shard_map/all_to_all | solution.py:631
  80.5 0.0 copy-start.8
  80.5 0.0 copy-start.12
  80.5 0.9 shard_map.204
  81.4 5.7 %all-to-all-start.9 = ((f32[16,8,768]{2,1,0:T(8,128)}), f32[16,8,768]{2,1,0:T(8,128)S(1)}, u32[]{:S(2)}, u32[]{:S(2)}) async-start(f32[16,8,768]{2,1,0:T(8,128)} %shard_map.204), calls=%async_computation.9 | async-start | bytes 786432 | tf_op jit(solution)/shard_map/all_to_all | solution.py:637
  87.1 0.0 copy-done.14
  87.1 0.1 copy.151.ridge_ref
  87.2 0.5 slice.37
  88.4 0.1 shard_map.205.lists_ref
  88.5 16.7 %all-to-all-done.9.got_ref = f32[16,8,768]{2,1,0:T(8,128)S(1)} async-done(((f32[16,8,768]{2,1,0:T(8,128)}), f32[16,8,768]{2,1,0:T(8,128)S(1)}, u32[]{:S(2)}, u32[]{:S(2)}) %all-to-all-start.9) | async-done | bytes 393248 | tf_op jit(solution)/shard_map/all_to_all | solution.py:637
  105.2 0.0 copy-done.2
  105.2 0.0 copy-done.3
  105.2 0.0 copy-done.4
  105.2 0.0 copy-done.7
  105.2 0.0 copy-done.9
  105.2 0.0 copy-done.10
  105.2 0.0 copy-done.11
  105.2 3.0 %shard_map.206 = (f32[4,4096]{1,0:T(4,128)S(1)}, f32[16,80]{1,0:T(8,128)S(1)}, f32[1,128]{1,0:T(1,128)S(1)}) custom-call(f32[16,8,768]{2,1,0:T(8,128)S(1)} %all-to-all-done.9.got_ref, f32[4,4096]{1,0:T(4,128)S(1)} %get-tuple-element.155.c_ref, s32[1,4096]{1,0:T(1,128)S(1)} %get-tuple-element.140.rank_ref, s32[1,4096]{1,0:T(1,128)S(1)} %bitcast.81, ...), custom_call_target="tpu_custom_call" | custom-call | tf_op jit(solution)/shard_map/pallas_call | solution.py:643
  108.3 16.3 %all_to_all.64 = f32[32,1,128]{2,1,0:T(1,128)S(1)} all-to-all(f32[32,1,128]{2,1,0:T(1,128)S(1)} %broadcast_in_dim.161), channel_id=1, replica_groups=mesh['y'=4,'z'=16,'c'=2,'x'=4] {'y','c','x'}, dimensions={0} | all-to-all | bytes 32768 | tf_op jit(solution)/shard_map/all_to_all | solution.py:657
  124.6 0.6 broadcast_in_dim.162
  125.2 6.0 %all-to-all-start.11 = ((f32[16,1,128]{2,1,0:T(1,128)}), f32[16,1,128]{2,1,0:T(1,128)S(1)}, u32[]{:S(2)}, u32[]{:S(2)}) async-start(f32[16,1,128]{2,1,0:T(1,128)} %broadcast_in_dim.162), calls=%async_computation.11 | async-start | bytes 16384 | tf_op jit(solution)/shard_map/all_to_all | solution.py:661
  131.2 11.2 %all-to-all-done.11.sums_ref = f32[16,1,128]{2,1,0:T(1,128)S(1)} async-done(((f32[16,1,128]{2,1,0:T(1,128)}), f32[16,1,128]{2,1,0:T(1,128)S(1)}, u32[]{:S(2)}, u32[]{:S(2)}) %all-to-all-start.11) | async-done | bytes 8224 | tf_op jit(solution)/shard_map/all_to_all | solution.py:661
  142.4 0.0 copy-done.8
  142.4 0.0 copy-done.12
  142.4 0.8 shard_map.207
  (7 shorter events, 0.1 us)
Async XLA Ops:
  0.6 36.8 %copy-start.6 = (s32[4096]{0:T(1024)S(1)}, s32[4096]{0:T(1024)}, u32[]{:S(2)}) copy-start(s32[4096]{0:T(1024)} %param.35) | copy-start | bytes 49156
  0.6 36.8 %copy-start.5 = (s32[4096]{0:T(1024)S(1)}, s32[4096]{0:T(1024)}, u32[]{:S(2)}) copy-start(s32[4096]{0:T(1024)} %param.34) | copy-start | bytes 49156
  0.7 36.8 %copy-start.13 = (f32[4,16]{1,0:T(4,128)S(1)}, f32[4,16]{1,0:T(4,128)}, u32[]{:S(2)}) copy-start(f32[4,16]{1,0:T(4,128)} %mix_ref.1) | copy-start | bytes 772
  3.8 48.0 %copy-start = (bf16[32,10240]{1,0:T(8,128)(2,1)S(1)}, bf16[32,10240]{1,0:T(8,128)(2,1)}, u32[]{:S(2)}) copy-start(bf16[32,10240]{1,0:T(8,128)(2,1)} %geno_ref.3) | copy-start | bytes 1966084
  3.8 48.0 %copy-start.1 = (f32[10240]{0:T(1024)S(1)}, f32[10240]{0:T(1024)}, u32[]{:S(2)}) copy-start(f32[10240]{0:T(1024)} %param.30) | copy-start | bytes 122884
  3.9 28.4 %all-to-all-start.5 = ((f32[16,8,384]{2,1,0:T(8,128)}), f32[16,8,384]{2,1,0:T(8,128)S(1)}, u32[]{:S(2)}, u32[]{:S(2)}) async-start(f32[16,8,384]{2,1,0:T(8,128)} %get-tuple-element.136), calls=%async_computation.5 | async-start | bytes 393216 | tf_op jit(solution)/shard_map/all_to_all | solution.py:589
  19.7 17.6 %collective-permute-start.2 = (f32[128,128]{1,0:T(8,128)S(1)}, f32[128,128]{1,0:T(8,128)S(1)}, u32[]{:S(2)}, u32[]{:S(2)}) collective-permute-start(f32[128,128]{1,0:T(8,128)S(1)} %get-tuple-element.139), channel_id=1, source_target_pairs={{0,1},{1,2},{2,3},{3,0},{4,5},{5,6},{6,7},{7,4},{8,9},{9,10},{10,1... | collective-permute-start | bytes 196616 | tf_op jit(solution)/shard_map/ppermute | solution.py:591
  22.9 14.5 %collective-permute-start.1 = (f32[128,128]{1,0:T(8,128)S(1)}, f32[128,128]{1,0:T(8,128)S(1)}, u32[]{:S(2)}, u32[]{:S(2)}) collective-permute-start(f32[128,128]{1,0:T(8,128)S(1)} %get-tuple-element.139), channel_id=1, source_target_pairs={{0,2},{1,3},{2,0},{3,1},{4,6},{5,7},{6,4},{7,5},{8,10},{9,11},{10,... | collective-permute-start | bytes 196616 | tf_op jit(solution)/shard_map/ppermute | solution.py:591
  27.2 10.1 %collective-permute-start = (f32[128,128]{1,0:T(8,128)S(1)}, f32[128,128]{1,0:T(8,128)S(1)}, u32[]{:S(2)}, u32[]{:S(2)}) collective-permute-start(f32[128,128]{1,0:T(8,128)S(1)} %get-tuple-element.139), channel_id=1, source_target_pairs={{0,3},{1,0},{2,1},{3,2},{4,7},{5,4},{6,5},{7,6},{8,11},{9,8},{10,9... | collective-permute-start | bytes 196616 | tf_op jit(solution)/shard_map/ppermute | solution.py:591
  33.1 10.4 %all-to-all-start.6 = ((f32[4,16,1536]{2,1,0:T(8,128)}), f32[4,16,1536]{2,1,0:T(8,128)S(1)}, u32[]{:S(2)}, u32[]{:S(2)}) async-start(f32[4,16,1536]{2,1,0:T(8,128)} %shard_map.200), calls=%async_computation.6 | async-start | bytes 786432 | tf_op jit(solution)/shard_map/all_to_all | solution.py:605
  62.3 24.8 %copy-start.14 = (f32[16]{0:T(128)S(1)}, f32[16]{0:T(128)}, u32[]{:S(2)}) copy-start(f32[16]{0:T(128)} %param.32) | copy-start | bytes 196
  62.3 42.9 %copy-start.2 = (f32[4,4096]{1,0:T(4,128)S(1)}, f32[4,4096]{1,0:T(4,128)}, u32[]{:S(2)}) copy-start(f32[4,4096]{1,0:T(4,128)} %dir_ref.5) | copy-start | bytes 196612
  62.3 42.9 %copy-start.3 = (f32[4,4096]{1,0:T(4,128)S(1)}, f32[4,4096]{1,0:T(4,128)}, u32[]{:S(2)}) copy-start(f32[4,4096]{1,0:T(4,128)} %res_ref.3) | copy-start | bytes 196612
  62.3 42.8 %copy-start.4 = (f32[4,4096]{1,0:T(4,128)S(1)}, f32[4,4096]{1,0:T(4,128)}, u32[]{:S(2)}) copy-start(f32[4,4096]{1,0:T(4,128)} %inv_ref.3) | copy-start | bytes 196612
  62.4 42.8 %copy-start.7 = (f32[4,4096]{1,0:T(4,128)S(1)}, f32[4,4096]{1,0:T(4,128)}, u32[]{:S(2)}) copy-start(f32[4,4096]{1,0:T(4,128)} %rec_ref.1) | copy-start | bytes 196612
  62.4 42.8 %copy-start.9 = (f32[16,1,80]{2,1,0:T(1,128)S(1)}, f32[16,1,80]{2,1,0:T(1,128)}, u32[]{:S(2)}) copy-start(f32[16,1,80]{2,1,0:T(1,128)} %param.27) | copy-start | bytes 15364
  62.4 42.8 %copy-start.10 = (f32[16,1,80]{2,1,0:T(1,128)S(1)}, f32[16,1,80]{2,1,0:T(1,128)}, u32[]{:S(2)}) copy-start(f32[16,1,80]{2,1,0:T(1,128)} %param.26) | copy-start | bytes 15364
  62.4 42.8 %copy-start.11 = (f32[16,1,80]{2,1,0:T(1,128)S(1)}, f32[16,1,80]{2,1,0:T(1,128)}, u32[]{:S(2)}) copy-start(f32[16,1,80]{2,1,0:T(1,128)} %param.28) | copy-start | bytes 15364
  80.5 61.9 %copy-start.8 = (f32[4,4096]{1,0:T(4,128)S(1)}, f32[4,4096]{1,0:T(4,128)}, u32[]{:S(2)}) copy-start(f32[4,4096]{1,0:T(4,128)} %sol_ref.1) | copy-start | bytes 196612
  80.5 61.9 %copy-start.12 = (f32[16,1,80]{2,1,0:T(1,128)S(1)}, f32[16,1,80]{2,1,0:T(1,128)}, u32[]{:S(2)}) copy-start(f32[16,1,80]{2,1,0:T(1,128)} %param.25) | copy-start | bytes 15364
  81.4 23.8 %all-to-all-start.9 = ((f32[16,8,768]{2,1,0:T(8,128)}), f32[16,8,768]{2,1,0:T(8,128)S(1)}, u32[]{:S(2)}, u32[]{:S(2)}) async-start(f32[16,8,768]{2,1,0:T(8,128)} %shard_map.204), calls=%async_computation.9 | async-start | bytes 786432 | tf_op jit(solution)/shard_map/all_to_all | solution.py:637
  125.2 17.3 %all-to-all-start.11 = ((f32[16,1,128]{2,1,0:T(1,128)}), f32[16,1,128]{2,1,0:T(1,128)S(1)}, u32[]{:S(2)}, u32[]{:S(2)}) async-start(f32[16,1,128]{2,1,0:T(1,128)} %broadcast_in_dim.162), calls=%async_computation.11 | async-start | bytes 16384 | tf_op jit(solution)/shard_map/all_to_all | solution.py:661
